TPU v7x, 256 devices: a whole 4x4x8 slice. The times are simulated.
256 devices in a mesh: seq: 32 (over y, x, core), dp: 8 (over z).
Axes of the slice: x: 4, y: 4, z: 8, core: 2. Of those that a mesh axis runs over, the one named last changes fastest.
Arguments:
- tokens: bfloat16 [8, 8192, 2048], P('dp', 'seq'), may hold values from -6 to 6
- w_qkv: bfloat16 [2048, 3, 1024], P('seq'), may hold values from -0.125 to 0.125
- weight_table: float32 [16, 8], replicated, may hold values from 0.3 to 3
- weight_index: int32 [8, 64, 6], P('dp', 'seq'), may hold values from 0 to 15
- cotangent: bfloat16 [8, 8192, 1024], P('dp', 'seq'), may hold values from -6 to 6
Outputs:
- attn_out: bfloat16 [8, 8192, 1024], P('dp', 'seq')
- grad_w: float32 [2048, 3, 1024], P('seq')
All inputs are finite; a program needn't handle non-finite values.
Results may differ from a plain program's by a relative error of at most 0.02.
Values may be sent and summed in bfloat16 or wider, within the bound.
No kernel may reach another device: no remote copies, remote signals or barrier semaphores. Data moves between devices by JAX's collectives and lax.ppermute only.
A program may use at most 128 MiB of HBM per device.

v0:
```python
import functools
import math

import jax
import jax.numpy as jnp
from jax import lax
from jax.experimental import pallas as pl
from jax.experimental.pallas import tpu as pltpu
from jax.sharding import Mesh, PartitionSpec as P

BF = jnp.bfloat16
F32 = jnp.float32
HEAD = 128
QB = 128
BLOCK = 256
D = 2048
COLS = 768
MIB = 1024 * 1024
SETS = 0x66
HALVES = 0xB4


def ring(value, phase, step):
    pairs = []
    for y in range(4):
        for x in range(4):
            for core in range(2):
                at = (y, (x - step) % 4) if core == phase else ((y - step) % 4, x)
                pairs.append(((y * 4 + x) * 2 + core, (at[0] * 4 + at[1]) * 2 + core))
    return lax.ppermute(value, ("y", "x", "core"), pairs)


def swap(value, axis, size, mask):
    return lax.ppermute(value, axis, [(i, i ^ mask) for i in range(size)])


def same_set_neighbour(value):
    return lax.ppermute(value, "dp", [(z, (z + 1 if z % 2 else z - 1) % 8) for z in range(8)])


def same_set_far(value):
    return lax.ppermute(value, "dp", [(z, ((7 if SETS >> z & 1 else 3) - z) % 8) for z in range(8)])


def behind(value, *others, index=None):
    zero = sum(other[0, 0].astype(F32) for other in others) * 0.0
    if index is not None:
        zero = zero + (index[-1, -1] < 0).astype(F32)
    return (value.astype(F32) + zero).astype(value.dtype)


def dot(a, b, ca, cb):
    return lax.dot_general(a, b, (((ca,), (cb,)), ((), ())), preferred_element_type=F32)


def smem():
    return pl.BlockSpec(memory_space=pltpu.SMEM)


def vmem():
    return pl.BlockSpec(memory_space=pltpu.VMEM)


def call(kernel, args, n_smem, outs, scratch=(), grant=16, flops=0, nbytes=0, n_any=0):
    return pl.pallas_call(
        kernel,
        out_shape=[jax.ShapeDtypeStruct(*out) for out in outs],
        in_specs=[smem()] * n_smem
        + [vmem()] * (len(args) - n_smem - n_any)
        + [pl.BlockSpec(memory_space=pl.ANY)] * n_any,
        out_specs=[vmem()] * len(outs),
        scratch_shapes=list(scratch),
        compiler_params=pltpu.CompilerParams(vmem_limit_bytes=grant * MIB),
        cost_estimate=pl.CostEstimate(flops=flops, bytes_accessed=nbytes, transcendentals=0),
    )(*args)


def lanes(start):
    return pl.ds(pl.multiple_of(start, HEAD), HEAD)


def level_coef(pos, idx, table, blk, group, level, head):
    cs = blk // 2
    y, x, core = pos[0], pos[1], pos[2]
    row = idx[blk, group * 6 + level]
    lam = table[row, (core * 2 + pos[4]) * 2 + head]
    if level == 0:
        return lam * (1.0 / math.sqrt(HEAD * BLOCK))
    bit = [(core + cs) & 1, x & 1, (x >> 1) & 1, y & 1, (y >> 1) & 1][level - 1]
    return lam * bit.astype(F32) * (1.0 / math.sqrt(HEAD * 2 ** (level - 1) * BLOCK))


def prepare_kernel(pos, w, w_own, w_core):
    core, kind = pos[2], pos[4]
    mine = pl.multiple_of((core * 2 + kind) * 256, 256)
    other = pl.multiple_of(((1 - core) * 2 + kind) * 256, 256)
    for third in range(3):
        at = slice(third * 256, third * 256 + 256)
        w_own[:, at] = w[third, :, pl.ds(mine, 256)]
        w_core[:, at] = w[third, :, pl.ds(other, 256)]


def split_kernel(pos, cot, own, to_core, to_z):
    core, kind = pos[2], pos[4]

    def columns(cs, zs):
        group = ((core + cs) & 1) * 2 + ((kind + zs) & 1)
        return cot[:, pl.ds(pl.multiple_of(group * 256, 256), 256)]

    own[...] = columns(0, 0)
    to_core[...] = columns(1, 0)
    to_z[:, :256] = columns(0, 1)
    to_z[:, 256:] = columns(1, 1)


def project_kernel(pos, idx, table, t0, t1, t2, t3, c0, c1, c2, c3, *refs):
    toks = (t0, t1, t2, t3)
    parts = (refs[0:2], refs[2:4], refs[6:8], refs[4:6])
    qkv, cots, s1, x0, g1, m2, m3, m4, m5, w = refs[8:]
    y, x, core = pos[0], pos[1], pos[2]
    for slot in range(4):
        for dist in range(4):
            yy = (y + dist + core * (slot - dist)) & 3
            xx = (x + slot + core * (dist - slot)) & 3
            for cs in range(2):
                row = pl.multiple_of((yy * 4 + xx) * 128 + ((core + cs) & 1) * 64, 64)
                start = (slot % 2) * 128 + cs * 64
                w[pl.ds(row, 64), :] = parts[dist][slot // 2][start : start + 64, :]
    for blk, src in enumerate((c0, c1, c2, c3)):
        cots[blk] = src[...]

    @pl.loop(0, 3)
    def _(part):
        cols = pl.ds(pl.multiple_of(part * 256, 256), 256)
        for blk in range(4):
            qkv[blk, :, cols] = dot(toks[blk][...], w[:, cols], 1, 0).astype(BF)

    @pl.loop(0, 4)
    def _(step):
        zs, h = step // 2, step % 2
        total = None
        sums = [None] * 4
        for cs in range(2):
            blk = cs * 2 + zs
            state = dot(qkv[blk, :, lanes(256 + h * HEAD)], qkv[blk, :, lanes(512 + h * HEAD)], 0, 0)
            s1[blk, h] = state.astype(BF)
            total = state if total is None else total + state
            first = None
            for g in range(2):
                rows = slice(g * QB, g * QB + QB)
                outer = dot(qkv[blk, rows, lanes(h * HEAD)], cots[blk, rows, lanes(h * HEAD)], 0, 0)
                term = outer * level_coef(pos, idx, table, blk, g, 1, h)
                first = term if first is None else first + term
                for k in range(4):
                    term = outer * level_coef(pos, idx, table, blk, g, k + 2, h)
                    sums[k] = term if sums[k] is None else sums[k] + term
            g1[blk, h] = first
        x0[zs, h] = total.astype(BF)
        for out, value in zip((m2, m3, m4, m5), sums):
            out[zs, h] = value.astype(out.dtype)


def local_kernel(pos, idx, table, qkv, cots, loc):
    rows = lax.broadcasted_iota(jnp.int32, (BLOCK, BLOCK), 0)
    cols = lax.broadcasted_iota(jnp.int32, (BLOCK, BLOCK), 1)
    causal = rows >= cols
    upper = rows < QB

    @pl.loop(0, 4)
    def _(blk):
        for h in range(2):
            qs = slice(h * HEAD, h * HEAD + HEAD)
            ks = slice(256 + h * HEAD, 256 + h * HEAD + HEAD)
            vs = slice(512 + h * HEAD, 512 + h * HEAD + HEAD)
            q, k, v, c = qkv[blk, :, qs], qkv[blk, :, ks], qkv[blk, :, vs], cots[blk, :, qs]
            scale = jnp.where(
                upper,
                level_coef(pos, idx, table, blk, 0, 0, h),
                level_coef(pos, idx, table, blk, 1, 0, h),
            )
            scale = jnp.where(causal, scale, 0.0)
            scores = (dot(q, k, 1, 1) * scale).astype(BF)
            dscores = (dot(c, v, 1, 1) * scale).astype(BF)
            loc[blk, :, qs] = dot(dscores, k, 1, 0)
            loc[blk, :, ks] = dot(dscores, q, 0, 0)
            loc[blk, :, vs] = dot(scores, c, 0, 0)
            loc[blk, :, 768 + h * HEAD : 768 + h * HEAD + HEAD] = dot(scores, v, 1, 0)


def gradient_pair(pos, toks, grads, dist, first, store):
    y, x, core, half = pos[0], pos[1], pos[2], pos[5]
    at = []
    for slot in (first, first + 1):
        yy = (y + dist + core * (slot - dist)) & 3
        xx = (x + slot + core * (dist - slot)) & 3
        at.append(lanes((yy * 4 + xx) * 128))
    part = None
    for blk in range(4):
        rows = jnp.concatenate([toks[blk][:, at[0]], toks[blk][:, at[1]]], axis=1)
        term = dot(rows, grads[blk], 0, 0)
        part = term if part is None else part + term
    part = part.astype(BF)
    for sub in range(2):
        for c in range(2):
            for piece in range(2):
                row = ((c + core) & 1) * 64 + ((piece + half) & 1) * 32
                start = sub * 128 + c * 64 + piece * 32
                store(sub, pl.ds(pl.multiple_of(row, 32), 32), part[start : start + 32])


def finish_kernel(pos, idx, table, *refs):
    toks = refs[0:4]
    cots, qkv, loc, s1, g1 = refs[4:9]
    cx1, cx2, cx3, cy1, cy2, cy3 = refs[9:15]
    own, r1, r2, r3 = refs[15:19]
    attn, grads, low, high = refs[19:]

    @pl.loop(0, 4)
    def _(step):
        zs, h = step // 2, step % 2
        far = [
            None,
            cx1[zs, h].astype(F32),
            cx2[zs, h].astype(F32) + cx3[zs, h].astype(F32),
            cy1[zs, h].astype(F32),
            cy2[zs, h].astype(F32) + cy3[zs, h].astype(F32),
        ]
        chip = own[zs, h].astype(F32) + r1[zs, h].astype(F32)
        chip = chip + r2[zs, h].astype(F32) + r3[zs, h].astype(F32)
        qs, ks = lanes(h * HEAD), lanes(256 + h * HEAD)
        vs, ats = lanes(512 + h * HEAD), lanes(768 + h * HEAD)
        for cs in range(2):
            blk = cs * 2 + zs
            other = (1 - cs) * 2 + zs
            far[0] = s1[other, h].astype(F32)
            grad = (chip + g1[other, h]).astype(BF)
            for g in range(2):
                rows = slice(g * QB, g * QB + QB)
                mixed = None
                for level in range(1, 6):
                    term = far[level - 1] * level_coef(pos, idx, table, blk, g, level, h)
                    mixed = term if mixed is None else mixed + term
                mixed = mixed.astype(BF)
                out = loc[blk, rows, ats] + dot(qkv[blk, rows, qs], mixed, 1, 0)
                attn[blk, rows, qs] = out.astype(BF)
                dq = loc[blk, rows, qs] + dot(cots[blk, rows, qs], mixed, 1, 1)
                grads[blk, rows, qs] = dq.astype(BF)
            dk = loc[blk, :, ks] + dot(qkv[blk, :, vs], grad, 1, 1)
            grads[blk, :, ks] = dk.astype(BF)
            dv = loc[blk, :, vs] + dot(qkv[blk, :, ks], grad, 1, 0)
            grads[blk, :, vs] = dv.astype(BF)

    for first, out in ((0, low), (2, high)):

        def store(sub, rows, value, out=out):
            out[sub, rows, :] = value

        gradient_pair(pos, toks, grads, 2, first, store)


def gradient_kernel(dists, pos, t0, t1, t2, t3, grads, _, *outs):
    toks = (t0, t1, t2, t3)

    @pl.loop(0, 2)
    def _(pair):
        for dist, out in zip(dists, outs):

            def store(sub, rows, value, out=out):
                out[pair * 2 + sub, rows, :] = value

            gradient_pair(pos, toks, grads, dist, pair * 2, store)


def total_kernel(pos, own, r1, r2, attn, from_core, from_z, t0, t1, t2, t3, attn_out):
    core, kind = pos[2], pos[4]
    for slot, out in enumerate((t0, t1, t2, t3)):
        total = own[slot].astype(F32) + r1[slot].astype(F32) + r2[slot].astype(F32)
        out[...] = total.astype(BF)
    attns = ((attn.at[0], from_z.at[0]), (from_core.at[0], from_z.at[1]))
    for cs in range(2):
        for zs in range(2):
            group = ((core + cs) & 1) * 2 + ((kind + zs) & 1)
            attn_out[:, pl.ds(pl.multiple_of(group * 256, 256), 256)] = attns[cs][zs][...]


def place_kernel(pos, mine, near, theirs, beyond, grad_w):
    core, kind = pos[2], pos[4]
    halves = (pos[5], pos[6])
    for cs in range(2):
        for zs in range(2):
            group = ((core + cs) & 1) * 2 + ((kind + zs) & 1)
            lane = pl.ds(pl.multiple_of(group * 256, 256), 256)
            for piece in range(2):
                part = ((mine, near), (theirs, beyond))[zs][piece]
                row = pl.ds(pl.multiple_of(((halves[zs] + piece) & 1) * 32, 32), 32)
                for third in range(3):
                    grad_w[third, row, lane] = part[
                        cs, :, third * 256 : third * 256 + 256
                    ].astype(F32)


def add(*parts):
    total = parts[0].astype(F32)
    for part in parts[1:]:
        total = total + part.astype(F32)
    return total.astype(BF)


def per_device(tokens, w_qkv, weight_table, weight_index, cotangent):
    y, x, core = lax.axis_index("y"), lax.axis_index("x"), lax.axis_index("core")
    z = lax.axis_index("dp")
    pos = jnp.stack(
        [y, x, core, z, (SETS >> z) & 1, (HALVES >> z) & 1, (HALVES >> (z ^ 1)) & 1]
    ).astype(jnp.int32)
    inputs = tokens[0]

    rows = weight_index.reshape(1, 12)
    rows = jnp.concatenate([rows, swap(rows, "dp", 8, 1)], axis=0)
    idx = jnp.concatenate([rows, swap(rows, "core", 2, 1)], axis=0)
    scalars = [pos, idx, weight_table]

    w_own, w_core = call(
        prepare_kernel,
        [pos, jnp.transpose(w_qkv, (1, 0, 2))],
        1,
        [((64, COLS), BF)] * 2,
        grant=58,
        nbytes=MIB,
    )
    c_own, c_core, c_z = call(
        split_kernel,
        [pos, cotangent[0]],
        1,
        [((BLOCK, 256), BF)] * 2 + [((BLOCK, 512), BF)],
        grant=58,
        nbytes=MIB,
    )

    chunk = jnp.concatenate([w_own, swap(w_core, "core", 2, 1)], axis=0)
    near = [chunk] + [ring(chunk, 0, step) for step in (1, 2, 3)]
    mine = [jnp.concatenate(near[:2], axis=0), jnp.concatenate(near[2:], axis=0)]
    behind_low, ahead_high = ring(mine[0], 1, 3), ring(mine[1], 1, 1)
    far = [ring(behind_low, 1, 3), ring(ahead_high, 1, 1)]
    tok01 = behind(swap(inputs, "dp", 8, 1), behind_low, ahead_high, index=rows)
    ahead_low = ring(behind(mine[0], tok01), 1, 1)
    behind_high = ring(behind(mine[1], tok01), 1, 3)
    gathered = mine + [ahead_low, ahead_high, behind_low, behind_high] + far

    c_core = swap(c_core, "core", 2, 1)
    c_z = swap(behind(c_z, tok01), "dp", 8, 1)
    c_near, c_across = c_z[:, :256], swap(c_z[:, 256:], "core", 2, 1)
    tok10 = swap(inputs, "core", 2, 1)
    tok11 = swap(tok01, "core", 2, 1)
    toks = [inputs, tok01, tok10, tok11]

    tile = (HEAD, HEAD)
    qkv, cots, s1, x0, g1, m2, m3, m4, m5 = call(
        project_kernel,
        scalars + toks + [c_own, c_near, c_core, c_across] + gathered,
        3,
        [
            ((4, BLOCK, COLS), BF),
            ((4, BLOCK, 256), BF),
            ((4, 2) + tile, BF),
            ((2, 2) + tile, BF),
            ((4, 2) + tile, F32),
            ((2, 2) + tile, F32),
            ((2, 2) + tile, F32),
            ((2, 2) + tile, BF),
            ((2, 2) + tile, BF),
        ],
        scratch=[pltpu.VMEM((D, COLS), BF)],
        grant=58,
        flops=2 * 1024 * D * COLS,
        nbytes=10 * MIB,
    )

    cx = [swap(x0, "x", 4, mask) for mask in (1, 2, 3)]
    dy = [swap(m, "y", 4, mask) for mask, m in ((1, m4), (2, m5), (3, m5))]
    (loc,) = call(
        local_kernel,
        scalars + [qkv, cots],
        3,
        [((4, BLOCK, 1024), F32)],
        grant=12,
        flops=8 * 6 * 2 * BLOCK * BLOCK * HEAD,
        nbytes=8 * MIB,
    )
    x1 = add(x0, *cx)
    cy = [swap(x1, "y", 4, mask) for mask in (1, 2, 3)]
    high = dy[0].astype(F32) + dy[1].astype(F32) + dy[2].astype(F32)
    near = (high + m2).astype(BF)
    far = (high + m3).astype(BF)
    dx = [swap(m, "x", 4, mask) for mask, m in ((1, near), (2, far), (3, far))]

    attn, grads, low, high = call(
        finish_kernel,
        scalars + toks + [cots, qkv, loc, s1, g1] + cx + cy + [high.astype(BF)] + dx,
        3,
        [
            ((4, BLOCK, 256), BF),
            ((4, BLOCK, COLS), BF),
            ((2, 128, COLS), BF),
            ((2, 128, COLS), BF),
        ],
        grant=24,
        flops=1024 * D * COLS,
        nbytes=12 * MIB,
    )
    low, high = ring(low, 1, 3), ring(high, 1, 1)
    from_core = swap(attn[2:], "core", 2, 1)
    onward, backward = call(
        functools.partial(gradient_kernel, (1, 3)),
        [pos] + toks + [grads, from_core],
        1,
        [((4, 128, COLS), BF)] * 2,
        grant=20,
        flops=1024 * D * COLS,
        nbytes=9 * MIB,
        n_any=1,
    )
    onward = jnp.concatenate([add(onward[:2], low), onward[2:]], axis=0)
    backward = jnp.concatenate([backward[:2], add(backward[2:], high)], axis=0)
    onward, backward = ring(onward, 1, 3), ring(backward, 1, 1)
    back = swap(jnp.stack([attn[1], from_core[1]], axis=0), "dp", 8, 1)
    (own,) = call(
        functools.partial(gradient_kernel, (0,)),
        [pos] + toks + [grads, from_core],
        1,
        [((4, 128, COLS), BF)],
        grant=20,
        flops=1024 * 512 * COLS,
        nbytes=9 * MIB,
        n_any=1,
    )
    *total, attn_out = call(
        total_kernel,
        [pos, own, onward, backward, attn, from_core, back],
        1,
        [((128, COLS), BF)] * 4 + [((BLOCK, 1024), BF)],
        grant=10,
        nbytes=4 * MIB,
    )
    chip_sum = add(total[0], *[ring(total[step], 0, -step) for step in (1, 2, 3)])
    pair = jnp.stack([chip_sum[:64], swap(chip_sum[64:], "core", 2, 1)], axis=0)
    mine = add(pair[:, :32], same_set_neighbour(pair[:, 32:]))
    mine = add(mine, same_set_far(mine))
    near = same_set_neighbour(mine)
    theirs = swap(mine, "dp", 8, 1)
    beyond = swap(near, "dp", 8, 1)

    (grad_w,) = call(
        place_kernel,
        [pos, mine, near, theirs, beyond],
        1,
        [((3, 64, 1024), F32)],
        grant=6,
        nbytes=3 * MIB,
    )
    return attn_out[None], jnp.transpose(grad_w, (1, 0, 2))


def solution(mesh):
    grid = Mesh(mesh.devices.reshape(4, 4, 2, 8), ("y", "x", "core", "dp"))
    seq = ("y", "x", "core")
    return jax.shard_map(
        per_device,
        mesh=grid,
        in_specs=(P("dp", seq, None), P(seq, None, None), P(), P("dp", seq, None), P("dp", seq, None)),
        out_specs=(P("dp", seq, None), P(seq, None, None)),
        check_vma=False,
    )
```

profile of v0, /device:TPU:6, one launch (start us, length us, event | category | flops | bytes accessed | tf_op | source)
XLA Modules:
  0.0 164.7 jit_solution(8334341411682430996)
XLA Ops:
  3.1 1.9 %collective-permute-start = (bf16[256,2048]{1,0:T(8,128)(2,1)}, bf16[256,2048]{1,0:T(8,128)(2,1)S(1)}, u32[]{:S(2)}, u32[]{:S(2)}) collective-permute-start(bf16[256,2048]{1,0:T(8,128)(2,1)} %bitcast.17), channel_id=1, source_target_pairs={{0,1},{1,0},{2,3},{3,2},{4,5},{5,4},{6,7},{7,6},{8,9},{9,8},{10,11... | collective-permute-start | bytes 3145736 | tf_op jit(solution)/shard_map/ppermute | solution.py:34
  9.1 2.1 %collective-permute-start.5 = (bf16[128,768]{1,0:T(8,128)(2,1)S(1)}, bf16[128,768]{1,0:T(8,128)(2,1)S(1)}, u32[]{:S(2)}, u32[]{:S(2)}) collective-permute-start(bf16[128,768]{1,0:T(8,128)(2,1)S(1)} %get-tuple-element.59), channel_id=1, source_target_pairs={{0,16},{8,72},{16,32},{24,88},{32,48},{40,104},{48,0},{56,120},{64... | collective-permute-start | bytes 589832 | tf_op jit(solution)/shard_map/ppermute | solution.py:30
  11.2 4.9 %collective-permute-done.2 = bf16[128,768]{1,0:T(8,128)(2,1)S(1)} collective-permute-done((bf16[128,768]{1,0:T(8,128)(2,1)S(1)}, bf16[128,768]{1,0:T(8,128)(2,1)S(1)}, u32[]{:S(2)}, u32[]{:S(2)}) %collective-permute-start.2) | collective-permute-done | bytes 196640 | tf_op jit(solution)/shard_map/ppermute | solution.py:30
  20.4 1.9 %shard_map.69 = (bf16[256,256]{1,0:T(8,128)(2,1)}, bf16[256,256]{1,0:T(8,128)(2,1)}, bf16[256,512]{1,0:T(8,128)(2,1)}) custom-call(s32[7]{0:T(128)} %stack.43.pos, bf16[256,1024]{1,0:T(8,128)(2,1)} %bitcast.27), custom_call_target="tpu_custom_call" | custom-call | bytes 1048576 | tf_op jit(solution)/shard_map/pallas_call | solution.py:65
  22.3 6.8 %collective-permute-done.7 = s32[1,12]{1,0:T(1,128)S(1)} collective-permute-done((s32[1,12]{1,0:T(1,128)S(1)}, s32[1,12]{1,0:T(1,128)S(1)}, u32[]{:S(2)}, u32[]{:S(2)}) %collective-permute-start.7) | collective-permute-done | bytes 80 | tf_op jit(solution)/shard_map/ppermute | solution.py:34
  38.4 1.8 %collective-permute-start.11 = (bf16[256,512]{1,0:T(8,128)(2,1)S(1)}, bf16[256,512]{1,0:T(8,128)(2,1)S(1)}, u32[]{:S(2)}, u32[]{:S(2)}) collective-permute-start(bf16[256,512]{1,0:T(8,128)(2,1)S(1)} %add_convert_fusion.5), channel_id=1, source_target_pairs={{0,1},{1,0},{2,3},{3,2},{4,5},{5,4},{6,7},{7,6},{8,9},{9,8},{10,11... | collective-permute-start | bytes 786440 | tf_op jit(solution)/shard_map/ppermute | solution.py:34
  42.6 1.8 %add_convert_fusion.4 = bf16[256,768]{1,0:T(8,128)(2,1)} fusion(bf16[256,768]{1,0:T(8,128)(2,1)} %constant_dynamic-update-slice_fusion.2.refs_0_, f32[]{:T(128)} %bitcast.11), kind=kLoop, calls=%fused_computation.6 | loop fusion | flops 589824 | bytes 786436 | tf_op jit(solution)/shard_map/convert_element_type | solution.py:49
  46.1 1.8 %collective-permute-start.14 = (bf16[256,768]{1,0:T(8,128)(2,1)}, bf16[256,768]{1,0:T(8,128)(2,1)S(1)}, u32[]{:S(2)}, u32[]{:S(2)}) collective-permute-start(bf16[256,768]{1,0:T(8,128)(2,1)} %add_convert_fusion.4), channel_id=1, source_target_pairs={{0,192},{8,56},{16,208},{24,8},{32,224},{40,24},{48,240},{56,40},{... | collective-permute-start | bytes 1179656 | tf_op jit(solution)/shard_map/ppermute | solution.py:30
  52.5 4.2 %collective-permute-done.14.refs_2_ = bf16[256,768]{1,0:T(8,128)(2,1)S(1)} collective-permute-done((bf16[256,768]{1,0:T(8,128)(2,1)}, bf16[256,768]{1,0:T(8,128)(2,1)S(1)}, u32[]{:S(2)}, u32[]{:S(2)}) %collective-permute-start.14) | collective-permute-done | bytes 393248 | tf_op jit(solution)/shard_map/ppermute | solution.py:30
  57.9 10.2 %shard_map.70 = (bf16[4,256,768]{2,1,0:T(8,128)(2,1)}, bf16[4,256,256]{2,1,0:T(8,128)(2,1)}, bf16[4,2,128,128]{3,2,1,0:T(8,128)(2,1)}, bf16[2,2,128,128]{3,2,1,0...) custom-call(s32[7]{0:T(128)} %stack.43.pos, ...), custom_call_target="tpu_custom_call" | custom-call | flops 3221225472 | bytes 10485760 | tf_op jit(solution)/shard_map/pallas_call | solution.py:65
  69.5 1.9 %collective-permute-start.26 = (bf16[2,2,128,128]{3,2,1,0:T(8,128)(2,1)}, bf16[2,2,128,128]{3,2,1,0:T(8,128)(2,1)S(1)}, u32[]{:S(2)}, u32[]{:S(2)}) collective-permute-start(bf16[2,2,128,128]{3,2,1,0:T(8,128)(2,1)} %get-tuple-element.38), channel_id=1, source_target_pairs={{0,192},{64,128},{128,64},{192,0},{1,193},{65,129},{129,65},{193,1... | collective-permute-start | bytes 393224 | tf_op jit(solution)/shard_map/ppermute | solution.py:34
  76.4 2.2 %collective-permute-done.26 = bf16[2,2,128,128]{3,2,1,0:T(8,128)(2,1)S(1)} collective-permute-done((bf16[2,2,128,128]{3,2,1,0:T(8,128)(2,1)}, bf16[2,2,128,128]{3,2,1,0:T(8,128)(2,1)S(1)}, u32[]{:S(2)}, u32[]{:S(2)}) %collective-permute-start.26) | collective-permute-done | bytes 131104 | tf_op jit(solution)/shard_map/ppermute | solution.py:34
  80.3 2.3 %collective-permute-start.28 = (bf16[2,2,128,128]{3,2,1,0:T(8,128)(2,1)S(1)}, bf16[2,2,128,128]{3,2,1,0:T(8,128)(2,1)S(1)}, u32[]{:S(2)}, u32[]{:S(2)}) collective-permute-start(bf16[2,2,128,128]{3,2,1,0:T(8,128)(2,1)S(1)} %get-tuple-element.52), channel_id=1, source_target_pairs={{0,32},{16,48},{32,0},{48,16},{1,33},{17,49},{33,1},{49,17},{2,34}... | collective-permute-start | bytes 393224 | tf_op jit(solution)/shard_map/ppermute | solution.py:34
  90.2 4.4 %shard_map.71.refs_6_ = f32[4,256,1024]{2,1,0:T(8,128)S(1)} custom-call(s32[7]{0:T(128)S(1)} %copy-done.12, s32[4,12]{1,0:T(4,128)S(1)} %copy-done.13, f32[16,8]{1,0:T(8,128)S(1)} %copy-done.11, bf16[4,256,768]{2,1,0:T(8,128)(2,1)S(1)} %copy-done.6, bf16[4,256,256]{2,1,0:T(8,128)(2,1)S(1)} %copy-done.7), custom_call_target="tpu_custom_call" | custom-call | flops 805306368 | bytes 8388608 | tf_op jit(solution)/shard_map/pallas_call | solution.py:65
  94.7 3.9 %shard_map.72 = (bf16[4,256,256]{2,1,0:T(8,128)(2,1)S(1)}, bf16[4,256,768]{2,1,0:T(8,128)(2,1)S(1)}, bf16[2,128,768]{2,1,0:T(8,128)(2,1)S(1)}, bf16[2,128,768]{2,1,0:T(8,128)(2,1)S(1)}) custom-call(s32[7]{0:T(128)S(1)} %copy-done.12, s32[4,12]{1,0:T(4,128)S(1)} %copy-done.13, f32[16,8]{1,0:T(8,128)S(1)} %copy-done.11, bf16[256,2048]{1,0:T(8,128)(2,1)S(1)} %bitcast.20, ...), custom_call_target="tpu_custom_call" | custom-call | flops 1610612736 | bytes 12582912 | tf_op jit(solution)/shard_map/pallas_call | solution.py:65
  101.0 3.3 %shard_map.74 = (bf16[4,128,768]{2,1,0:T(8,128)(2,1)S(1)}, bf16[4,128,768]{2,1,0:T(8,128)(2,1)S(1)}) custom-call(s32[7]{0:T(128)S(1)} %copy-done.12, bf16[256,2048]{1,0:T(8,128)(2,1)S(1)} %bitcast.21, bf16[256,2048]{1,0:T(8,128)(2,1)S(1)} %copy-done.1, bf16[256,2048]{1,0:T(8,128)(2,1)S(1)} %copy-done.5, bf16[256,2048]{1,0:T(8,128)(2,1)} %collective-permute-done.9.t3.refs_3_, ...), custom_call_target="tpu_custom_call" | custom-call | flops 1610612736 | bytes 9437184 | tf_op jit(solution)/shard_map/pallas_call | solution.py:65
  104.4 2.3 %collective-permute-done.33 = bf16[2,128,768]{2,1,0:T(8,128)(2,1)S(1)} collective-permute-done((bf16[2,128,768]{2,1,0:T(8,128)(2,1)S(1)}, bf16[2,128,768]{2,1,0:T(8,128)(2,1)S(1)}, u32[]{:S(2)}, u32[]{:S(2)}) %collective-permute-start.33) | collective-permute-done | bytes 393248 | tf_op jit(solution)/shard_map/ppermute | solution.py:30
  107.0 2.7 %collective-permute-start.34 = (bf16[4,128,768]{2,1,0:T(8,128)(2,1)S(1)}, bf16[4,128,768]{2,1,0:T(8,128)(2,1)S(1)}, u32[]{:S(2)}, u32[]{:S(2)}) collective-permute-start(bf16[4,128,768]{2,1,0:T(8,128)(2,1)S(1)} %pad_maximum_fusion.1), channel_id=1, source_target_pairs={{0,192},{8,56},{16,208},{24,8},{32,224},{40,24},{48,240},{56,40},{... | collective-permute-start | bytes 2359304 | tf_op jit(solution)/shard_map/ppermute | solution.py:30
  110.8 2.5 %shard_map.73.own = bf16[4,128,768]{2,1,0:T(8,128)(2,1)S(1)} custom-call(s32[7]{0:T(128)S(1)} %copy-done.12, bf16[256,2048]{1,0:T(8,128)(2,1)S(1)} %bitcast.22, bf16[256,2048]{1,0:T(8,128)(2,1)S(1)} %copy-done.1, bf16[256,2048]{1,0:T(8,128)(2,1)S(1)} %copy-done.5, bf16[256,2048]{1,0:T(8,128)(2,1)} %collective-permute-done.9.t3.refs_3_, ...), custom_call_target="tpu_custom_call" | custom-call | flops 402653184 | bytes 9437184 | tf_op jit(solution)/shard_map/pallas_call | solution.py:65
  113.3 5.6 %collective-permute-done.35.from_z = bf16[2,256,256]{2,1,0:T(8,128)(2,1)S(1)} collective-permute-done((bf16[2,256,256]{2,1,0:T(8,128)(2,1)S(1)}, bf16[2,256,256]{2,1,0:T(8,128)(2,1)S(1)}, u32[]{:S(2)}, u32[]{:S(2)}) %collective-permute-start.35) | collective-permute-done | bytes 262176 | tf_op jit(solution)/shard_map/ppermute | solution.py:34
  119.2 3.9 %collective-permute-done.32.r1 = bf16[4,128,768]{2,1,0:T(8,128)(2,1)S(1)} collective-permute-done((bf16[4,128,768]{2,1,0:T(8,128)(2,1)S(1)}, bf16[4,128,768]{2,1,0:T(8,128)(2,1)S(1)}, u32[]{:S(2)}, u32[]{:S(2)}) %collective-permute-start.32) | collective-permute-done | bytes 786464 | tf_op jit(solution)/shard_map/ppermute | solution.py:30
  125.3 2.2 %collective-permute-start.37 = (bf16[128,768]{1,0:T(8,128)(2,1)S(1)}, bf16[128,768]{1,0:T(8,128)(2,1)S(1)}, u32[]{:S(2)}, u32[]{:S(2)}) collective-permute-start(bf16[128,768]{1,0:T(8,128)(2,1)S(1)} %get-tuple-element.50), channel_id=1, source_target_pairs={{0,32},{8,136},{16,48},{24,152},{32,0},{40,168},{48,16},{56,184},{... | collective-permute-start | bytes 589832 | tf_op jit(solution)/shard_map/ppermute | solution.py:30
  127.6 2.8 %collective-permute-done.36 = bf16[128,768]{1,0:T(8,128)(2,1)S(1)} collective-permute-done((bf16[128,768]{1,0:T(8,128)(2,1)S(1)}, bf16[128,768]{1,0:T(8,128)(2,1)S(1)}, u32[]{:S(2)}, u32[]{:S(2)}) %collective-permute-start.36) | collective-permute-done | bytes 196640 | tf_op jit(solution)/shard_map/ppermute | solution.py:30
  130.4 2.1 %collective-permute-done.37 = bf16[128,768]{1,0:T(8,128)(2,1)S(1)} collective-permute-done((bf16[128,768]{1,0:T(8,128)(2,1)S(1)}, bf16[128,768]{1,0:T(8,128)(2,1)S(1)}, u32[]{:S(2)}, u32[]{:S(2)}) %collective-permute-start.37) | collective-permute-done | bytes 196640 | tf_op jit(solution)/shard_map/ppermute | solution.py:30
  132.5 2.1 %collective-permute-done.38 = bf16[128,768]{1,0:T(8,128)(2,1)S(1)} collective-permute-done((bf16[128,768]{1,0:T(8,128)(2,1)S(1)}, bf16[128,768]{1,0:T(8,128)(2,1)S(1)}, u32[]{:S(2)}, u32[]{:S(2)}) %collective-permute-start.38) | collective-permute-done | bytes 196640 | tf_op jit(solution)/shard_map/ppermute | solution.py:30
  136.1 5.0 %collective-permute-start.40 = (bf16[2,32,768]{2,1,0:T(8,128)(2,1)S(1)}, bf16[2,32,768]{2,1,0:T(8,128)(2,1)S(1)}, u32[]{:S(2)}, u32[]{:S(2)}) collective-permute-start(bf16[2,32,768]{2,1,0:T(8,128)(2,1)S(1)} %pad_maximum_fusion.3), channel_id=1, source_target_pairs={{0,7},{1,2},{2,1},{3,4},{4,3},{5,6},{6,5},{7,0},{8,15},{9,10},{10,... | collective-permute-start | bytes 294920 | tf_op jit(solution)/shard_map/ppermute | solution.py:38
  141.1 3.1 %collective-permute-done.40 = bf16[2,32,768]{2,1,0:T(8,128)(2,1)S(1)} collective-permute-done((bf16[2,32,768]{2,1,0:T(8,128)(2,1)S(1)}, bf16[2,32,768]{2,1,0:T(8,128)(2,1)S(1)}, u32[]{:S(2)}, u32[]{:S(2)}) %collective-permute-start.40) | collective-permute-done | bytes 98336 | tf_op jit(solution)/shard_map/ppermute | solution.py:38
  144.2 2.0 %collective-permute-start.41 = (bf16[2,32,768]{2,1,0:T(8,128)(2,1)S(1)}, bf16[2,32,768]{2,1,0:T(8,128)(2,1)S(1)}, u32[]{:S(2)}, u32[]{:S(2)}) collective-permute-start(bf16[2,32,768]{2,1,0:T(8,128)(2,1)S(1)} %add_convert_fusion.11), channel_id=1, source_target_pairs={{0,3},{1,6},{2,5},{3,0},{4,7},{5,2},{6,1},{7,4},{8,11},{9,14},{10,... | collective-permute-start | bytes 294920 | tf_op jit(solution)/shard_map/ppermute | solution.py:42
  146.2 6.4 %collective-permute-done.41 = bf16[2,32,768]{2,1,0:T(8,128)(2,1)S(1)} collective-permute-done((bf16[2,32,768]{2,1,0:T(8,128)(2,1)S(1)}, bf16[2,32,768]{2,1,0:T(8,128)(2,1)S(1)}, u32[]{:S(2)}, u32[]{:S(2)}) %collective-permute-start.41) | collective-permute-done | bytes 98336 | tf_op jit(solution)/shard_map/ppermute | solution.py:42
  152.6 2.6 %collective-permute-start.42 = (bf16[2,32,768]{2,1,0:T(8,128)(2,1)S(1)}, bf16[2,32,768]{2,1,0:T(8,128)(2,1)S(1)}, u32[]{:S(2)}, u32[]{:S(2)}) collective-permute-start(bf16[2,32,768]{2,1,0:T(8,128)(2,1)S(1)} %add_convert_fusion.10.mine), channel_id=1, source_target_pairs={{0,7},{1,2},{2,1},{3,4},{4,3},{5,6},{6,5},{7,0},{8,15},{9,10},{10,... | collective-permute-start | bytes 294920 | tf_op jit(solution)/shard_map/ppermute | solution.py:38
  155.3 3.3 %collective-permute-done.42.near = bf16[2,32,768]{2,1,0:T(8,128)(2,1)S(1)} collective-permute-done((bf16[2,32,768]{2,1,0:T(8,128)(2,1)S(1)}, bf16[2,32,768]{2,1,0:T(8,128)(2,1)S(1)}, u32[]{:S(2)}, u32[]{:S(2)}) %collective-permute-start.42) | collective-permute-done | bytes 98336 | tf_op jit(solution)/shard_map/ppermute | solution.py:38
  160.3 2.8 %collective-permute-done.44.beyond = bf16[2,32,768]{2,1,0:T(8,128)(2,1)S(1)} collective-permute-done((bf16[2,32,768]{2,1,0:T(8,128)(2,1)S(1)}, bf16[2,32,768]{2,1,0:T(8,128)(2,1)S(1)}, u32[]{:S(2)}, u32[]{:S(2)}) %collective-permute-start.44) | collective-permute-done | bytes 98336 | tf_op jit(solution)/shard_map/ppermute | solution.py:34
  (153 shorter events, 54.0 us)
Async XLA Ops:
  3.1 31.6 %collective-permute-start = (bf16[256,2048]{1,0:T(8,128)(2,1)}, bf16[256,2048]{1,0:T(8,128)(2,1)S(1)}, u32[]{:S(2)}, u32[]{:S(2)}) collective-permute-start(bf16[256,2048]{1,0:T(8,128)(2,1)} %bitcast.17), channel_id=1, source_target_pairs={{0,1},{1,0},{2,3},{3,2},{4,5},{5,4},{6,7},{7,6},{8,9},{9,8},{10,11... | collective-permute-start | bytes 3145736 | tf_op jit(solution)/shard_map/ppermute | solution.py:34
  7.2 9.0 %collective-permute-start.2 = (bf16[128,768]{1,0:T(8,128)(2,1)S(1)}, bf16[128,768]{1,0:T(8,128)(2,1)S(1)}, u32[]{:S(2)}, u32[]{:S(2)}) collective-permute-start(bf16[128,768]{1,0:T(8,128)(2,1)S(1)} %get-tuple-element.59), channel_id=1, source_target_pairs={{0,48},{8,200},{16,0},{24,216},{32,16},{40,232},{48,32},{56,248},{... | collective-permute-start | bytes 589832 | tf_op jit(solution)/shard_map/ppermute | solution.py:30
  8.0 10.4 %collective-permute-start.4 = (bf16[128,768]{1,0:T(8,128)(2,1)S(1)}, bf16[128,768]{1,0:T(8,128)(2,1)S(1)}, u32[]{:S(2)}, u32[]{:S(2)}) collective-permute-start(bf16[128,768]{1,0:T(8,128)(2,1)S(1)} %get-tuple-element.59), channel_id=1, source_target_pairs={{0,32},{8,136},{16,48},{24,152},{32,0},{40,168},{48,16},{56,184},{... | collective-permute-start | bytes 589832 | tf_op jit(solution)/shard_map/ppermute | solution.py:30
  9.1 9.3 %collective-permute-start.5 = (bf16[128,768]{1,0:T(8,128)(2,1)S(1)}, bf16[128,768]{1,0:T(8,128)(2,1)S(1)}, u32[]{:S(2)}, u32[]{:S(2)}) collective-permute-start(bf16[128,768]{1,0:T(8,128)(2,1)S(1)} %get-tuple-element.59), channel_id=1, source_target_pairs={{0,16},{8,72},{16,32},{24,88},{32,48},{40,104},{48,0},{56,120},{64... | collective-permute-start | bytes 589832 | tf_op jit(solution)/shard_map/ppermute | solution.py:30
  16.8 13.5 %collective-permute-start.3 = (bf16[256,768]{1,0:T(8,128)(2,1)}, bf16[256,768]{1,0:T(8,128)(2,1)}, u32[]{:S(2)}, u32[]{:S(2)}) collective-permute-start(bf16[256,768]{1,0:T(8,128)(2,1)} %constant_dynamic-update-slice_fusion.2.refs_0_), channel_id=1, source_target_pairs={{0,64},{8,24},{16,80},{24,40},{32,96},{40,56},{48,112},{56,8},{64,... | collective-permute-start | bytes 1179656 | tf_op jit(solution)/shard_map/ppermute | solution.py:30
  18.5 13.6 %collective-permute-start.6 = (bf16[256,768]{1,0:T(8,128)(2,1)S(1)}, bf16[256,768]{1,0:T(8,128)(2,1)}, u32[]{:S(2)}, u32[]{:S(2)}) collective-permute-start(bf16[256,768]{1,0:T(8,128)(2,1)S(1)} %constant_dynamic-update-slice_fusion.5.refs_1_), channel_id=1, source_target_pairs={{0,192},{8,56},{16,208},{24,8},{32,224},{40,24},{48,240},{56,40},{... | collective-permute-start | bytes 1179656 | tf_op jit(solution)/shard_map/ppermute | solution.py:30
  20.2 25.9 %collective-permute-start.8 = (bf16[256,2048]{1,0:T(8,128)(2,1)S(1)}, bf16[256,2048]{1,0:T(8,128)(2,1)S(1)}, u32[]{:S(2)}, u32[]{:S(2)}) collective-permute-start(bf16[256,2048]{1,0:T(8,128)(2,1)S(1)} %bitcast.19), channel_id=1, source_target_pairs={{0,8},{8,0},{1,9},{9,1},{2,10},{10,2},{3,11},{11,3},{4,12},{12,4},... | collective-permute-start | bytes 3145736 | tf_op jit(solution)/shard_map/ppermute | solution.py:34
  20.3 8.8 %collective-permute-start.7 = (s32[1,12]{1,0:T(1,128)S(1)}, s32[1,12]{1,0:T(1,128)S(1)}, u32[]{:S(2)}, u32[]{:S(2)}) collective-permute-start(s32[1,12]{1,0:T(1,128)S(1)} %reshape.19), channel_id=1, source_target_pairs={{0,1},{1,0},{2,3},{3,2},{4,5},{5,4},{6,7},{7,6},{8,9},{9,8},{10,11... | collective-permute-start | bytes 152 | tf_op jit(solution)/shard_map/ppermute | solution.py:34
  29.1 15.3 %collective-permute-start.12 = (bf16[256,256]{1,0:T(8,128)(2,1)}, bf16[256,256]{1,0:T(8,128)(2,1)S(1)}, u32[]{:S(2)}, u32[]{:S(2)}) collective-permute-start(bf16[256,256]{1,0:T(8,128)(2,1)} %get-tuple-element.31), channel_id=1, source_target_pairs={{0,8},{8,0},{1,9},{9,1},{2,10},{10,2},{3,11},{11,3},{4,12},{12,4},... | collective-permute-start | bytes 393224 | tf_op jit(solution)/shard_map/ppermute | solution.py:34
  30.3 10.7 %collective-permute-start.10 = (s32[2,12]{1,0:T(2,128)S(1)}, s32[2,12]{1,0:T(2,128)S(1)}, u32[]{:S(2)}, u32[]{:S(2)}) collective-permute-start(s32[2,12]{1,0:T(2,128)S(1)} %pad_add_fusion.1), channel_id=1, source_target_pairs={{0,8},{8,0},{1,9},{9,1},{2,10},{10,2},{3,11},{11,3},{4,12},{12,4},... | collective-permute-start | bytes 296 | tf_op jit(solution)/shard_map/ppermute | solution.py:34
  37.6 19.5 %collective-permute-start.9 = (bf16[256,2048]{1,0:T(8,128)(2,1)S(1)}, bf16[256,2048]{1,0:T(8,128)(2,1)}, u32[]{:S(2)}, u32[]{:S(2)}) collective-permute-start(bf16[256,2048]{1,0:T(8,128)(2,1)S(1)} %add_convert_fusion.t1.refs_1_), channel_id=1, source_target_pairs={{0,8},{8,0},{1,9},{9,1},{2,10},{10,2},{3,11},{11,3},{4,12},{12,4},... | collective-permute-start | bytes 3145736 | tf_op jit(solution)/shard_map/ppermute | solution.py:34
  38.4 9.6 %collective-permute-start.11 = (bf16[256,512]{1,0:T(8,128)(2,1)S(1)}, bf16[256,512]{1,0:T(8,128)(2,1)S(1)}, u32[]{:S(2)}, u32[]{:S(2)}) collective-permute-start(bf16[256,512]{1,0:T(8,128)(2,1)S(1)} %add_convert_fusion.5), channel_id=1, source_target_pairs={{0,1},{1,0},{2,3},{3,2},{4,5},{5,4},{6,7},{7,6},{8,9},{9,8},{10,11... | collective-permute-start | bytes 786440 | tf_op jit(solution)/shard_map/ppermute | solution.py:34
  41.0 9.2 %collective-permute-start.16 = (bf16[256,768]{1,0:T(8,128)(2,1)}, bf16[256,768]{1,0:T(8,128)(2,1)S(1)}, u32[]{:S(2)}, u32[]{:S(2)}) collective-permute-start(bf16[256,768]{1,0:T(8,128)(2,1)} %collective-permute-done.3.refs_4_), channel_id=1, source_target_pairs={{0,64},{8,24},{16,80},{24,40},{32,96},{40,56},{48,112},{56,8},{64,... | collective-permute-start | bytes 1179656 | tf_op jit(solution)/shard_map/ppermute | solution.py:30
  44.4 8.1 %collective-permute-start.17 = (bf16[256,768]{1,0:T(8,128)(2,1)}, bf16[256,768]{1,0:T(8,128)(2,1)S(1)}, u32[]{:S(2)}, u32[]{:S(2)}) collective-permute-start(bf16[256,768]{1,0:T(8,128)(2,1)} %collective-permute-done.6.refs_3_), channel_id=1, source_target_pairs={{0,192},{8,56},{16,208},{24,8},{32,224},{40,24},{48,240},{56,40},{... | collective-permute-start | bytes 1179656 | tf_op jit(solution)/shard_map/ppermute | solution.py:30
  46.1 10.5 %collective-permute-start.14 = (bf16[256,768]{1,0:T(8,128)(2,1)}, bf16[256,768]{1,0:T(8,128)(2,1)S(1)}, u32[]{:S(2)}, u32[]{:S(2)}) collective-permute-start(bf16[256,768]{1,0:T(8,128)(2,1)} %add_convert_fusion.4), channel_id=1, source_target_pairs={{0,192},{8,56},{16,208},{24,8},{32,224},{40,24},{48,240},{56,40},{... | collective-permute-start | bytes 1179656 | tf_op jit(solution)/shard_map/ppermute | solution.py:30
  47.9 9.2 %collective-permute-start.15 = (bf16[256,768]{1,0:T(8,128)(2,1)}, bf16[256,768]{1,0:T(8,128)(2,1)S(1)}, u32[]{:S(2)}, u32[]{:S(2)}) collective-permute-start(bf16[256,768]{1,0:T(8,128)(2,1)} %add_convert_fusion.3), channel_id=1, source_target_pairs={{0,64},{8,24},{16,80},{24,40},{32,96},{40,56},{48,112},{56,8},{64,... | collective-permute-start | bytes 1179656 | tf_op jit(solution)/shard_map/ppermute | solution.py:30
  69.5 9.1 %collective-permute-start.26 = (bf16[2,2,128,128]{3,2,1,0:T(8,128)(2,1)}, bf16[2,2,128,128]{3,2,1,0:T(8,128)(2,1)S(1)}, u32[]{:S(2)}, u32[]{:S(2)}) collective-permute-start(bf16[2,2,128,128]{3,2,1,0:T(8,128)(2,1)} %get-tuple-element.38), channel_id=1, source_target_pairs={{0,192},{64,128},{128,64},{192,0},{1,193},{65,129},{129,65},{193,1... | collective-permute-start | bytes 393224 | tf_op jit(solution)/shard_map/ppermute | solution.py:34
  71.3 7.2 %collective-permute-start.25 = (bf16[2,2,128,128]{3,2,1,0:T(8,128)(2,1)}, bf16[2,2,128,128]{3,2,1,0:T(8,128)(2,1)S(1)}, u32[]{:S(2)}, u32[]{:S(2)}) collective-permute-start(bf16[2,2,128,128]{3,2,1,0:T(8,128)(2,1)} %get-tuple-element.38), channel_id=1, source_target_pairs={{0,128},{64,192},{128,0},{192,64},{1,129},{65,193},{129,1},{193,65... | collective-permute-start | bytes 393224 | tf_op jit(solution)/shard_map/ppermute | solution.py:34
  72.3 10.3 %collective-permute-start.20 = (bf16[2,2,128,128]{3,2,1,0:T(8,128)(2,1)}, bf16[2,2,128,128]{3,2,1,0:T(8,128)(2,1)S(1)}, u32[]{:S(2)}, u32[]{:S(2)}) collective-permute-start(bf16[2,2,128,128]{3,2,1,0:T(8,128)(2,1)} %get-tuple-element.36), channel_id=1, source_target_pairs={{0,48},{16,32},{32,16},{48,0},{1,49},{17,33},{33,17},{49,1},{2,50}... | collective-permute-start | bytes 393224 | tf_op jit(solution)/shard_map/ppermute | solution.py:34
  73.6 10.3 %collective-permute-start.19 = (bf16[2,2,128,128]{3,2,1,0:T(8,128)(2,1)}, bf16[2,2,128,128]{3,2,1,0:T(8,128)(2,1)S(1)}, u32[]{:S(2)}, u32[]{:S(2)}) collective-permute-start(bf16[2,2,128,128]{3,2,1,0:T(8,128)(2,1)} %get-tuple-element.36), channel_id=1, source_target_pairs={{0,32},{16,48},{32,0},{48,16},{1,33},{17,49},{33,1},{49,17},{2,34}... | collective-permute-start | bytes 393224 | tf_op jit(solution)/shard_map/ppermute | solution.py:34
  75.2 8.7 %collective-permute-start.18 = (bf16[2,2,128,128]{3,2,1,0:T(8,128)(2,1)}, bf16[2,2,128,128]{3,2,1,0:T(8,128)(2,1)S(1)}, u32[]{:S(2)}, u32[]{:S(2)}) collective-permute-start(bf16[2,2,128,128]{3,2,1,0:T(8,128)(2,1)} %get-tuple-element.36), channel_id=1, source_target_pairs={{0,16},{16,0},{32,48},{48,32},{1,17},{17,1},{33,49},{49,33},{2,18}... | collective-permute-start | bytes 393224 | tf_op jit(solution)/shard_map/ppermute | solution.py:34
  79.7 14.9 %collective-permute-start.29 = (bf16[2,2,128,128]{3,2,1,0:T(8,128)(2,1)S(1)}, bf16[2,2,128,128]{3,2,1,0:T(8,128)(2,1)S(1)}, u32[]{:S(2)}, u32[]{:S(2)}) collective-permute-start(bf16[2,2,128,128]{3,2,1,0:T(8,128)(2,1)S(1)} %get-tuple-element.52), channel_id=1, source_target_pairs={{0,48},{16,32},{32,16},{48,0},{1,49},{17,33},{33,17},{49,1},{2,50}... | collective-permute-start | bytes 393224 | tf_op jit(solution)/shard_map/ppermute | solution.py:34
  80.3 14.3 %collective-permute-start.28 = (bf16[2,2,128,128]{3,2,1,0:T(8,128)(2,1)S(1)}, bf16[2,2,128,128]{3,2,1,0:T(8,128)(2,1)S(1)}, u32[]{:S(2)}, u32[]{:S(2)}) collective-permute-start(bf16[2,2,128,128]{3,2,1,0:T(8,128)(2,1)S(1)} %get-tuple-element.52), channel_id=1, source_target_pairs={{0,32},{16,48},{32,0},{48,16},{1,33},{17,49},{33,1},{49,17},{2,34}... | collective-permute-start | bytes 393224 | tf_op jit(solution)/shard_map/ppermute | solution.py:34
  84.9 9.7 %collective-permute-start.23 = (bf16[2,2,128,128]{3,2,1,0:T(8,128)(2,1)S(1)}, bf16[2,2,128,128]{3,2,1,0:T(8,128)(2,1)S(1)}, u32[]{:S(2)}, u32[]{:S(2)}) collective-permute-start(bf16[2,2,128,128]{3,2,1,0:T(8,128)(2,1)S(1)} %add_convert_fusion.9), channel_id=1, source_target_pairs={{0,192},{64,128},{128,64},{192,0},{1,193},{65,129},{129,65},{193,1... | collective-permute-start | bytes 393224 | tf_op jit(solution)/shard_map/ppermute | solution.py:34
  86.4 8.2 %collective-permute-start.22 = (bf16[2,2,128,128]{3,2,1,0:T(8,128)(2,1)S(1)}, bf16[2,2,128,128]{3,2,1,0:T(8,128)(2,1)S(1)}, u32[]{:S(2)}, u32[]{:S(2)}) collective-permute-start(bf16[2,2,128,128]{3,2,1,0:T(8,128)(2,1)S(1)} %add_convert_fusion.9), channel_id=1, source_target_pairs={{0,128},{64,192},{128,0},{192,64},{1,129},{65,193},{129,1},{193,65... | collective-permute-start | bytes 393224 | tf_op jit(solution)/shard_map/ppermute | solution.py:34
  98.7 8.1 %collective-permute-start.33 = (bf16[2,128,768]{2,1,0:T(8,128)(2,1)S(1)}, bf16[2,128,768]{2,1,0:T(8,128)(2,1)S(1)}, u32[]{:S(2)}, u32[]{:S(2)}) collective-permute-start(bf16[2,128,768]{2,1,0:T(8,128)(2,1)S(1)} %get-tuple-element.46), channel_id=1, source_target_pairs={{0,192},{8,56},{16,208},{24,8},{32,224},{40,24},{48,240},{56,40},{... | collective-permute-start | bytes 1179656 | tf_op jit(solution)/shard_map/ppermute | solution.py:30
  100.4 9.2 %collective-permute-start.31 = (bf16[2,128,768]{2,1,0:T(8,128)(2,1)S(1)}, bf16[2,128,768]{2,1,0:T(8,128)(2,1)S(1)}, u32[]{:S(2)}, u32[]{:S(2)}) collective-permute-start(bf16[2,128,768]{2,1,0:T(8,128)(2,1)S(1)} %get-tuple-element.44), channel_id=1, source_target_pairs={{0,64},{8,24},{16,80},{24,40},{32,96},{40,56},{48,112},{56,8},{64,... | collective-permute-start | bytes 1179656 | tf_op jit(solution)/shard_map/ppermute | solution.py:30
  107.0 12.2 %collective-permute-start.34 = (bf16[4,128,768]{2,1,0:T(8,128)(2,1)S(1)}, bf16[4,128,768]{2,1,0:T(8,128)(2,1)S(1)}, u32[]{:S(2)}, u32[]{:S(2)}) collective-permute-start(bf16[4,128,768]{2,1,0:T(8,128)(2,1)S(1)} %pad_maximum_fusion.1), channel_id=1, source_target_pairs={{0,192},{8,56},{16,208},{24,8},{32,224},{40,24},{48,240},{56,40},{... | collective-permute-start | bytes 2359304 | tf_op jit(solution)/shard_map/ppermute | solution.py:30
  109.9 13.3 %collective-permute-start.32 = (bf16[4,128,768]{2,1,0:T(8,128)(2,1)S(1)}, bf16[4,128,768]{2,1,0:T(8,128)(2,1)S(1)}, u32[]{:S(2)}, u32[]{:S(2)}) collective-permute-start(bf16[4,128,768]{2,1,0:T(8,128)(2,1)S(1)} %pad_maximum_fusion), channel_id=1, source_target_pairs={{0,64},{8,24},{16,80},{24,40},{32,96},{40,56},{48,112},{56,8},{64,... | collective-permute-start | bytes 2359304 | tf_op jit(solution)/shard_map/ppermute | solution.py:30
  110.0 8.9 %collective-permute-start.35 = (bf16[2,256,256]{2,1,0:T(8,128)(2,1)S(1)}, bf16[2,256,256]{2,1,0:T(8,128)(2,1)S(1)}, u32[]{:S(2)}, u32[]{:S(2)}) collective-permute-start(bf16[2,256,256]{2,1,0:T(8,128)(2,1)S(1)} %pad_maximum_fusion.2), channel_id=1, source_target_pairs={{0,1},{1,0},{2,3},{3,2},{4,5},{5,4},{6,7},{7,6},{8,9},{9,8},{10,11... | collective-permute-start | bytes 786440 | tf_op jit(solution)/shard_map/ppermute | solution.py:34
  136.1 8.1 %collective-permute-start.40 = (bf16[2,32,768]{2,1,0:T(8,128)(2,1)S(1)}, bf16[2,32,768]{2,1,0:T(8,128)(2,1)S(1)}, u32[]{:S(2)}, u32[]{:S(2)}) collective-permute-start(bf16[2,32,768]{2,1,0:T(8,128)(2,1)S(1)} %pad_maximum_fusion.3), channel_id=1, source_target_pairs={{0,7},{1,2},{2,1},{3,4},{4,3},{5,6},{6,5},{7,0},{8,15},{9,10},{10,... | collective-permute-start | bytes 294920 | tf_op jit(solution)/shard_map/ppermute | solution.py:38
  144.2 8.4 %collective-permute-start.41 = (bf16[2,32,768]{2,1,0:T(8,128)(2,1)S(1)}, bf16[2,32,768]{2,1,0:T(8,128)(2,1)S(1)}, u32[]{:S(2)}, u32[]{:S(2)}) collective-permute-start(bf16[2,32,768]{2,1,0:T(8,128)(2,1)S(1)} %add_convert_fusion.11), channel_id=1, source_target_pairs={{0,3},{1,6},{2,5},{3,0},{4,7},{5,2},{6,1},{7,4},{8,11},{9,14},{10,... | collective-permute-start | bytes 294920 | tf_op jit(solution)/shard_map/ppermute | solution.py:42
  (38 other events, 352.8 us)
where the time goes:
time: 166 us; the launch traced here: 165 us
  waiting for transfers between devices  58.4 us (35%)
  starting transfers between devices  52 us (31%)
  Pallas kernels  31 us (19%)
  local copies, waits for them, and re-layouts  12.2 us (7%)
  other arithmetic  7.34 us (4%)
  between operations  3.7 us (2%)
    pallas_call x9, Pallas kernels, call(): pl.pallas_call(kernel, out_shape=[jax.ShapeDtypeStruct(*out) for out in o...  31 us
    ppermute x16, waiting for transfers between devices, ring(): return lax.ppermute(value, ('y', 'x', 'core'), pairs)  24.2 us
    ppermute x26, waiting for transfers between devices, swap(): return lax.ppermute(value, axis, [(i, i ^ mask) for i in range(size)])  21.5 us
    ppermute x16, starting transfers between devices, ring(): return lax.ppermute(value, ('y', 'x', 'core'), pairs)  21.3 us
    ppermute x26, starting transfers between devices, swap(): return lax.ppermute(value, axis, [(i, i ^ mask) for i in range(size)])  21.1 us
    ppermute x2, starting transfers between devices, same_set_neighbour(): lax.ppermute(value, 'dp', [(z, (z + 1 if z % 2 else z - 1) % 8) for z in...  7.62 us
    ppermute x1, waiting for transfers between devices, same_set_far(): lax.ppermute(value, 'dp', [(z, ((7 if SETS >> z & 1 else 3) - z) % 8) for...  6.37 us
    ppermute x2, waiting for transfers between devices, same_set_neighbour(): lax.ppermute(value, 'dp', [(z, (z + 1 if z % 2 else z - 1) % 8) for z in...  6.36 us
  transfers between devices with their start and end apart: 45, of which 21 were waited for; matrix products, arithmetic and copies ran while one was open for 9% of the time, Pallas kernels for 7%

commit v1 on v0

--- a/solution.py
+++ b/solution.py
@@ -341,15 +341,14 @@
     mine = [jnp.concatenate(near[:2], axis=0), jnp.concatenate(near[2:], axis=0)]
     behind_low, ahead_high = ring(mine[0], 1, 3), ring(mine[1], 1, 1)
     far = [ring(behind_low, 1, 3), ring(ahead_high, 1, 1)]
-    tok01 = behind(swap(inputs, "dp", 8, 1), behind_low, ahead_high, index=rows)
-    ahead_low = ring(behind(mine[0], tok01), 1, 1)
-    behind_high = ring(behind(mine[1], tok01), 1, 3)
+    ahead_low, behind_high = ring(mine[0], 1, 1), ring(mine[1], 1, 3)
     gathered = mine + [ahead_low, ahead_high, behind_low, behind_high] + far
 
     c_core = swap(c_core, "core", 2, 1)
-    c_z = swap(behind(c_z, tok01), "dp", 8, 1)
+    c_z = swap(c_z, "dp", 8, 1)
     c_near, c_across = c_z[:, :256], swap(c_z[:, 256:], "core", 2, 1)
     tok10 = swap(inputs, "core", 2, 1)
+    tok01 = behind(swap(inputs, "dp", 8, 1), c_across, *far, ahead_low, behind_high, index=idx)
     tok11 = swap(tok01, "core", 2, 1)
     toks = [inputs, tok01, tok10, tok11]
 
@@ -370,7 +369,7 @@
             ((2, 2) + tile, BF),
         ],
         scratch=[pltpu.VMEM((D, COLS), BF)],
-        grant=58,
+        grant=52,
         flops=2 * 1024 * D * COLS,
         nbytes=10 * MIB,
     )

time: 166 us -> 176 us (1.060)
  waiting for transfers between devices: 58.4 us -> 71.9 us
  other arithmetic: 7.34 us -> 2.83 us
    ppermute x26, waiting for transfers between devices: 21.5 us -> 36.6 us  [swap(): return lax.ppermute(value, axis, [(i, i ^ mask) for i in range(size)])]
    convert_element_type x4 -> x1, other arithmetic: 4.11 us -> 1.43 us  [behind(): return (value.astype(F32) + zero).astype(value.dtype)]
    unnamed x53 -> x47, local copies, waits for them, and re-layouts: 5.8 us -> 5.41 us
  transfers between devices with their start and end apart: 45 -> 45, of which waited for: 21 -> 22; matrix products, arithmetic and copies ran while one was open for 9% -> 6% of each run, Pallas kernels for 7% -> 7%
where the time goes in v1:
time: 176 us; the launch traced here: 175 us
  waiting for transfers between devices  71.9 us (41%)
  starting transfers between devices  52.9 us (30%)
  Pallas kernels  30.7 us (17%)
  local copies, waits for them, and re-layouts  11.8 us (7%)
  between operations  4.92 us (3%)
  other arithmetic  2.83 us (2%)
    ppermute x26, waiting for transfers between devices, swap(): return lax.ppermute(value, axis, [(i, i ^ mask) for i in range(size)])  36.6 us
    pallas_call x9, Pallas kernels, call(): pl.pallas_call(kernel, out_shape=[jax.ShapeDtypeStruct(*out) for out in o...  30.7 us
    ppermute x16, waiting for transfers between devices, ring(): return lax.ppermute(value, ('y', 'x', 'core'), pairs)  23.3 us
    ppermute x26, starting transfers between devices, swap(): return lax.ppermute(value, axis, [(i, i ^ mask) for i in range(size)])  22.1 us
    ppermute x16, starting transfers between devices, ring(): return lax.ppermute(value, ('y', 'x', 'core'), pairs)  20.1 us
    ppermute x2, starting transfers between devices, same_set_neighbour(): lax.ppermute(value, 'dp', [(z, (z + 1 if z % 2 else z - 1) % 8) for z in...  8.74 us
    ppermute x1, waiting for transfers between devices, same_set_far(): lax.ppermute(value, 'dp', [(z, ((7 if SETS >> z & 1 else 3) - z) % 8) for...  6.07 us
    ppermute x2, waiting for transfers between devices, same_set_neighbour(): lax.ppermute(value, 'dp', [(z, (z + 1 if z % 2 else z - 1) % 8) for z in...  6.04 us
  transfers between devices with their start and end apart: 45, of which 22 were waited for; matrix products, arithmetic and copies ran while one was open for 6% of the time, Pallas kernels for 7%

profile of v1, /device:TPU:6, one launch (start us, length us, event | category | flops | bytes accessed | tf_op | source)
XLA Modules:
  0.0 175.1 jit_solution(18246028581964882202)
XLA Ops:
  6.1 2.8 %collective-permute-start.7 = (bf16[128,768]{1,0:T(8,128)(2,1)S(1)}, bf16[128,768]{1,0:T(8,128)(2,1)S(1)}, u32[]{:S(2)}, u32[]{:S(2)}) collective-permute-start(bf16[128,768]{1,0:T(8,128)(2,1)S(1)} %get-tuple-element.59), channel_id=1, source_target_pairs={{0,32},{8,136},{16,48},{24,152},{32,0},{40,168},{48,16},{56,184},{... | collective-permute-start | bytes 589832 | tf_op jit(solution)/shard_map/ppermute | solution.py:30
  8.9 1.9 %shard_map.68 = (bf16[256,256]{1,0:T(8,128)(2,1)}, bf16[256,256]{1,0:T(8,128)(2,1)}, bf16[256,512]{1,0:T(8,128)(2,1)}) custom-call(s32[7]{0:T(128)} %stack.43.pos, bf16[256,1024]{1,0:T(8,128)(2,1)} %bitcast.26), custom_call_target="tpu_custom_call" | custom-call | bytes 1048576 | tf_op jit(solution)/shard_map/pallas_call | solution.py:65
  14.0 2.6 %collective-permute-start.5 = (bf16[256,768]{1,0:T(8,128)(2,1)}, bf16[256,768]{1,0:T(8,128)(2,1)}, u32[]{:S(2)}, u32[]{:S(2)}) collective-permute-start(bf16[256,768]{1,0:T(8,128)(2,1)} %constant_dynamic-update-slice_fusion.2.refs_0_), channel_id=1, source_target_pairs={{0,64},{8,24},{16,80},{24,40},{32,96},{40,56},{48,112},{56,8},{64,... | collective-permute-start | bytes 1179656 | tf_op jit(solution)/shard_map/ppermute | solution.py:30
  17.2 3.2 %collective-permute-done.8 = bf16[128,768]{1,0:T(8,128)(2,1)S(1)} collective-permute-done((bf16[128,768]{1,0:T(8,128)(2,1)S(1)}, bf16[128,768]{1,0:T(8,128)(2,1)S(1)}, u32[]{:S(2)}, u32[]{:S(2)}) %collective-permute-start.8) | collective-permute-done | bytes 196640 | tf_op jit(solution)/shard_map/ppermute | solution.py:30
  23.3 18.6 %collective-permute-done.13 = s32[1,12]{1,0:T(1,128)S(1)} collective-permute-done((s32[1,12]{1,0:T(1,128)S(1)}, s32[1,12]{1,0:T(1,128)S(1)}, u32[]{:S(2)}, u32[]{:S(2)}) %collective-permute-start.13) | collective-permute-done | bytes 80 | tf_op jit(solution)/shard_map/ppermute | solution.py:34
  45.7 2.8 %collective-permute-start.10 = (bf16[256,768]{1,0:T(8,128)(2,1)}, bf16[256,768]{1,0:T(8,128)(2,1)S(1)}, u32[]{:S(2)}, u32[]{:S(2)}) collective-permute-start(bf16[256,768]{1,0:T(8,128)(2,1)} %collective-permute-done.9.refs_3_), channel_id=1, source_target_pairs={{0,192},{8,56},{16,208},{24,8},{32,224},{40,24},{48,240},{56,40},{... | collective-permute-start | bytes 1179656 | tf_op jit(solution)/shard_map/ppermute | solution.py:30
  54.0 3.6 %collective-permute-done.6.refs_6_ = bf16[256,768]{1,0:T(8,128)(2,1)S(1)} collective-permute-done((bf16[256,768]{1,0:T(8,128)(2,1)}, bf16[256,768]{1,0:T(8,128)(2,1)S(1)}, u32[]{:S(2)}, u32[]{:S(2)}) %collective-permute-start.6) | collective-permute-done | bytes 393248 | tf_op jit(solution)/shard_map/ppermute | solution.py:30
  68.8 9.8 %shard_map.70 = (bf16[4,256,768]{2,1,0:T(8,128)(2,1)}, bf16[4,256,256]{2,1,0:T(8,128)(2,1)}, bf16[4,2,128,128]{3,2,1,0:T(8,128)(2,1)S(1)}, bf16[2,2,128,128]{3,2...) custom-call(s32[7]{0:T(128)S(1)} %copy-done.10, ...), custom_call_target="tpu_custom_call" | custom-call | flops 3221225472 | bytes 10485760 | tf_op jit(solution)/shard_map/pallas_call | solution.py:65
  79.5 3.3 %collective-permute-start.25 = (bf16[2,2,128,128]{3,2,1,0:T(8,128)(2,1)S(1)}, bf16[2,2,128,128]{3,2,1,0:T(8,128)(2,1)S(1)}, u32[]{:S(2)}, u32[]{:S(2)}) collective-permute-start(bf16[2,2,128,128]{3,2,1,0:T(8,128)(2,1)S(1)} %get-tuple-element.38), channel_id=1, source_target_pairs={{0,128},{64,192},{128,0},{192,64},{1,129},{65,193},{129,1},{193,65... | collective-permute-start | bytes 393224 | tf_op jit(solution)/shard_map/ppermute | solution.py:34
  82.8 2.0 %collective-permute-start.20 = (bf16[2,2,128,128]{3,2,1,0:T(8,128)(2,1)S(1)}, bf16[2,2,128,128]{3,2,1,0:T(8,128)(2,1)S(1)}, u32[]{:S(2)}, u32[]{:S(2)}) collective-permute-start(bf16[2,2,128,128]{3,2,1,0:T(8,128)(2,1)S(1)} %get-tuple-element.36), channel_id=1, source_target_pairs={{0,48},{16,32},{32,16},{48,0},{1,49},{17,33},{33,17},{49,1},{2,50}... | collective-permute-start | bytes 393224 | tf_op jit(solution)/shard_map/ppermute | solution.py:34
  88.5 2.1 %collective-permute-start.29 = (bf16[2,2,128,128]{3,2,1,0:T(8,128)(2,1)S(1)}, bf16[2,2,128,128]{3,2,1,0:T(8,128)(2,1)S(1)}, u32[]{:S(2)}, u32[]{:S(2)}) collective-permute-start(bf16[2,2,128,128]{3,2,1,0:T(8,128)(2,1)S(1)} %get-tuple-element.52), channel_id=1, source_target_pairs={{0,48},{16,32},{32,16},{48,0},{1,49},{17,33},{33,17},{49,1},{2,50}... | collective-permute-start | bytes 393224 | tf_op jit(solution)/shard_map/ppermute | solution.py:34
  95.3 2.7 %collective-permute-done.27.refs_16_ = bf16[2,2,128,128]{3,2,1,0:T(8,128)(2,1)S(1)} collective-permute-done((bf16[2,2,128,128]{3,2,1,0:T(8,128)(2,1)S(1)}, bf16[2,2,128,128]{3,2,1,0:T(8,128)(2,1)S(1)}, u32[]{:S(2)}, u32[]{:S(2)}) %collective-permute-start.27) | collective-permute-done | bytes 131104 | tf_op jit(solution)/shard_map/ppermute | solution.py:34
  99.2 4.4 %shard_map.71.refs_6_ = f32[4,256,1024]{2,1,0:T(8,128)S(1)} custom-call(s32[7]{0:T(128)S(1)} %copy-done.10, s32[4,12]{1,0:T(4,128)S(1)} %pad_add_fusion.idx, f32[16,8]{1,0:T(8,128)S(1)} %copy.9.table, bf16[4,256,768]{2,1,0:T(8,128)(2,1)S(1)} %copy-done.6, bf16[4,256,256]{2,1,0:T(8,128)(2,1)S(1)} %copy-done.7), custom_call_target="tpu_custom_call" | custom-call | flops 805306368 | bytes 8388608 | tf_op jit(solution)/shard_map/pallas_call | solution.py:65
  103.8 3.9 %shard_map.72 = (bf16[4,256,256]{2,1,0:T(8,128)(2,1)S(1)}, bf16[4,256,768]{2,1,0:T(8,128)(2,1)S(1)}, bf16[2,128,768]{2,1,0:T(8,128)(2,1)S(1)}, bf16[2,128,768]{2,1,0:T(8,128)(2,1)S(1)}) custom-call(s32[7]{0:T(128)S(1)} %copy-done.10, s32[4,12]{1,0:T(4,128)S(1)} %pad_add_fusion.idx, f32[16,8]{1,0:T(8,128)S(1)} %copy.9.table, bf16[256,2048]{1,0:T(8,128)(2,1)S(1)} %bitcast.19, ...), custom_call_target="tpu_custom_call" | custom-call | flops 1610612736 | bytes 12582912 | tf_op jit(solution)/shard_map/pallas_call | solution.py:65
  110.0 3.3 %shard_map.74 = (bf16[4,128,768]{2,1,0:T(8,128)(2,1)S(1)}, bf16[4,128,768]{2,1,0:T(8,128)(2,1)S(1)}) custom-call(s32[7]{0:T(128)S(1)} %copy-done.10, bf16[256,2048]{1,0:T(8,128)(2,1)S(1)} %bitcast.20, bf16[256,2048]{1,0:T(8,128)(2,1)S(1)} %copy-done.1, bf16[256,2048]{1,0:T(8,128)(2,1)S(1)} %copy-done.5, ...), custom_call_target="tpu_custom_call" | custom-call | flops 1610612736 | bytes 9437184 | tf_op jit(solution)/shard_map/pallas_call | solution.py:65
  113.4 2.2 %collective-permute-done.33 = bf16[2,128,768]{2,1,0:T(8,128)(2,1)S(1)} collective-permute-done((bf16[2,128,768]{2,1,0:T(8,128)(2,1)S(1)}, bf16[2,128,768]{2,1,0:T(8,128)(2,1)S(1)}, u32[]{:S(2)}, u32[]{:S(2)}) %collective-permute-start.33) | collective-permute-done | bytes 393248 | tf_op jit(solution)/shard_map/ppermute | solution.py:30
  115.8 2.4 %collective-permute-start.34 = (bf16[4,128,768]{2,1,0:T(8,128)(2,1)S(1)}, bf16[4,128,768]{2,1,0:T(8,128)(2,1)S(1)}, u32[]{:S(2)}, u32[]{:S(2)}) collective-permute-start(bf16[4,128,768]{2,1,0:T(8,128)(2,1)S(1)} %pad_maximum_fusion.1), channel_id=1, source_target_pairs={{0,192},{8,56},{16,208},{24,8},{32,224},{40,24},{48,240},{56,40},{... | collective-permute-start | bytes 2359304 | tf_op jit(solution)/shard_map/ppermute | solution.py:30
  120.3 2.5 %shard_map.73.own = bf16[4,128,768]{2,1,0:T(8,128)(2,1)S(1)} custom-call(s32[7]{0:T(128)S(1)} %copy-done.10, bf16[256,2048]{1,0:T(8,128)(2,1)S(1)} %bitcast.21, bf16[256,2048]{1,0:T(8,128)(2,1)S(1)} %copy-done.1, bf16[256,2048]{1,0:T(8,128)(2,1)S(1)} %copy-done.5, bf16[256,2048]{1,0:T(8,128)(2,1)} %collective-permute-done.16.t3.refs_3_, ...), custom_call_target="tpu_custom_call" | custom-call | flops 402653184 | bytes 9437184 | tf_op jit(solution)/shard_map/pallas_call | solution.py:65
  122.8 4.8 %collective-permute-done.35.from_z = bf16[2,256,256]{2,1,0:T(8,128)(2,1)S(1)} collective-permute-done((bf16[2,256,256]{2,1,0:T(8,128)(2,1)S(1)}, bf16[2,256,256]{2,1,0:T(8,128)(2,1)S(1)}, u32[]{:S(2)}, u32[]{:S(2)}) %collective-permute-start.35) | collective-permute-done | bytes 262176 | tf_op jit(solution)/shard_map/ppermute | solution.py:34
  127.9 3.8 %collective-permute-done.32.r1 = bf16[4,128,768]{2,1,0:T(8,128)(2,1)S(1)} collective-permute-done((bf16[4,128,768]{2,1,0:T(8,128)(2,1)S(1)}, bf16[4,128,768]{2,1,0:T(8,128)(2,1)S(1)}, u32[]{:S(2)}, u32[]{:S(2)}) %collective-permute-start.32) | collective-permute-done | bytes 786464 | tf_op jit(solution)/shard_map/ppermute | solution.py:30
  133.3 2.0 %collective-permute-start.36 = (bf16[128,768]{1,0:T(8,128)(2,1)S(1)}, bf16[128,768]{1,0:T(8,128)(2,1)S(1)}, u32[]{:S(2)}, u32[]{:S(2)}) collective-permute-start(bf16[128,768]{1,0:T(8,128)(2,1)S(1)} %get-tuple-element.49), channel_id=1, source_target_pairs={{0,16},{8,72},{16,32},{24,88},{32,48},{40,104},{48,0},{56,120},{64... | collective-permute-start | bytes 589832 | tf_op jit(solution)/shard_map/ppermute | solution.py:30
  136.4 4.2 %collective-permute-done.36 = bf16[128,768]{1,0:T(8,128)(2,1)S(1)} collective-permute-done((bf16[128,768]{1,0:T(8,128)(2,1)S(1)}, bf16[128,768]{1,0:T(8,128)(2,1)S(1)}, u32[]{:S(2)}, u32[]{:S(2)}) %collective-permute-start.36) | collective-permute-done | bytes 196640 | tf_op jit(solution)/shard_map/ppermute | solution.py:30
  140.6 1.9 %collective-permute-done.37 = bf16[128,768]{1,0:T(8,128)(2,1)S(1)} collective-permute-done((bf16[128,768]{1,0:T(8,128)(2,1)S(1)}, bf16[128,768]{1,0:T(8,128)(2,1)S(1)}, u32[]{:S(2)}, u32[]{:S(2)}) %collective-permute-start.37) | collective-permute-done | bytes 196640 | tf_op jit(solution)/shard_map/ppermute | solution.py:30
  142.6 2.0 %collective-permute-done.38 = bf16[128,768]{1,0:T(8,128)(2,1)S(1)} collective-permute-done((bf16[128,768]{1,0:T(8,128)(2,1)S(1)}, bf16[128,768]{1,0:T(8,128)(2,1)S(1)}, u32[]{:S(2)}, u32[]{:S(2)}) %collective-permute-start.38) | collective-permute-done | bytes 196640 | tf_op jit(solution)/shard_map/ppermute | solution.py:30
  146.1 5.8 %collective-permute-start.40 = (bf16[2,32,768]{2,1,0:T(8,128)(2,1)S(1)}, bf16[2,32,768]{2,1,0:T(8,128)(2,1)S(1)}, u32[]{:S(2)}, u32[]{:S(2)}) collective-permute-start(bf16[2,32,768]{2,1,0:T(8,128)(2,1)S(1)} %pad_maximum_fusion.3), channel_id=1, source_target_pairs={{0,7},{1,2},{2,1},{3,4},{4,3},{5,6},{6,5},{7,0},{8,15},{9,10},{10,... | collective-permute-start | bytes 294920 | tf_op jit(solution)/shard_map/ppermute | solution.py:38
  151.9 3.1 %collective-permute-done.40 = bf16[2,32,768]{2,1,0:T(8,128)(2,1)S(1)} collective-permute-done((bf16[2,32,768]{2,1,0:T(8,128)(2,1)S(1)}, bf16[2,32,768]{2,1,0:T(8,128)(2,1)S(1)}, u32[]{:S(2)}, u32[]{:S(2)}) %collective-permute-start.40) | collective-permute-done | bytes 98336 | tf_op jit(solution)/shard_map/ppermute | solution.py:38
  155.0 2.0 %collective-permute-start.41 = (bf16[2,32,768]{2,1,0:T(8,128)(2,1)S(1)}, bf16[2,32,768]{2,1,0:T(8,128)(2,1)S(1)}, u32[]{:S(2)}, u32[]{:S(2)}) collective-permute-start(bf16[2,32,768]{2,1,0:T(8,128)(2,1)S(1)} %add_convert_fusion.8), channel_id=1, source_target_pairs={{0,3},{1,6},{2,5},{3,0},{4,7},{5,2},{6,1},{7,4},{8,11},{9,14},{10,... | collective-permute-start | bytes 294920 | tf_op jit(solution)/shard_map/ppermute | solution.py:42
  157.0 6.1 %collective-permute-done.41 = bf16[2,32,768]{2,1,0:T(8,128)(2,1)S(1)} collective-permute-done((bf16[2,32,768]{2,1,0:T(8,128)(2,1)S(1)}, bf16[2,32,768]{2,1,0:T(8,128)(2,1)S(1)}, u32[]{:S(2)}, u32[]{:S(2)}) %collective-permute-start.41) | collective-permute-done | bytes 98336 | tf_op jit(solution)/shard_map/ppermute | solution.py:42
  163.1 2.9 %collective-permute-start.42 = (bf16[2,32,768]{2,1,0:T(8,128)(2,1)S(1)}, bf16[2,32,768]{2,1,0:T(8,128)(2,1)S(1)}, u32[]{:S(2)}, u32[]{:S(2)}) collective-permute-start(bf16[2,32,768]{2,1,0:T(8,128)(2,1)S(1)} %add_convert_fusion.7.mine), channel_id=1, source_target_pairs={{0,7},{1,2},{2,1},{3,4},{4,3},{5,6},{6,5},{7,0},{8,15},{9,10},{10,... | collective-permute-start | bytes 294920 | tf_op jit(solution)/shard_map/ppermute | solution.py:38
  166.0 3.0 %collective-permute-done.42.near = bf16[2,32,768]{2,1,0:T(8,128)(2,1)S(1)} collective-permute-done((bf16[2,32,768]{2,1,0:T(8,128)(2,1)S(1)}, bf16[2,32,768]{2,1,0:T(8,128)(2,1)S(1)}, u32[]{:S(2)}, u32[]{:S(2)}) %collective-permute-start.42) | collective-permute-done | bytes 98336 | tf_op jit(solution)/shard_map/ppermute | solution.py:38
  169.0 2.3 %collective-permute-done.43.theirs = bf16[2,32,768]{2,1,0:T(8,128)(2,1)S(1)} collective-permute-done((bf16[2,32,768]{2,1,0:T(8,128)(2,1)S(1)}, bf16[2,32,768]{2,1,0:T(8,128)(2,1)S(1)}, u32[]{:S(2)}, u32[]{:S(2)}) %collective-permute-start.43) | collective-permute-done | bytes 98336 | tf_op jit(solution)/shard_map/ppermute | solution.py:34
  171.4 2.3 %collective-permute-done.44.beyond = bf16[2,32,768]{2,1,0:T(8,128)(2,1)S(1)} collective-permute-done((bf16[2,32,768]{2,1,0:T(8,128)(2,1)S(1)}, bf16[2,32,768]{2,1,0:T(8,128)(2,1)S(1)}, u32[]{:S(2)}, u32[]{:S(2)}) %collective-permute-start.44) | collective-permute-done | bytes 98336 | tf_op jit(solution)/shard_map/ppermute | solution.py:34
  (146 shorter events, 49.9 us)
Async XLA Ops:
  5.3 8.0 %collective-permute-start.4 = (bf16[128,768]{1,0:T(8,128)(2,1)S(1)}, bf16[128,768]{1,0:T(8,128)(2,1)S(1)}, u32[]{:S(2)}, u32[]{:S(2)}) collective-permute-start(bf16[128,768]{1,0:T(8,128)(2,1)S(1)} %get-tuple-element.59), channel_id=1, source_target_pairs={{0,48},{8,200},{16,0},{24,216},{32,16},{40,232},{48,32},{56,248},{... | collective-permute-start | bytes 589832 | tf_op jit(solution)/shard_map/ppermute | solution.py:30
  6.1 10.5 %collective-permute-start.7 = (bf16[128,768]{1,0:T(8,128)(2,1)S(1)}, bf16[128,768]{1,0:T(8,128)(2,1)S(1)}, u32[]{:S(2)}, u32[]{:S(2)}) collective-permute-start(bf16[128,768]{1,0:T(8,128)(2,1)S(1)} %get-tuple-element.59), channel_id=1, source_target_pairs={{0,32},{8,136},{16,48},{24,152},{32,0},{40,168},{48,16},{56,184},{... | collective-permute-start | bytes 589832 | tf_op jit(solution)/shard_map/ppermute | solution.py:30
  10.9 10.5 %collective-permute-start.1 = (bf16[256,512]{1,0:T(8,128)(2,1)}, bf16[256,512]{1,0:T(8,128)(2,1)S(1)}, u32[]{:S(2)}, u32[]{:S(2)}) collective-permute-start(bf16[256,512]{1,0:T(8,128)(2,1)} %get-tuple-element.27), channel_id=1, source_target_pairs={{0,1},{1,0},{2,3},{3,2},{4,5},{5,4},{6,7},{7,6},{8,9},{9,8},{10,11... | collective-permute-start | bytes 786440 | tf_op jit(solution)/shard_map/ppermute | solution.py:34
  11.0 51.0 %collective-permute-start = (bf16[256,2048]{1,0:T(8,128)(2,1)}, bf16[256,2048]{1,0:T(8,128)(2,1)S(1)}, u32[]{:S(2)}, u32[]{:S(2)}) collective-permute-start(bf16[256,2048]{1,0:T(8,128)(2,1)} %bitcast.16), channel_id=1, source_target_pairs={{0,1},{1,0},{2,3},{3,2},{4,5},{5,4},{6,7},{7,6},{8,9},{9,8},{10,11... | collective-permute-start | bytes 3145736 | tf_op jit(solution)/shard_map/ppermute | solution.py:34
  12.9 7.5 %collective-permute-start.8 = (bf16[128,768]{1,0:T(8,128)(2,1)S(1)}, bf16[128,768]{1,0:T(8,128)(2,1)S(1)}, u32[]{:S(2)}, u32[]{:S(2)}) collective-permute-start(bf16[128,768]{1,0:T(8,128)(2,1)S(1)} %get-tuple-element.59), channel_id=1, source_target_pairs={{0,16},{8,72},{16,32},{24,88},{32,48},{40,104},{48,0},{56,120},{64... | collective-permute-start | bytes 589832 | tf_op jit(solution)/shard_map/ppermute | solution.py:30
  14.0 31.2 %collective-permute-start.5 = (bf16[256,768]{1,0:T(8,128)(2,1)}, bf16[256,768]{1,0:T(8,128)(2,1)}, u32[]{:S(2)}, u32[]{:S(2)}) collective-permute-start(bf16[256,768]{1,0:T(8,128)(2,1)} %constant_dynamic-update-slice_fusion.2.refs_0_), channel_id=1, source_target_pairs={{0,64},{8,24},{16,80},{24,40},{32,96},{40,56},{48,112},{56,8},{64,... | collective-permute-start | bytes 1179656 | tf_op jit(solution)/shard_map/ppermute | solution.py:30
  21.1 24.6 %collective-permute-start.9 = (bf16[256,768]{1,0:T(8,128)(2,1)}, bf16[256,768]{1,0:T(8,128)(2,1)}, u32[]{:S(2)}, u32[]{:S(2)}) collective-permute-start(bf16[256,768]{1,0:T(8,128)(2,1)} %constant_dynamic-update-slice_fusion.5.refs_1_), channel_id=1, source_target_pairs={{0,192},{8,56},{16,208},{24,8},{32,224},{40,24},{48,240},{56,40},{... | collective-permute-start | bytes 1179656 | tf_op jit(solution)/shard_map/ppermute | solution.py:30
  21.4 22.8 %collective-permute-start.2 = (bf16[256,256]{1,0:T(8,128)(2,1)S(1)}, bf16[256,256]{1,0:T(8,128)(2,1)S(1)}, u32[]{:S(2)}, u32[]{:S(2)}) collective-permute-start(bf16[256,256]{1,0:T(8,128)(2,1)S(1)} %get-tuple-element.56), channel_id=1, source_target_pairs={{0,8},{8,0},{1,9},{9,1},{2,10},{10,2},{3,11},{11,3},{4,12},{12,4},... | collective-permute-start | bytes 393224 | tf_op jit(solution)/shard_map/ppermute | solution.py:34
  21.6 20.3 %collective-permute-start.13 = (s32[1,12]{1,0:T(1,128)S(1)}, s32[1,12]{1,0:T(1,128)S(1)}, u32[]{:S(2)}, u32[]{:S(2)}) collective-permute-start(s32[1,12]{1,0:T(1,128)S(1)} %reshape.20), channel_id=1, source_target_pairs={{0,1},{1,0},{2,3},{3,2},{4,5},{5,4},{6,7},{7,6},{8,9},{9,8},{10,11... | collective-permute-start | bytes 152 | tf_op jit(solution)/shard_map/ppermute | solution.py:34
  43.2 8.0 %collective-permute-start.11 = (bf16[256,768]{1,0:T(8,128)(2,1)}, bf16[256,768]{1,0:T(8,128)(2,1)S(1)}, u32[]{:S(2)}, u32[]{:S(2)}) collective-permute-start(bf16[256,768]{1,0:T(8,128)(2,1)} %constant_dynamic-update-slice_fusion.2.refs_0_), channel_id=1, source_target_pairs={{0,192},{8,56},{16,208},{24,8},{32,224},{40,24},{48,240},{56,40},{... | collective-permute-start | bytes 1179656 | tf_op jit(solution)/shard_map/ppermute | solution.py:30
  44.2 9.2 %collective-permute-start.12 = (bf16[256,768]{1,0:T(8,128)(2,1)}, bf16[256,768]{1,0:T(8,128)(2,1)S(1)}, u32[]{:S(2)}, u32[]{:S(2)}) collective-permute-start(bf16[256,768]{1,0:T(8,128)(2,1)} %constant_dynamic-update-slice_fusion.5.refs_1_), channel_id=1, source_target_pairs={{0,64},{8,24},{16,80},{24,40},{32,96},{40,56},{48,112},{56,8},{64,... | collective-permute-start | bytes 1179656 | tf_op jit(solution)/shard_map/ppermute | solution.py:30
  45.2 12.4 %collective-permute-start.6 = (bf16[256,768]{1,0:T(8,128)(2,1)}, bf16[256,768]{1,0:T(8,128)(2,1)S(1)}, u32[]{:S(2)}, u32[]{:S(2)}) collective-permute-start(bf16[256,768]{1,0:T(8,128)(2,1)} %collective-permute-done.5.refs_4_), channel_id=1, source_target_pairs={{0,64},{8,24},{16,80},{24,40},{32,96},{40,56},{48,112},{56,8},{64,... | collective-permute-start | bytes 1179656 | tf_op jit(solution)/shard_map/ppermute | solution.py:30
  45.7 13.9 %collective-permute-start.10 = (bf16[256,768]{1,0:T(8,128)(2,1)}, bf16[256,768]{1,0:T(8,128)(2,1)S(1)}, u32[]{:S(2)}, u32[]{:S(2)}) collective-permute-start(bf16[256,768]{1,0:T(8,128)(2,1)} %collective-permute-done.9.refs_3_), channel_id=1, source_target_pairs={{0,192},{8,56},{16,208},{24,8},{32,224},{40,24},{48,240},{56,40},{... | collective-permute-start | bytes 1179656 | tf_op jit(solution)/shard_map/ppermute | solution.py:30
  51.1 16.7 %collective-permute-start.15 = (bf16[256,2048]{1,0:T(8,128)(2,1)S(1)}, bf16[256,2048]{1,0:T(8,128)(2,1)S(1)}, u32[]{:S(2)}, u32[]{:S(2)}) collective-permute-start(bf16[256,2048]{1,0:T(8,128)(2,1)S(1)} %bitcast.18), channel_id=1, source_target_pairs={{0,8},{8,0},{1,9},{9,1},{2,10},{10,2},{3,11},{11,3},{4,12},{12,4},... | collective-permute-start | bytes 3145736 | tf_op jit(solution)/shard_map/ppermute | solution.py:34
  78.7 9.7 %collective-permute-start.26 = (bf16[2,2,128,128]{3,2,1,0:T(8,128)(2,1)S(1)}, bf16[2,2,128,128]{3,2,1,0:T(8,128)(2,1)S(1)}, u32[]{:S(2)}, u32[]{:S(2)}) collective-permute-start(bf16[2,2,128,128]{3,2,1,0:T(8,128)(2,1)S(1)} %get-tuple-element.38), channel_id=1, source_target_pairs={{0,192},{64,128},{128,64},{192,0},{1,193},{65,129},{129,65},{193,1... | collective-permute-start | bytes 393224 | tf_op jit(solution)/shard_map/ppermute | solution.py:34
  79.5 8.8 %collective-permute-start.25 = (bf16[2,2,128,128]{3,2,1,0:T(8,128)(2,1)S(1)}, bf16[2,2,128,128]{3,2,1,0:T(8,128)(2,1)S(1)}, u32[]{:S(2)}, u32[]{:S(2)}) collective-permute-start(bf16[2,2,128,128]{3,2,1,0:T(8,128)(2,1)S(1)} %get-tuple-element.38), channel_id=1, source_target_pairs={{0,128},{64,192},{128,0},{192,64},{1,129},{65,193},{129,1},{193,65... | collective-permute-start | bytes 393224 | tf_op jit(solution)/shard_map/ppermute | solution.py:34
  82.8 8.7 %collective-permute-start.20 = (bf16[2,2,128,128]{3,2,1,0:T(8,128)(2,1)S(1)}, bf16[2,2,128,128]{3,2,1,0:T(8,128)(2,1)S(1)}, u32[]{:S(2)}, u32[]{:S(2)}) collective-permute-start(bf16[2,2,128,128]{3,2,1,0:T(8,128)(2,1)S(1)} %get-tuple-element.36), channel_id=1, source_target_pairs={{0,48},{16,32},{32,16},{48,0},{1,49},{17,33},{33,17},{49,1},{2,50}... | collective-permute-start | bytes 393224 | tf_op jit(solution)/shard_map/ppermute | solution.py:34
  84.8 7.8 %collective-permute-start.19 = (bf16[2,2,128,128]{3,2,1,0:T(8,128)(2,1)S(1)}, bf16[2,2,128,128]{3,2,1,0:T(8,128)(2,1)S(1)}, u32[]{:S(2)}, u32[]{:S(2)}) collective-permute-start(bf16[2,2,128,128]{3,2,1,0:T(8,128)(2,1)S(1)} %get-tuple-element.36), channel_id=1, source_target_pairs={{0,32},{16,48},{32,0},{48,16},{1,33},{17,49},{33,1},{49,17},{2,34}... | collective-permute-start | bytes 393224 | tf_op jit(solution)/shard_map/ppermute | solution.py:34
  88.5 15.2 %collective-permute-start.29 = (bf16[2,2,128,128]{3,2,1,0:T(8,128)(2,1)S(1)}, bf16[2,2,128,128]{3,2,1,0:T(8,128)(2,1)S(1)}, u32[]{:S(2)}, u32[]{:S(2)}) collective-permute-start(bf16[2,2,128,128]{3,2,1,0:T(8,128)(2,1)S(1)} %get-tuple-element.52), channel_id=1, source_target_pairs={{0,48},{16,32},{32,16},{48,0},{1,49},{17,33},{33,17},{49,1},{2,50}... | collective-permute-start | bytes 393224 | tf_op jit(solution)/shard_map/ppermute | solution.py:34
  90.6 13.1 %collective-permute-start.28 = (bf16[2,2,128,128]{3,2,1,0:T(8,128)(2,1)S(1)}, bf16[2,2,128,128]{3,2,1,0:T(8,128)(2,1)S(1)}, u32[]{:S(2)}, u32[]{:S(2)}) collective-permute-start(bf16[2,2,128,128]{3,2,1,0:T(8,128)(2,1)S(1)} %get-tuple-element.52), channel_id=1, source_target_pairs={{0,32},{16,48},{32,0},{48,16},{1,33},{17,49},{33,1},{49,17},{2,34}... | collective-permute-start | bytes 393224 | tf_op jit(solution)/shard_map/ppermute | solution.py:34
  92.7 11.0 %collective-permute-start.23 = (bf16[2,2,128,128]{3,2,1,0:T(8,128)(2,1)S(1)}, bf16[2,2,128,128]{3,2,1,0:T(8,128)(2,1)S(1)}, u32[]{:S(2)}, u32[]{:S(2)}) collective-permute-start(bf16[2,2,128,128]{3,2,1,0:T(8,128)(2,1)S(1)} %add_convert_fusion.6), channel_id=1, source_target_pairs={{0,192},{64,128},{128,64},{192,0},{1,193},{65,129},{129,65},{193,1... | collective-permute-start | bytes 393224 | tf_op jit(solution)/shard_map/ppermute | solution.py:34
  94.2 9.5 %collective-permute-start.22 = (bf16[2,2,128,128]{3,2,1,0:T(8,128)(2,1)S(1)}, bf16[2,2,128,128]{3,2,1,0:T(8,128)(2,1)S(1)}, u32[]{:S(2)}, u32[]{:S(2)}) collective-permute-start(bf16[2,2,128,128]{3,2,1,0:T(8,128)(2,1)S(1)} %add_convert_fusion.6), channel_id=1, source_target_pairs={{0,128},{64,192},{128,0},{192,64},{1,129},{65,193},{129,1},{193,65... | collective-permute-start | bytes 393224 | tf_op jit(solution)/shard_map/ppermute | solution.py:34
  107.8 7.9 %collective-permute-start.33 = (bf16[2,128,768]{2,1,0:T(8,128)(2,1)S(1)}, bf16[2,128,768]{2,1,0:T(8,128)(2,1)S(1)}, u32[]{:S(2)}, u32[]{:S(2)}) collective-permute-start(bf16[2,128,768]{2,1,0:T(8,128)(2,1)S(1)} %get-tuple-element.46), channel_id=1, source_target_pairs={{0,192},{8,56},{16,208},{24,8},{32,224},{40,24},{48,240},{56,40},{... | collective-permute-start | bytes 1179656 | tf_op jit(solution)/shard_map/ppermute | solution.py:30
  109.0 9.2 %collective-permute-start.31 = (bf16[2,128,768]{2,1,0:T(8,128)(2,1)S(1)}, bf16[2,128,768]{2,1,0:T(8,128)(2,1)S(1)}, u32[]{:S(2)}, u32[]{:S(2)}) collective-permute-start(bf16[2,128,768]{2,1,0:T(8,128)(2,1)S(1)} %get-tuple-element.44), channel_id=1, source_target_pairs={{0,64},{8,24},{16,80},{24,40},{32,96},{40,56},{48,112},{56,8},{64,... | collective-permute-start | bytes 1179656 | tf_op jit(solution)/shard_map/ppermute | solution.py:30
  115.8 12.1 %collective-permute-start.34 = (bf16[4,128,768]{2,1,0:T(8,128)(2,1)S(1)}, bf16[4,128,768]{2,1,0:T(8,128)(2,1)S(1)}, u32[]{:S(2)}, u32[]{:S(2)}) collective-permute-start(bf16[4,128,768]{2,1,0:T(8,128)(2,1)S(1)} %pad_maximum_fusion.1), channel_id=1, source_target_pairs={{0,192},{8,56},{16,208},{24,8},{32,224},{40,24},{48,240},{56,40},{... | collective-permute-start | bytes 2359304 | tf_op jit(solution)/shard_map/ppermute | solution.py:30
  118.4 13.3 %collective-permute-start.32 = (bf16[4,128,768]{2,1,0:T(8,128)(2,1)S(1)}, bf16[4,128,768]{2,1,0:T(8,128)(2,1)S(1)}, u32[]{:S(2)}, u32[]{:S(2)}) collective-permute-start(bf16[4,128,768]{2,1,0:T(8,128)(2,1)S(1)} %pad_maximum_fusion), channel_id=1, source_target_pairs={{0,64},{8,24},{16,80},{24,40},{32,96},{40,56},{48,112},{56,8},{64,... | collective-permute-start | bytes 2359304 | tf_op jit(solution)/shard_map/ppermute | solution.py:30
  118.5 9.1 %collective-permute-start.35 = (bf16[2,256,256]{2,1,0:T(8,128)(2,1)S(1)}, bf16[2,256,256]{2,1,0:T(8,128)(2,1)S(1)}, u32[]{:S(2)}, u32[]{:S(2)}) collective-permute-start(bf16[2,256,256]{2,1,0:T(8,128)(2,1)S(1)} %pad_maximum_fusion.2), channel_id=1, source_target_pairs={{0,1},{1,0},{2,3},{3,2},{4,5},{5,4},{6,7},{7,6},{8,9},{9,8},{10,11... | collective-permute-start | bytes 786440 | tf_op jit(solution)/shard_map/ppermute | solution.py:34
  133.3 7.3 %collective-permute-start.36 = (bf16[128,768]{1,0:T(8,128)(2,1)S(1)}, bf16[128,768]{1,0:T(8,128)(2,1)S(1)}, u32[]{:S(2)}, u32[]{:S(2)}) collective-permute-start(bf16[128,768]{1,0:T(8,128)(2,1)S(1)} %get-tuple-element.49), channel_id=1, source_target_pairs={{0,16},{8,72},{16,32},{24,88},{32,48},{40,104},{48,0},{56,120},{64... | collective-permute-start | bytes 589832 | tf_op jit(solution)/shard_map/ppermute | solution.py:30
  135.3 7.3 %collective-permute-start.37 = (bf16[128,768]{1,0:T(8,128)(2,1)S(1)}, bf16[128,768]{1,0:T(8,128)(2,1)S(1)}, u32[]{:S(2)}, u32[]{:S(2)}) collective-permute-start(bf16[128,768]{1,0:T(8,128)(2,1)S(1)} %get-tuple-element.50), channel_id=1, source_target_pairs={{0,32},{8,136},{16,48},{24,152},{32,0},{40,168},{48,16},{56,184},{... | collective-permute-start | bytes 589832 | tf_op jit(solution)/shard_map/ppermute | solution.py:30
  136.2 8.4 %collective-permute-start.38 = (bf16[128,768]{1,0:T(8,128)(2,1)S(1)}, bf16[128,768]{1,0:T(8,128)(2,1)S(1)}, u32[]{:S(2)}, u32[]{:S(2)}) collective-permute-start(bf16[128,768]{1,0:T(8,128)(2,1)S(1)} %get-tuple-element.51), channel_id=1, source_target_pairs={{0,48},{8,200},{16,0},{24,216},{32,16},{40,232},{48,32},{56,248},{... | collective-permute-start | bytes 589832 | tf_op jit(solution)/shard_map/ppermute | solution.py:30
  146.1 8.9 %collective-permute-start.40 = (bf16[2,32,768]{2,1,0:T(8,128)(2,1)S(1)}, bf16[2,32,768]{2,1,0:T(8,128)(2,1)S(1)}, u32[]{:S(2)}, u32[]{:S(2)}) collective-permute-start(bf16[2,32,768]{2,1,0:T(8,128)(2,1)S(1)} %pad_maximum_fusion.3), channel_id=1, source_target_pairs={{0,7},{1,2},{2,1},{3,4},{4,3},{5,6},{6,5},{7,0},{8,15},{9,10},{10,... | collective-permute-start | bytes 294920 | tf_op jit(solution)/shard_map/ppermute | solution.py:38
  155.0 8.1 %collective-permute-start.41 = (bf16[2,32,768]{2,1,0:T(8,128)(2,1)S(1)}, bf16[2,32,768]{2,1,0:T(8,128)(2,1)S(1)}, u32[]{:S(2)}, u32[]{:S(2)}) collective-permute-start(bf16[2,32,768]{2,1,0:T(8,128)(2,1)S(1)} %add_convert_fusion.8), channel_id=1, source_target_pairs={{0,3},{1,6},{2,5},{3,0},{4,7},{5,2},{6,1},{7,4},{8,11},{9,14},{10,... | collective-permute-start | bytes 294920 | tf_op jit(solution)/shard_map/ppermute | solution.py:42
  (35 other events, 448.5 us)

commit v2 on v1

--- a/solution.py
+++ b/solution.py
@@ -43,7 +43,7 @@
 
 
 def behind(value, *others, index=None):
-    zero = sum(other[0, 0].astype(F32) for other in others) * 0.0
+    zero = sum([other[0, 0].astype(F32) for other in others], jnp.zeros((), F32)) * 0.0
     if index is not None:
         zero = zero + (index[-1, -1] < 0).astype(F32)
     return (value.astype(F32) + zero).astype(value.dtype)
@@ -347,10 +347,10 @@
     c_core = swap(c_core, "core", 2, 1)
     c_z = swap(c_z, "dp", 8, 1)
     c_near, c_across = c_z[:, :256], swap(c_z[:, 256:], "core", 2, 1)
-    tok10 = swap(inputs, "core", 2, 1)
-    tok01 = behind(swap(inputs, "dp", 8, 1), c_across, *far, ahead_low, behind_high, index=idx)
-    tok11 = swap(tok01, "core", 2, 1)
-    toks = [inputs, tok01, tok10, tok11]
+    own = behind(inputs, index=rows)
+    tok01 = behind(swap(own, "dp", 8, 1), c_across, *far, ahead_low, behind_high)
+    tok10, tok11 = swap(own, "core", 2, 1), swap(tok01, "core", 2, 1)
+    toks = [own, tok01, tok10, tok11]
 
     tile = (HEAD, HEAD)
     qkv, cots, s1, x0, g1, m2, m3, m4, m5 = call(

time: 176 us -> 155 us (0.88)
  waiting for transfers between devices: 71.9 us -> 53.8 us
  local copies, waits for them, and re-layouts: 11.8 us -> 7.94 us
  starting transfers between devices: 52.9 us -> 55.1 us
    ppermute x26, waiting for transfers between devices: 36.6 us -> 18.4 us  [swap(): return lax.ppermute(value, axis, [(i, i ^ mask) for i in range(size)])]
    ppermute x16, starting transfers between devices: 20.1 us -> 25.8 us  [ring(): return lax.ppermute(value, ('y', 'x', 'core'), pairs)]
    unnamed x47 -> x55, local copies, waits for them, and re-layouts: 5.41 us -> 3.07 us
    ppermute x26, starting transfers between devices: 22.1 us -> 20.1 us  [swap(): return lax.ppermute(value, axis, [(i, i ^ mask) for i in range(size)])]
  transfers between devices with their start and end apart: 45 -> 45, of which waited for: 22 -> 21; matrix products, arithmetic and copies ran while one was open for 6% -> 5% of each run, Pallas kernels for 7% -> 9%
where the time goes in v2:
time: 155 us
  starting transfers between devices  55.1 us (36%)
  waiting for transfers between devices  53.8 us (35%)
  Pallas kernels  30.7 us (20%)
  local copies, waits for them, and re-layouts  7.94 us (5%)
  between operations  4.91 us (3%)
  other arithmetic  2.37 us (2%)
    pallas_call x9, Pallas kernels, call(): pl.pallas_call(kernel, out_shape=[jax.ShapeDtypeStruct(*out) for out in o...  30.7 us
    ppermute x16, starting transfers between devices, ring(): return lax.ppermute(value, ('y', 'x', 'core'), pairs)  25.8 us
    ppermute x16, waiting for transfers between devices, ring(): return lax.ppermute(value, ('y', 'x', 'core'), pairs)  23.4 us
    ppermute x26, starting transfers between devices, swap(): return lax.ppermute(value, axis, [(i, i ^ mask) for i in range(size)])  20.1 us
    ppermute x26, waiting for transfers between devices, swap(): return lax.ppermute(value, axis, [(i, i ^ mask) for i in range(size)])  18.4 us
    ppermute x2, starting transfers between devices, same_set_neighbour(): lax.ppermute(value, 'dp', [(z, (z + 1 if z % 2 else z - 1) % 8) for z in...  7.2 us
    ppermute x1, waiting for transfers between devices, same_set_far(): lax.ppermute(value, 'dp', [(z, ((7 if SETS >> z & 1 else 3) - z) % 8) for...  5.99 us
    ppermute x2, waiting for transfers between devices, same_set_neighbour(): lax.ppermute(value, 'dp', [(z, (z + 1 if z % 2 else z - 1) % 8) for z in...  5.97 us
  transfers between devices with their start and end apart: 45, of which 21 were waited for; matrix products, arithmetic and copies ran while one was open for 5% of the time, Pallas kernels for 9%

profile of v2, /device:TPU:6, one launch (start us, length us, event | category | flops | bytes accessed | tf_op | source)
XLA Modules:
  0.0 154.8 jit_solution(6025534334983809872)
XLA Ops:
  1.5 1.9 %collective-permute-start = (s32[1,12]{1,0:T(1,128)S(1)}, s32[1,12]{1,0:T(1,128)S(1)}, u32[]{:S(2)}, u32[]{:S(2)}) collective-permute-start(s32[1,12]{1,0:T(1,128)S(1)} %reshape.24), channel_id=1, source_target_pairs={{0,1},{1,0},{2,3},{3,2},{4,5},{5,4},{6,7},{7,6},{8,9},{9,8},{10,11... | collective-permute-start | bytes 152 | tf_op jit(solution)/shard_map/ppermute | solution.py:34
  5.7 1.9 %shard_map.68 = (bf16[256,256]{1,0:T(8,128)(2,1)}, bf16[256,256]{1,0:T(8,128)(2,1)}, bf16[256,512]{1,0:T(8,128)(2,1)}) custom-call(s32[7]{0:T(128)} %stack.43.pos, bf16[256,1024]{1,0:T(8,128)(2,1)} %bitcast.22), custom_call_target="tpu_custom_call" | custom-call | bytes 1048576 | tf_op jit(solution)/shard_map/pallas_call | solution.py:65
  13.6 3.2 %collective-permute-start.9 = (bf16[128,768]{1,0:T(8,128)(2,1)S(1)}, bf16[128,768]{1,0:T(8,128)(2,1)S(1)}, u32[]{:S(2)}, u32[]{:S(2)}) collective-permute-start(bf16[128,768]{1,0:T(8,128)(2,1)S(1)} %get-tuple-element.59), channel_id=1, source_target_pairs={{0,16},{8,72},{16,32},{24,88},{32,48},{40,104},{48,0},{56,120},{64... | collective-permute-start | bytes 589832 | tf_op jit(solution)/shard_map/ppermute | solution.py:30
  16.8 2.3 %collective-permute-done.5 = bf16[128,768]{1,0:T(8,128)(2,1)S(1)} collective-permute-done((bf16[128,768]{1,0:T(8,128)(2,1)S(1)}, bf16[128,768]{1,0:T(8,128)(2,1)S(1)}, u32[]{:S(2)}, u32[]{:S(2)}) %collective-permute-start.5) | collective-permute-done | bytes 196640 | tf_op jit(solution)/shard_map/ppermute | solution.py:30
  20.9 3.0 %collective-permute-start.10 = (bf16[256,768]{1,0:T(8,128)(2,1)S(1)}, bf16[256,768]{1,0:T(8,128)(2,1)S(1)}, u32[]{:S(2)}, u32[]{:S(2)}) collective-permute-start(bf16[256,768]{1,0:T(8,128)(2,1)S(1)} %constant_dynamic-update-slice_fusion.5.refs_1_), channel_id=1, source_target_pairs={{0,192},{8,56},{16,208},{24,8},{32,224},{40,24},{48,240},{56,40},{... | collective-permute-start | bytes 1179656 | tf_op jit(solution)/shard_map/ppermute | solution.py:30
  26.1 2.1 %collective-permute-done.6.refs_4_ = bf16[256,768]{1,0:T(8,128)(2,1)S(1)} collective-permute-done((bf16[256,768]{1,0:T(8,128)(2,1)S(1)}, bf16[256,768]{1,0:T(8,128)(2,1)S(1)}, u32[]{:S(2)}, u32[]{:S(2)}) %collective-permute-start.6) | collective-permute-done | bytes 393248 | tf_op jit(solution)/shard_map/ppermute | solution.py:30
  29.2 3.7 %collective-permute-start.11 = (bf16[256,768]{1,0:T(8,128)(2,1)S(1)}, bf16[256,768]{1,0:T(8,128)(2,1)S(1)}, u32[]{:S(2)}, u32[]{:S(2)}) collective-permute-start(bf16[256,768]{1,0:T(8,128)(2,1)S(1)} %collective-permute-done.10.refs_3_), channel_id=1, source_target_pairs={{0,192},{8,56},{16,208},{24,8},{32,224},{40,24},{48,240},{56,40},{... | collective-permute-start | bytes 1179656 | tf_op jit(solution)/shard_map/ppermute | solution.py:30
  35.4 3.6 %collective-permute-done.7.refs_6_ = bf16[256,768]{1,0:T(8,128)(2,1)S(1)} collective-permute-done((bf16[256,768]{1,0:T(8,128)(2,1)S(1)}, bf16[256,768]{1,0:T(8,128)(2,1)S(1)}, u32[]{:S(2)}, u32[]{:S(2)}) %collective-permute-start.7) | collective-permute-done | bytes 393248 | tf_op jit(solution)/shard_map/ppermute | solution.py:30
  48.2 9.8 %shard_map.70 = (bf16[4,256,768]{2,1,0:T(8,128)(2,1)}, bf16[4,256,256]{2,1,0:T(8,128)(2,1)}, bf16[4,2,128,128]{3,2,1,0:T(8,128)(2,1)S(1)}, bf16[2,2,128,128]{3,2...) custom-call(s32[7]{0:T(128)S(1)} %copy-done.10, ...), custom_call_target="tpu_custom_call" | custom-call | flops 3221225472 | bytes 10485760 | tf_op jit(solution)/shard_map/pallas_call | solution.py:65
  59.2 3.0 %collective-permute-start.25 = (bf16[2,2,128,128]{3,2,1,0:T(8,128)(2,1)S(1)}, bf16[2,2,128,128]{3,2,1,0:T(8,128)(2,1)S(1)}, u32[]{:S(2)}, u32[]{:S(2)}) collective-permute-start(bf16[2,2,128,128]{3,2,1,0:T(8,128)(2,1)S(1)} %get-tuple-element.38), channel_id=1, source_target_pairs={{0,128},{64,192},{128,0},{192,64},{1,129},{65,193},{129,1},{193,65... | collective-permute-start | bytes 393224 | tf_op jit(solution)/shard_map/ppermute | solution.py:34
  62.1 3.7 %collective-permute-start.20 = (bf16[2,2,128,128]{3,2,1,0:T(8,128)(2,1)S(1)}, bf16[2,2,128,128]{3,2,1,0:T(8,128)(2,1)S(1)}, u32[]{:S(2)}, u32[]{:S(2)}) collective-permute-start(bf16[2,2,128,128]{3,2,1,0:T(8,128)(2,1)S(1)} %get-tuple-element.36), channel_id=1, source_target_pairs={{0,48},{16,32},{32,16},{48,0},{1,49},{17,33},{33,17},{49,1},{2,50}... | collective-permute-start | bytes 393224 | tf_op jit(solution)/shard_map/ppermute | solution.py:34
  68.0 3.8 %collective-permute-start.29 = (bf16[2,2,128,128]{3,2,1,0:T(8,128)(2,1)S(1)}, bf16[2,2,128,128]{3,2,1,0:T(8,128)(2,1)S(1)}, u32[]{:S(2)}, u32[]{:S(2)}) collective-permute-start(bf16[2,2,128,128]{3,2,1,0:T(8,128)(2,1)S(1)} %get-tuple-element.52), channel_id=1, source_target_pairs={{0,48},{16,32},{32,16},{48,0},{1,49},{17,33},{33,17},{49,1},{2,50}... | collective-permute-start | bytes 393224 | tf_op jit(solution)/shard_map/ppermute | solution.py:34
  76.0 2.4 %collective-permute-done.27.refs_16_ = bf16[2,2,128,128]{3,2,1,0:T(8,128)(2,1)S(1)} collective-permute-done((bf16[2,2,128,128]{3,2,1,0:T(8,128)(2,1)S(1)}, bf16[2,2,128,128]{3,2,1,0:T(8,128)(2,1)S(1)}, u32[]{:S(2)}, u32[]{:S(2)}) %collective-permute-start.27) | collective-permute-done | bytes 131104 | tf_op jit(solution)/shard_map/ppermute | solution.py:34
  79.6 4.4 %shard_map.71.refs_6_ = f32[4,256,1024]{2,1,0:T(8,128)S(1)} custom-call(s32[7]{0:T(128)S(1)} %copy-done.10, s32[4,12]{1,0:T(4,128)S(1)} %pad_add_fusion.idx, f32[16,8]{1,0:T(8,128)S(1)} %copy.9.table, bf16[4,256,768]{2,1,0:T(8,128)(2,1)S(1)} %copy-done.6, bf16[4,256,256]{2,1,0:T(8,128)(2,1)S(1)} %copy-done.7), custom_call_target="tpu_custom_call" | custom-call | flops 805306368 | bytes 8388608 | tf_op jit(solution)/shard_map/pallas_call | solution.py:65
  84.1 3.9 %shard_map.72 = (bf16[4,256,256]{2,1,0:T(8,128)(2,1)S(1)}, bf16[4,256,768]{2,1,0:T(8,128)(2,1)S(1)}, bf16[2,128,768]{2,1,0:T(8,128)(2,1)S(1)}, bf16[2,128,768]{2,1,0:T(8,128)(2,1)S(1)}) custom-call(s32[7]{0:T(128)S(1)} %copy-done.10, s32[4,12]{1,0:T(4,128)S(1)} %pad_add_fusion.idx, f32[16,8]{1,0:T(8,128)S(1)} %copy.9.table, bf16[256,2048]{1,0:T(8,128)(2,1)S(1)} %copy-done.1, ...), custom_call_target="tpu_custom_call" | custom-call | flops 1610612736 | bytes 12582912 | tf_op jit(solution)/shard_map/pallas_call | solution.py:65
  90.5 3.3 %shard_map.74 = (bf16[4,128,768]{2,1,0:T(8,128)(2,1)S(1)}, bf16[4,128,768]{2,1,0:T(8,128)(2,1)S(1)}) custom-call(s32[7]{0:T(128)S(1)} %copy-done.10, bf16[256,2048]{1,0:T(8,128)(2,1)S(1)} %copy-done.1, bf16[256,2048]{1,0:T(8,128)(2,1)S(1)} %copy-done.3, bf16[256,2048]{1,0:T(8,128)(2,1)S(1)} %copy-done.5, ...), custom_call_target="tpu_custom_call" | custom-call | flops 1610612736 | bytes 9437184 | tf_op jit(solution)/shard_map/pallas_call | solution.py:65
  93.9 2.1 %collective-permute-done.33 = bf16[2,128,768]{2,1,0:T(8,128)(2,1)S(1)} collective-permute-done((bf16[2,128,768]{2,1,0:T(8,128)(2,1)S(1)}, bf16[2,128,768]{2,1,0:T(8,128)(2,1)S(1)}, u32[]{:S(2)}, u32[]{:S(2)}) %collective-permute-start.33) | collective-permute-done | bytes 393248 | tf_op jit(solution)/shard_map/ppermute | solution.py:30
  96.2 2.5 %collective-permute-start.34 = (bf16[4,128,768]{2,1,0:T(8,128)(2,1)S(1)}, bf16[4,128,768]{2,1,0:T(8,128)(2,1)S(1)}, u32[]{:S(2)}, u32[]{:S(2)}) collective-permute-start(bf16[4,128,768]{2,1,0:T(8,128)(2,1)S(1)} %pad_maximum_fusion.1), channel_id=1, source_target_pairs={{0,192},{8,56},{16,208},{24,8},{32,224},{40,24},{48,240},{56,40},{... | collective-permute-start | bytes 2359304 | tf_op jit(solution)/shard_map/ppermute | solution.py:30
  99.2 2.5 %shard_map.73.own = bf16[4,128,768]{2,1,0:T(8,128)(2,1)S(1)} custom-call(s32[7]{0:T(128)S(1)} %copy-done.10, bf16[256,2048]{1,0:T(8,128)(2,1)S(1)} %copy-done.1, bf16[256,2048]{1,0:T(8,128)(2,1)S(1)} %copy-done.3, bf16[256,2048]{1,0:T(8,128)(2,1)S(1)} %copy-done.5, bf16[256,2048]{1,0:T(8,128)(2,1)} %collective-permute-done.15.t3.refs_3_, ...), custom_call_target="tpu_custom_call" | custom-call | flops 402653184 | bytes 9437184 | tf_op jit(solution)/shard_map/pallas_call | solution.py:65
  101.7 6.6 %collective-permute-done.35.from_z = bf16[2,256,256]{2,1,0:T(8,128)(2,1)S(1)} collective-permute-done((bf16[2,256,256]{2,1,0:T(8,128)(2,1)S(1)}, bf16[2,256,256]{2,1,0:T(8,128)(2,1)S(1)}, u32[]{:S(2)}, u32[]{:S(2)}) %collective-permute-start.35) | collective-permute-done | bytes 262176 | tf_op jit(solution)/shard_map/ppermute | solution.py:34
  108.3 3.9 %collective-permute-done.32.r1 = bf16[4,128,768]{2,1,0:T(8,128)(2,1)S(1)} collective-permute-done((bf16[4,128,768]{2,1,0:T(8,128)(2,1)S(1)}, bf16[4,128,768]{2,1,0:T(8,128)(2,1)S(1)}, u32[]{:S(2)}, u32[]{:S(2)}) %collective-permute-start.32) | collective-permute-done | bytes 786464 | tf_op jit(solution)/shard_map/ppermute | solution.py:30
  113.8 2.9 %collective-permute-start.36 = (bf16[128,768]{1,0:T(8,128)(2,1)S(1)}, bf16[128,768]{1,0:T(8,128)(2,1)S(1)}, u32[]{:S(2)}, u32[]{:S(2)}) collective-permute-start(bf16[128,768]{1,0:T(8,128)(2,1)S(1)} %get-tuple-element.49), channel_id=1, source_target_pairs={{0,16},{8,72},{16,32},{24,88},{32,48},{40,104},{48,0},{56,120},{64... | collective-permute-start | bytes 589832 | tf_op jit(solution)/shard_map/ppermute | solution.py:30
  117.5 4.4 %collective-permute-done.36 = bf16[128,768]{1,0:T(8,128)(2,1)S(1)} collective-permute-done((bf16[128,768]{1,0:T(8,128)(2,1)S(1)}, bf16[128,768]{1,0:T(8,128)(2,1)S(1)}, u32[]{:S(2)}, u32[]{:S(2)}) %collective-permute-start.36) | collective-permute-done | bytes 196640 | tf_op jit(solution)/shard_map/ppermute | solution.py:30
  122.0 2.0 %collective-permute-done.37 = bf16[128,768]{1,0:T(8,128)(2,1)S(1)} collective-permute-done((bf16[128,768]{1,0:T(8,128)(2,1)S(1)}, bf16[128,768]{1,0:T(8,128)(2,1)S(1)}, u32[]{:S(2)}, u32[]{:S(2)}) %collective-permute-start.37) | collective-permute-done | bytes 196640 | tf_op jit(solution)/shard_map/ppermute | solution.py:30
  123.9 2.0 %collective-permute-done.38 = bf16[128,768]{1,0:T(8,128)(2,1)S(1)} collective-permute-done((bf16[128,768]{1,0:T(8,128)(2,1)S(1)}, bf16[128,768]{1,0:T(8,128)(2,1)S(1)}, u32[]{:S(2)}, u32[]{:S(2)}) %collective-permute-start.38) | collective-permute-done | bytes 196640 | tf_op jit(solution)/shard_map/ppermute | solution.py:30
  127.4 4.2 %collective-permute-start.40 = (bf16[2,32,768]{2,1,0:T(8,128)(2,1)S(1)}, bf16[2,32,768]{2,1,0:T(8,128)(2,1)S(1)}, u32[]{:S(2)}, u32[]{:S(2)}) collective-permute-start(bf16[2,32,768]{2,1,0:T(8,128)(2,1)S(1)} %pad_maximum_fusion.3), channel_id=1, source_target_pairs={{0,7},{1,2},{2,1},{3,4},{4,3},{5,6},{6,5},{7,0},{8,15},{9,10},{10,... | collective-permute-start | bytes 294920 | tf_op jit(solution)/shard_map/ppermute | solution.py:38
  131.6 3.1 %collective-permute-done.40 = bf16[2,32,768]{2,1,0:T(8,128)(2,1)S(1)} collective-permute-done((bf16[2,32,768]{2,1,0:T(8,128)(2,1)S(1)}, bf16[2,32,768]{2,1,0:T(8,128)(2,1)S(1)}, u32[]{:S(2)}, u32[]{:S(2)}) %collective-permute-start.40) | collective-permute-done | bytes 98336 | tf_op jit(solution)/shard_map/ppermute | solution.py:38
  134.7 2.0 %collective-permute-start.41 = (bf16[2,32,768]{2,1,0:T(8,128)(2,1)S(1)}, bf16[2,32,768]{2,1,0:T(8,128)(2,1)S(1)}, u32[]{:S(2)}, u32[]{:S(2)}) collective-permute-start(bf16[2,32,768]{2,1,0:T(8,128)(2,1)S(1)} %add_convert_fusion.9), channel_id=1, source_target_pairs={{0,3},{1,6},{2,5},{3,0},{4,7},{5,2},{6,1},{7,4},{8,11},{9,14},{10,... | collective-permute-start | bytes 294920 | tf_op jit(solution)/shard_map/ppermute | solution.py:42
  136.8 6.0 %collective-permute-done.41 = bf16[2,32,768]{2,1,0:T(8,128)(2,1)S(1)} collective-permute-done((bf16[2,32,768]{2,1,0:T(8,128)(2,1)S(1)}, bf16[2,32,768]{2,1,0:T(8,128)(2,1)S(1)}, u32[]{:S(2)}, u32[]{:S(2)}) %collective-permute-start.41) | collective-permute-done | bytes 98336 | tf_op jit(solution)/shard_map/ppermute | solution.py:42
  142.8 3.0 %collective-permute-start.42 = (bf16[2,32,768]{2,1,0:T(8,128)(2,1)S(1)}, bf16[2,32,768]{2,1,0:T(8,128)(2,1)S(1)}, u32[]{:S(2)}, u32[]{:S(2)}) collective-permute-start(bf16[2,32,768]{2,1,0:T(8,128)(2,1)S(1)} %add_convert_fusion.8.mine), channel_id=1, source_target_pairs={{0,7},{1,2},{2,1},{3,4},{4,3},{5,6},{6,5},{7,0},{8,15},{9,10},{10,... | collective-permute-start | bytes 294920 | tf_op jit(solution)/shard_map/ppermute | solution.py:38
  145.8 2.9 %collective-permute-done.42.near = bf16[2,32,768]{2,1,0:T(8,128)(2,1)S(1)} collective-permute-done((bf16[2,32,768]{2,1,0:T(8,128)(2,1)S(1)}, bf16[2,32,768]{2,1,0:T(8,128)(2,1)S(1)}, u32[]{:S(2)}, u32[]{:S(2)}) %collective-permute-start.42) | collective-permute-done | bytes 98336 | tf_op jit(solution)/shard_map/ppermute | solution.py:38
  150.4 2.9 %collective-permute-done.44.beyond = bf16[2,32,768]{2,1,0:T(8,128)(2,1)S(1)} collective-permute-done((bf16[2,32,768]{2,1,0:T(8,128)(2,1)S(1)}, bf16[2,32,768]{2,1,0:T(8,128)(2,1)S(1)}, u32[]{:S(2)}, u32[]{:S(2)}) %collective-permute-start.44) | collective-permute-done | bytes 98336 | tf_op jit(solution)/shard_map/ppermute | solution.py:34
  (155 shorter events, 40.7 us)
Async XLA Ops:
  7.7 16.3 %collective-permute-start.2 = (bf16[256,512]{1,0:T(8,128)(2,1)}, bf16[256,512]{1,0:T(8,128)(2,1)S(1)}, u32[]{:S(2)}, u32[]{:S(2)}) collective-permute-start(bf16[256,512]{1,0:T(8,128)(2,1)} %get-tuple-element.27), channel_id=1, source_target_pairs={{0,1},{1,0},{2,3},{3,2},{4,5},{5,4},{6,7},{7,6},{8,9},{9,8},{10,11... | collective-permute-start | bytes 786440 | tf_op jit(solution)/shard_map/ppermute | solution.py:34
  9.8 11.1 %collective-permute-start.8 = (bf16[128,768]{1,0:T(8,128)(2,1)S(1)}, bf16[128,768]{1,0:T(8,128)(2,1)S(1)}, u32[]{:S(2)}, u32[]{:S(2)}) collective-permute-start(bf16[128,768]{1,0:T(8,128)(2,1)S(1)} %get-tuple-element.59), channel_id=1, source_target_pairs={{0,32},{8,136},{16,48},{24,152},{32,0},{40,168},{48,16},{56,184},{... | collective-permute-start | bytes 589832 | tf_op jit(solution)/shard_map/ppermute | solution.py:30
  11.3 7.9 %collective-permute-start.5 = (bf16[128,768]{1,0:T(8,128)(2,1)S(1)}, bf16[128,768]{1,0:T(8,128)(2,1)S(1)}, u32[]{:S(2)}, u32[]{:S(2)}) collective-permute-start(bf16[128,768]{1,0:T(8,128)(2,1)S(1)} %get-tuple-element.59), channel_id=1, source_target_pairs={{0,48},{8,200},{16,0},{24,216},{32,16},{40,232},{48,32},{56,248},{... | collective-permute-start | bytes 589832 | tf_op jit(solution)/shard_map/ppermute | solution.py:30
  13.3 30.0 %collective-permute-start.1 = (bf16[256,2048]{1,0:T(8,128)(2,1)S(1)}, bf16[256,2048]{1,0:T(8,128)(2,1)S(1)}, u32[]{:S(2)}, u32[]{:S(2)}) collective-permute-start(bf16[256,2048]{1,0:T(8,128)(2,1)S(1)} %fusion.t0.refs_0_), channel_id=1, source_target_pairs={{0,1},{1,0},{2,3},{3,2},{4,5},{5,4},{6,7},{7,6},{8,9},{9,8},{10,11... | collective-permute-start | bytes 3145736 | tf_op jit(solution)/shard_map/ppermute | solution.py:34
  13.6 7.3 %collective-permute-start.9 = (bf16[128,768]{1,0:T(8,128)(2,1)S(1)}, bf16[128,768]{1,0:T(8,128)(2,1)S(1)}, u32[]{:S(2)}, u32[]{:S(2)}) collective-permute-start(bf16[128,768]{1,0:T(8,128)(2,1)S(1)} %get-tuple-element.59), channel_id=1, source_target_pairs={{0,16},{8,72},{16,32},{24,88},{32,48},{40,104},{48,0},{56,120},{64... | collective-permute-start | bytes 589832 | tf_op jit(solution)/shard_map/ppermute | solution.py:30
  19.2 9.1 %collective-permute-start.6 = (bf16[256,768]{1,0:T(8,128)(2,1)S(1)}, bf16[256,768]{1,0:T(8,128)(2,1)S(1)}, u32[]{:S(2)}, u32[]{:S(2)}) collective-permute-start(bf16[256,768]{1,0:T(8,128)(2,1)S(1)} %constant_dynamic-update-slice_fusion.2.refs_0_), channel_id=1, source_target_pairs={{0,64},{8,24},{16,80},{24,40},{32,96},{40,56},{48,112},{56,8},{64,... | collective-permute-start | bytes 1179656 | tf_op jit(solution)/shard_map/ppermute | solution.py:30
  20.9 8.3 %collective-permute-start.10 = (bf16[256,768]{1,0:T(8,128)(2,1)S(1)}, bf16[256,768]{1,0:T(8,128)(2,1)S(1)}, u32[]{:S(2)}, u32[]{:S(2)}) collective-permute-start(bf16[256,768]{1,0:T(8,128)(2,1)S(1)} %constant_dynamic-update-slice_fusion.5.refs_1_), channel_id=1, source_target_pairs={{0,192},{8,56},{16,208},{24,8},{32,224},{40,24},{48,240},{56,40},{... | collective-permute-start | bytes 1179656 | tf_op jit(solution)/shard_map/ppermute | solution.py:30
  24.0 9.4 %collective-permute-start.12 = (bf16[256,768]{1,0:T(8,128)(2,1)S(1)}, bf16[256,768]{1,0:T(8,128)(2,1)S(1)}, u32[]{:S(2)}, u32[]{:S(2)}) collective-permute-start(bf16[256,768]{1,0:T(8,128)(2,1)S(1)} %constant_dynamic-update-slice_fusion.2.refs_0_), channel_id=1, source_target_pairs={{0,192},{8,56},{16,208},{24,8},{32,224},{40,24},{48,240},{56,40},{... | collective-permute-start | bytes 1179656 | tf_op jit(solution)/shard_map/ppermute | solution.py:30
  25.8 9.0 %collective-permute-start.13 = (bf16[256,768]{1,0:T(8,128)(2,1)S(1)}, bf16[256,768]{1,0:T(8,128)(2,1)S(1)}, u32[]{:S(2)}, u32[]{:S(2)}) collective-permute-start(bf16[256,768]{1,0:T(8,128)(2,1)S(1)} %constant_dynamic-update-slice_fusion.5.refs_1_), channel_id=1, source_target_pairs={{0,64},{8,24},{16,80},{24,40},{32,96},{40,56},{48,112},{56,8},{64,... | collective-permute-start | bytes 1179656 | tf_op jit(solution)/shard_map/ppermute | solution.py:30
  28.3 10.7 %collective-permute-start.7 = (bf16[256,768]{1,0:T(8,128)(2,1)S(1)}, bf16[256,768]{1,0:T(8,128)(2,1)S(1)}, u32[]{:S(2)}, u32[]{:S(2)}) collective-permute-start(bf16[256,768]{1,0:T(8,128)(2,1)S(1)} %collective-permute-done.6.refs_4_), channel_id=1, source_target_pairs={{0,64},{8,24},{16,80},{24,40},{32,96},{40,56},{48,112},{56,8},{64,... | collective-permute-start | bytes 1179656 | tf_op jit(solution)/shard_map/ppermute | solution.py:30
  29.2 11.6 %collective-permute-start.11 = (bf16[256,768]{1,0:T(8,128)(2,1)S(1)}, bf16[256,768]{1,0:T(8,128)(2,1)S(1)}, u32[]{:S(2)}, u32[]{:S(2)}) collective-permute-start(bf16[256,768]{1,0:T(8,128)(2,1)S(1)} %collective-permute-done.10.refs_3_), channel_id=1, source_target_pairs={{0,192},{8,56},{16,208},{24,8},{32,224},{40,24},{48,240},{56,40},{... | collective-permute-start | bytes 1179656 | tf_op jit(solution)/shard_map/ppermute | solution.py:30
  33.4 13.8 %collective-permute-start.14 = (bf16[256,2048]{1,0:T(8,128)(2,1)S(1)}, bf16[256,2048]{1,0:T(8,128)(2,1)S(1)}, u32[]{:S(2)}, u32[]{:S(2)}) collective-permute-start(bf16[256,2048]{1,0:T(8,128)(2,1)S(1)} %fusion.t0.refs_0_), channel_id=1, source_target_pairs={{0,8},{8,0},{1,9},{9,1},{2,10},{10,2},{3,11},{11,3},{4,12},{12,4},... | collective-permute-start | bytes 3145736 | tf_op jit(solution)/shard_map/ppermute | solution.py:34
  58.0 7.8 %collective-permute-start.24 = (bf16[2,2,128,128]{3,2,1,0:T(8,128)(2,1)S(1)}, bf16[2,2,128,128]{3,2,1,0:T(8,128)(2,1)S(1)}, u32[]{:S(2)}, u32[]{:S(2)}) collective-permute-start(bf16[2,2,128,128]{3,2,1,0:T(8,128)(2,1)S(1)} %get-tuple-element.37), channel_id=1, source_target_pairs={{0,64},{64,0},{128,192},{192,128},{1,65},{65,1},{129,193},{193,129... | collective-permute-start | bytes 393224 | tf_op jit(solution)/shard_map/ppermute | solution.py:34
  58.0 9.8 %collective-permute-start.26 = (bf16[2,2,128,128]{3,2,1,0:T(8,128)(2,1)S(1)}, bf16[2,2,128,128]{3,2,1,0:T(8,128)(2,1)S(1)}, u32[]{:S(2)}, u32[]{:S(2)}) collective-permute-start(bf16[2,2,128,128]{3,2,1,0:T(8,128)(2,1)S(1)} %get-tuple-element.38), channel_id=1, source_target_pairs={{0,192},{64,128},{128,64},{192,0},{1,193},{65,129},{129,65},{193,1... | collective-permute-start | bytes 393224 | tf_op jit(solution)/shard_map/ppermute | solution.py:34
  59.2 8.7 %collective-permute-start.25 = (bf16[2,2,128,128]{3,2,1,0:T(8,128)(2,1)S(1)}, bf16[2,2,128,128]{3,2,1,0:T(8,128)(2,1)S(1)}, u32[]{:S(2)}, u32[]{:S(2)}) collective-permute-start(bf16[2,2,128,128]{3,2,1,0:T(8,128)(2,1)S(1)} %get-tuple-element.38), channel_id=1, source_target_pairs={{0,128},{64,192},{128,0},{192,64},{1,129},{65,193},{129,1},{193,65... | collective-permute-start | bytes 393224 | tf_op jit(solution)/shard_map/ppermute | solution.py:34
  62.1 9.6 %collective-permute-start.20 = (bf16[2,2,128,128]{3,2,1,0:T(8,128)(2,1)S(1)}, bf16[2,2,128,128]{3,2,1,0:T(8,128)(2,1)S(1)}, u32[]{:S(2)}, u32[]{:S(2)}) collective-permute-start(bf16[2,2,128,128]{3,2,1,0:T(8,128)(2,1)S(1)} %get-tuple-element.36), channel_id=1, source_target_pairs={{0,48},{16,32},{32,16},{48,0},{1,49},{17,33},{33,17},{49,1},{2,50}... | collective-permute-start | bytes 393224 | tf_op jit(solution)/shard_map/ppermute | solution.py:34
  65.8 7.6 %collective-permute-start.19 = (bf16[2,2,128,128]{3,2,1,0:T(8,128)(2,1)S(1)}, bf16[2,2,128,128]{3,2,1,0:T(8,128)(2,1)S(1)}, u32[]{:S(2)}, u32[]{:S(2)}) collective-permute-start(bf16[2,2,128,128]{3,2,1,0:T(8,128)(2,1)S(1)} %get-tuple-element.36), channel_id=1, source_target_pairs={{0,32},{16,48},{32,0},{48,16},{1,33},{17,49},{33,1},{49,17},{2,34}... | collective-permute-start | bytes 393224 | tf_op jit(solution)/shard_map/ppermute | solution.py:34
  65.8 7.6 %collective-permute-start.18 = (bf16[2,2,128,128]{3,2,1,0:T(8,128)(2,1)S(1)}, bf16[2,2,128,128]{3,2,1,0:T(8,128)(2,1)S(1)}, u32[]{:S(2)}, u32[]{:S(2)}) collective-permute-start(bf16[2,2,128,128]{3,2,1,0:T(8,128)(2,1)S(1)} %get-tuple-element.36), channel_id=1, source_target_pairs={{0,16},{16,0},{32,48},{48,32},{1,17},{17,1},{33,49},{49,33},{2,18}... | collective-permute-start | bytes 393224 | tf_op jit(solution)/shard_map/ppermute | solution.py:34
  68.0 16.1 %collective-permute-start.29 = (bf16[2,2,128,128]{3,2,1,0:T(8,128)(2,1)S(1)}, bf16[2,2,128,128]{3,2,1,0:T(8,128)(2,1)S(1)}, u32[]{:S(2)}, u32[]{:S(2)}) collective-permute-start(bf16[2,2,128,128]{3,2,1,0:T(8,128)(2,1)S(1)} %get-tuple-element.52), channel_id=1, source_target_pairs={{0,48},{16,32},{32,16},{48,0},{1,49},{17,33},{33,17},{49,1},{2,50}... | collective-permute-start | bytes 393224 | tf_op jit(solution)/shard_map/ppermute | solution.py:34
  71.7 12.3 %collective-permute-start.28 = (bf16[2,2,128,128]{3,2,1,0:T(8,128)(2,1)S(1)}, bf16[2,2,128,128]{3,2,1,0:T(8,128)(2,1)S(1)}, u32[]{:S(2)}, u32[]{:S(2)}) collective-permute-start(bf16[2,2,128,128]{3,2,1,0:T(8,128)(2,1)S(1)} %get-tuple-element.52), channel_id=1, source_target_pairs={{0,32},{16,48},{32,0},{48,16},{1,33},{17,49},{33,1},{49,17},{2,34}... | collective-permute-start | bytes 393224 | tf_op jit(solution)/shard_map/ppermute | solution.py:34
  73.5 10.6 %collective-permute-start.23 = (bf16[2,2,128,128]{3,2,1,0:T(8,128)(2,1)S(1)}, bf16[2,2,128,128]{3,2,1,0:T(8,128)(2,1)S(1)}, u32[]{:S(2)}, u32[]{:S(2)}) collective-permute-start(bf16[2,2,128,128]{3,2,1,0:T(8,128)(2,1)S(1)} %add_convert_fusion.7), channel_id=1, source_target_pairs={{0,192},{64,128},{128,64},{192,0},{1,193},{65,129},{129,65},{193,1... | collective-permute-start | bytes 393224 | tf_op jit(solution)/shard_map/ppermute | solution.py:34
  74.6 9.4 %collective-permute-start.22 = (bf16[2,2,128,128]{3,2,1,0:T(8,128)(2,1)S(1)}, bf16[2,2,128,128]{3,2,1,0:T(8,128)(2,1)S(1)}, u32[]{:S(2)}, u32[]{:S(2)}) collective-permute-start(bf16[2,2,128,128]{3,2,1,0:T(8,128)(2,1)S(1)} %add_convert_fusion.7), channel_id=1, source_target_pairs={{0,128},{64,192},{128,0},{192,64},{1,129},{65,193},{129,1},{193,65... | collective-permute-start | bytes 393224 | tf_op jit(solution)/shard_map/ppermute | solution.py:34
  88.2 7.9 %collective-permute-start.33 = (bf16[2,128,768]{2,1,0:T(8,128)(2,1)S(1)}, bf16[2,128,768]{2,1,0:T(8,128)(2,1)S(1)}, u32[]{:S(2)}, u32[]{:S(2)}) collective-permute-start(bf16[2,128,768]{2,1,0:T(8,128)(2,1)S(1)} %get-tuple-element.46), channel_id=1, source_target_pairs={{0,192},{8,56},{16,208},{24,8},{32,224},{40,24},{48,240},{56,40},{... | collective-permute-start | bytes 1179656 | tf_op jit(solution)/shard_map/ppermute | solution.py:30
  89.5 9.2 %collective-permute-start.31 = (bf16[2,128,768]{2,1,0:T(8,128)(2,1)S(1)}, bf16[2,128,768]{2,1,0:T(8,128)(2,1)S(1)}, u32[]{:S(2)}, u32[]{:S(2)}) collective-permute-start(bf16[2,128,768]{2,1,0:T(8,128)(2,1)S(1)} %get-tuple-element.44), channel_id=1, source_target_pairs={{0,64},{8,24},{16,80},{24,40},{32,96},{40,56},{48,112},{56,8},{64,... | collective-permute-start | bytes 1179656 | tf_op jit(solution)/shard_map/ppermute | solution.py:30
  96.2 12.1 %collective-permute-start.34 = (bf16[4,128,768]{2,1,0:T(8,128)(2,1)S(1)}, bf16[4,128,768]{2,1,0:T(8,128)(2,1)S(1)}, u32[]{:S(2)}, u32[]{:S(2)}) collective-permute-start(bf16[4,128,768]{2,1,0:T(8,128)(2,1)S(1)} %pad_maximum_fusion.1), channel_id=1, source_target_pairs={{0,192},{8,56},{16,208},{24,8},{32,224},{40,24},{48,240},{56,40},{... | collective-permute-start | bytes 2359304 | tf_op jit(solution)/shard_map/ppermute | solution.py:30
  98.9 13.3 %collective-permute-start.32 = (bf16[4,128,768]{2,1,0:T(8,128)(2,1)S(1)}, bf16[4,128,768]{2,1,0:T(8,128)(2,1)S(1)}, u32[]{:S(2)}, u32[]{:S(2)}) collective-permute-start(bf16[4,128,768]{2,1,0:T(8,128)(2,1)S(1)} %pad_maximum_fusion), channel_id=1, source_target_pairs={{0,64},{8,24},{16,80},{24,40},{32,96},{40,56},{48,112},{56,8},{64,... | collective-permute-start | bytes 2359304 | tf_op jit(solution)/shard_map/ppermute | solution.py:30
  99.1 9.2 %collective-permute-start.35 = (bf16[2,256,256]{2,1,0:T(8,128)(2,1)S(1)}, bf16[2,256,256]{2,1,0:T(8,128)(2,1)S(1)}, u32[]{:S(2)}, u32[]{:S(2)}) collective-permute-start(bf16[2,256,256]{2,1,0:T(8,128)(2,1)S(1)} %pad_maximum_fusion.2), channel_id=1, source_target_pairs={{0,1},{1,0},{2,3},{3,2},{4,5},{5,4},{6,7},{7,6},{8,9},{9,8},{10,11... | collective-permute-start | bytes 786440 | tf_op jit(solution)/shard_map/ppermute | solution.py:34
  113.8 8.2 %collective-permute-start.36 = (bf16[128,768]{1,0:T(8,128)(2,1)S(1)}, bf16[128,768]{1,0:T(8,128)(2,1)S(1)}, u32[]{:S(2)}, u32[]{:S(2)}) collective-permute-start(bf16[128,768]{1,0:T(8,128)(2,1)S(1)} %get-tuple-element.49), channel_id=1, source_target_pairs={{0,16},{8,72},{16,32},{24,88},{32,48},{40,104},{48,0},{56,120},{64... | collective-permute-start | bytes 589832 | tf_op jit(solution)/shard_map/ppermute | solution.py:30
  116.7 7.3 %collective-permute-start.37 = (bf16[128,768]{1,0:T(8,128)(2,1)S(1)}, bf16[128,768]{1,0:T(8,128)(2,1)S(1)}, u32[]{:S(2)}, u32[]{:S(2)}) collective-permute-start(bf16[128,768]{1,0:T(8,128)(2,1)S(1)} %get-tuple-element.50), channel_id=1, source_target_pairs={{0,32},{8,136},{16,48},{24,152},{32,0},{40,168},{48,16},{56,184},{... | collective-permute-start | bytes 589832 | tf_op jit(solution)/shard_map/ppermute | solution.py:30
  116.9 9.0 %collective-permute-start.38 = (bf16[128,768]{1,0:T(8,128)(2,1)S(1)}, bf16[128,768]{1,0:T(8,128)(2,1)S(1)}, u32[]{:S(2)}, u32[]{:S(2)}) collective-permute-start(bf16[128,768]{1,0:T(8,128)(2,1)S(1)} %get-tuple-element.51), channel_id=1, source_target_pairs={{0,48},{8,200},{16,0},{24,216},{32,16},{40,232},{48,32},{56,248},{... | collective-permute-start | bytes 589832 | tf_op jit(solution)/shard_map/ppermute | solution.py:30
  127.4 7.3 %collective-permute-start.40 = (bf16[2,32,768]{2,1,0:T(8,128)(2,1)S(1)}, bf16[2,32,768]{2,1,0:T(8,128)(2,1)S(1)}, u32[]{:S(2)}, u32[]{:S(2)}) collective-permute-start(bf16[2,32,768]{2,1,0:T(8,128)(2,1)S(1)} %pad_maximum_fusion.3), channel_id=1, source_target_pairs={{0,7},{1,2},{2,1},{3,4},{4,3},{5,6},{6,5},{7,0},{8,15},{9,10},{10,... | collective-permute-start | bytes 294920 | tf_op jit(solution)/shard_map/ppermute | solution.py:38
  134.7 8.0 %collective-permute-start.41 = (bf16[2,32,768]{2,1,0:T(8,128)(2,1)S(1)}, bf16[2,32,768]{2,1,0:T(8,128)(2,1)S(1)}, u32[]{:S(2)}, u32[]{:S(2)}) collective-permute-start(bf16[2,32,768]{2,1,0:T(8,128)(2,1)S(1)} %add_convert_fusion.9), channel_id=1, source_target_pairs={{0,3},{1,6},{2,5},{3,0},{4,7},{5,2},{6,1},{7,4},{8,11},{9,14},{10,... | collective-permute-start | bytes 294920 | tf_op jit(solution)/shard_map/ppermute | solution.py:42
  (39 other events, 429.7 us)

commit v3 on v2

--- a/solution.py
+++ b/solution.py
@@ -90,34 +90,30 @@
     return lam * bit.astype(F32) * (1.0 / math.sqrt(HEAD * 2 ** (level - 1) * BLOCK))
 
 
-def prepare_kernel(pos, w, w_own, w_core):
+def prepare_kernel(pos, w, cot, w_own, w_core, own, to_core, to_z):
     core, kind = pos[2], pos[4]
-    mine = pl.multiple_of((core * 2 + kind) * 256, 256)
-    other = pl.multiple_of(((1 - core) * 2 + kind) * 256, 256)
+
+    def columns(cs, zs):
+        group = ((core + cs) & 1) * 2 + ((kind + zs) & 1)
+        return pl.ds(pl.multiple_of(group * 256, 256), 256)
+
     for third in range(3):
         at = slice(third * 256, third * 256 + 256)
-        w_own[:, at] = w[third, :, pl.ds(mine, 256)]
-        w_core[:, at] = w[third, :, pl.ds(other, 256)]
-
-
-def split_kernel(pos, cot, own, to_core, to_z):
-    core, kind = pos[2], pos[4]
-
-    def columns(cs, zs):
-        group = ((core + cs) & 1) * 2 + ((kind + zs) & 1)
-        return cot[:, pl.ds(pl.multiple_of(group * 256, 256), 256)]
-
-    own[...] = columns(0, 0)
-    to_core[...] = columns(1, 0)
-    to_z[:, :256] = columns(0, 1)
-    to_z[:, 256:] = columns(1, 1)
-
-
-def project_kernel(pos, idx, table, t0, t1, t2, t3, c0, c1, c2, c3, *refs):
-    toks = (t0, t1, t2, t3)
+        w_own[:, at] = w[third, :, columns(0, 0)]
+        w_core[:, at] = w[third, :, columns(1, 0)]
+    own[...] = cot[:, columns(0, 0)]
+    to_core[...] = cot[:, columns(1, 0)]
+    to_z[:, :256] = cot[:, columns(0, 1)]
+    to_z[:, 256:] = cot[:, columns(1, 1)]
+
+
+def project_kernel(pos, idx, table, c0, c1, c2, c3, *refs):
     parts = (refs[0:2], refs[2:4], refs[6:8], refs[4:6])
-    qkv, cots, s1, x0, g1, m2, m3, m4, m5, w = refs[8:]
+    qkv, cots, s1, x0, g1, m2, m3, m4, m5, w, toks, sems = refs[12:]
     y, x, core = pos[0], pos[1], pos[2]
+    copies = [pltpu.make_async_copy(refs[8 + b], toks.at[b], sems.at[b]) for b in range(4)]
+    for copy in copies:
+        copy.start()
     for slot in range(4):
         for dist in range(4):
             yy = (y + dist + core * (slot - dist)) & 3
@@ -129,11 +125,13 @@
     for blk, src in enumerate((c0, c1, c2, c3)):
         cots[blk] = src[...]
 
-    @pl.loop(0, 3)
-    def _(part):
-        cols = pl.ds(pl.multiple_of(part * 256, 256), 256)
-        for blk in range(4):
-            qkv[blk, :, cols] = dot(toks[blk][...], w[:, cols], 1, 0).astype(BF)
+    for blk in range(4):
+        copies[blk].wait()
+
+        @pl.loop(0, 3)
+        def _(part, blk=blk):
+            cols = pl.ds(pl.multiple_of(part * 256, 256), 256)
+            qkv[blk, :, cols] = dot(toks[blk], w[:, cols], 1, 0).astype(BF)
 
     @pl.loop(0, 4)
     def _(step):
@@ -319,21 +317,13 @@
     idx = jnp.concatenate([rows, swap(rows, "core", 2, 1)], axis=0)
     scalars = [pos, idx, weight_table]
 
-    w_own, w_core = call(
+    w_own, w_core, c_own, c_core, c_z = call(
         prepare_kernel,
-        [pos, jnp.transpose(w_qkv, (1, 0, 2))],
+        [pos, jnp.transpose(w_qkv, (1, 0, 2)), cotangent[0]],
         1,
-        [((64, COLS), BF)] * 2,
+        [((64, COLS), BF)] * 2 + [((BLOCK, 256), BF)] * 2 + [((BLOCK, 512), BF)],
         grant=58,
-        nbytes=MIB,
-    )
-    c_own, c_core, c_z = call(
-        split_kernel,
-        [pos, cotangent[0]],
-        1,
-        [((BLOCK, 256), BF)] * 2 + [((BLOCK, 512), BF)],
-        grant=58,
-        nbytes=MIB,
+        nbytes=2 * MIB,
     )
 
     chunk = jnp.concatenate([w_own, swap(w_core, "core", 2, 1)], axis=0)
@@ -355,7 +345,7 @@
     tile = (HEAD, HEAD)
     qkv, cots, s1, x0, g1, m2, m3, m4, m5 = call(
         project_kernel,
-        scalars + toks + [c_own, c_near, c_core, c_across] + gathered,
+        scalars + [c_own, c_near, c_core, c_across] + gathered + toks,
         3,
         [
             ((4, BLOCK, COLS), BF),
@@ -368,8 +358,13 @@
             ((2, 2) + tile, BF),
             ((2, 2) + tile, BF),
         ],
-        scratch=[pltpu.VMEM((D, COLS), BF)],
+        scratch=[
+            pltpu.VMEM((D, COLS), BF),
+            pltpu.VMEM((4, BLOCK, D), BF),
+            pltpu.SemaphoreType.DMA((4,)),
+        ],
         grant=52,
+        n_any=4,
         flops=2 * 1024 * D * COLS,
         nbytes=10 * MIB,
     )

time: 155 us -> 156 us (level)
    pallas_call x9 -> x8, Pallas kernels: 30.7 us -> 30.7 us  [call(): pl.pallas_call(kernel, out_shape=[jax.ShapeDtypeStruct(*out) for out in o...]
  transfers between devices with their start and end apart: 45 -> 45, of which waited for: 21 -> 21; matrix products, arithmetic and copies ran while one was open for 5% -> 5% of each run, Pallas kernels for 9% -> 8%
where the time goes in v3:
time: 156 us; the launch traced here: 155 us
  starting transfers between devices  55.3 us (35%)
  waiting for transfers between devices  53.8 us (34%)
  Pallas kernels  30.7 us (20%)
  local copies, waits for them, and re-layouts  8.05 us (5%)
  between operations  5.1 us (3%)
  other arithmetic  2.39 us (2%)
    pallas_call x8, Pallas kernels, call(): pl.pallas_call(kernel, out_shape=[jax.ShapeDtypeStruct(*out) for out in o...  30.7 us
    ppermute x16, starting transfers between devices, ring(): return lax.ppermute(value, ('y', 'x', 'core'), pairs)  25.8 us
    ppermute x16, waiting for transfers between devices, ring(): return lax.ppermute(value, ('y', 'x', 'core'), pairs)  23.6 us
    ppermute x26, starting transfers between devices, swap(): return lax.ppermute(value, axis, [(i, i ^ mask) for i in range(size)])  20.1 us
    ppermute x26, waiting for transfers between devices, swap(): return lax.ppermute(value, axis, [(i, i ^ mask) for i in range(size)])  18.4 us
    ppermute x2, starting transfers between devices, same_set_neighbour(): lax.ppermute(value, 'dp', [(z, (z + 1 if z % 2 else z - 1) % 8) for z in...  7.41 us
    ppermute x1, waiting for transfers between devices, same_set_far(): lax.ppermute(value, 'dp', [(z, ((7 if SETS >> z & 1 else 3) - z) % 8) for...  5.99 us
    ppermute x2, waiting for transfers between devices, same_set_neighbour(): lax.ppermute(value, 'dp', [(z, (z + 1 if z % 2 else z - 1) % 8) for z in...  5.8 us
  transfers between devices with their start and end apart: 45, of which 21 were waited for; matrix products, arithmetic and copies ran while one was open for 5% of the time, Pallas kernels for 8%

profile of v3, /device:TPU:6, one launch (start us, length us, event | category | flops | bytes accessed | tf_op | source)
XLA Modules:
  0.0 155.4 jit_solution(179464564133413084)
XLA Ops:
  1.5 1.9 %collective-permute-start = (s32[1,12]{1,0:T(1,128)S(1)}, s32[1,12]{1,0:T(1,128)S(1)}, u32[]{:S(2)}, u32[]{:S(2)}) collective-permute-start(s32[1,12]{1,0:T(1,128)S(1)} %reshape.24), channel_id=1, source_target_pairs={{0,1},{1,0},{2,3},{3,2},{4,5},{5,4},{6,7},{7,6},{8,9},{9,8},{10,11... | collective-permute-start | bytes 152 | tf_op jit(solution)/shard_map/ppermute | solution.py:34
  4.0 2.1 %shard_map.68 = (bf16[64,768]{1,0:T(8,128)(2,1)}, bf16[64,768]{1,0:T(8,128)(2,1)}, bf16[256,256]{1,0:T(8,128)(2,1)}, bf16[256,256]{1,0:T(8,128)(2,1)}, bf16[256,512]{1,0:T(8,128)(2,1)}) custom-call(s32[7]{0:T(128)} %stack.43.pos, bf16[3,64,1024]{2,1,0:T(8,128)(2,1)} %bitcast.23, bf16[256,1024]{1,0:T(8,128)(2,1)} %bitcast.22), custom_call_target="tpu_custom_call" | custom-call | bytes 2097152 | tf_op jit(solution)/shard_map/pallas_call | solution.py:65
  12.3 3.2 %collective-permute-start.9 = (bf16[128,768]{1,0:T(8,128)(2,1)S(1)}, bf16[128,768]{1,0:T(8,128)(2,1)S(1)}, u32[]{:S(2)}, u32[]{:S(2)}) collective-permute-start(bf16[128,768]{1,0:T(8,128)(2,1)S(1)} %get-tuple-element.59), channel_id=1, source_target_pairs={{0,16},{8,72},{16,32},{24,88},{32,48},{40,104},{48,0},{56,120},{64... | collective-permute-start | bytes 589832 | tf_op jit(solution)/shard_map/ppermute | solution.py:30
  15.5 2.3 %collective-permute-done.5 = bf16[128,768]{1,0:T(8,128)(2,1)S(1)} collective-permute-done((bf16[128,768]{1,0:T(8,128)(2,1)S(1)}, bf16[128,768]{1,0:T(8,128)(2,1)S(1)}, u32[]{:S(2)}, u32[]{:S(2)}) %collective-permute-start.5) | collective-permute-done | bytes 196640 | tf_op jit(solution)/shard_map/ppermute | solution.py:30
  19.6 3.0 %collective-permute-start.10 = (bf16[256,768]{1,0:T(8,128)(2,1)S(1)}, bf16[256,768]{1,0:T(8,128)(2,1)S(1)}, u32[]{:S(2)}, u32[]{:S(2)}) collective-permute-start(bf16[256,768]{1,0:T(8,128)(2,1)S(1)} %constant_dynamic-update-slice_fusion.5.refs_1_), channel_id=1, source_target_pairs={{0,192},{8,56},{16,208},{24,8},{32,224},{40,24},{48,240},{56,40},{... | collective-permute-start | bytes 1179656 | tf_op jit(solution)/shard_map/ppermute | solution.py:30
  24.8 2.1 %collective-permute-done.6.refs_4_ = bf16[256,768]{1,0:T(8,128)(2,1)S(1)} collective-permute-done((bf16[256,768]{1,0:T(8,128)(2,1)S(1)}, bf16[256,768]{1,0:T(8,128)(2,1)S(1)}, u32[]{:S(2)}, u32[]{:S(2)}) %collective-permute-start.6) | collective-permute-done | bytes 393248 | tf_op jit(solution)/shard_map/ppermute | solution.py:30
  27.8 3.7 %collective-permute-start.11 = (bf16[256,768]{1,0:T(8,128)(2,1)S(1)}, bf16[256,768]{1,0:T(8,128)(2,1)S(1)}, u32[]{:S(2)}, u32[]{:S(2)}) collective-permute-start(bf16[256,768]{1,0:T(8,128)(2,1)S(1)} %collective-permute-done.10.refs_3_), channel_id=1, source_target_pairs={{0,192},{8,56},{16,208},{24,8},{32,224},{40,24},{48,240},{56,40},{... | collective-permute-start | bytes 1179656 | tf_op jit(solution)/shard_map/ppermute | solution.py:30
  34.0 3.7 %collective-permute-done.7.refs_6_ = bf16[256,768]{1,0:T(8,128)(2,1)S(1)} collective-permute-done((bf16[256,768]{1,0:T(8,128)(2,1)S(1)}, bf16[256,768]{1,0:T(8,128)(2,1)S(1)}, u32[]{:S(2)}, u32[]{:S(2)}) %collective-permute-start.7) | collective-permute-done | bytes 393248 | tf_op jit(solution)/shard_map/ppermute | solution.py:30
  47.0 11.4 %shard_map.69 = (bf16[4,256,768]{2,1,0:T(8,128)(2,1)}, bf16[4,256,256]{2,1,0:T(8,128)(2,1)}, bf16[4,2,128,128]{3,2,1,0:T(8,128)(2,1)S(1)}, bf16[2,2,128,128]{3,2...) custom-call(s32[7]{0:T(128)S(1)} %copy-done.10, ...), custom_call_target="tpu_custom_call" | custom-call | flops 3221225472 | bytes 10485760 | tf_op jit(solution)/shard_map/pallas_call | solution.py:65
  59.5 3.0 %collective-permute-start.25 = (bf16[2,2,128,128]{3,2,1,0:T(8,128)(2,1)S(1)}, bf16[2,2,128,128]{3,2,1,0:T(8,128)(2,1)S(1)}, u32[]{:S(2)}, u32[]{:S(2)}) collective-permute-start(bf16[2,2,128,128]{3,2,1,0:T(8,128)(2,1)S(1)} %get-tuple-element.38), channel_id=1, source_target_pairs={{0,128},{64,192},{128,0},{192,64},{1,129},{65,193},{129,1},{193,65... | collective-permute-start | bytes 393224 | tf_op jit(solution)/shard_map/ppermute | solution.py:34
  62.6 3.7 %collective-permute-start.20 = (bf16[2,2,128,128]{3,2,1,0:T(8,128)(2,1)S(1)}, bf16[2,2,128,128]{3,2,1,0:T(8,128)(2,1)S(1)}, u32[]{:S(2)}, u32[]{:S(2)}) collective-permute-start(bf16[2,2,128,128]{3,2,1,0:T(8,128)(2,1)S(1)} %get-tuple-element.36), channel_id=1, source_target_pairs={{0,48},{16,32},{32,16},{48,0},{1,49},{17,33},{33,17},{49,1},{2,50}... | collective-permute-start | bytes 393224 | tf_op jit(solution)/shard_map/ppermute | solution.py:34
  68.4 3.8 %collective-permute-start.29 = (bf16[2,2,128,128]{3,2,1,0:T(8,128)(2,1)S(1)}, bf16[2,2,128,128]{3,2,1,0:T(8,128)(2,1)S(1)}, u32[]{:S(2)}, u32[]{:S(2)}) collective-permute-start(bf16[2,2,128,128]{3,2,1,0:T(8,128)(2,1)S(1)} %get-tuple-element.52), channel_id=1, source_target_pairs={{0,48},{16,32},{32,16},{48,0},{1,49},{17,33},{33,17},{49,1},{2,50}... | collective-permute-start | bytes 393224 | tf_op jit(solution)/shard_map/ppermute | solution.py:34
  76.4 2.4 %collective-permute-done.27.refs_16_ = bf16[2,2,128,128]{3,2,1,0:T(8,128)(2,1)S(1)} collective-permute-done((bf16[2,2,128,128]{3,2,1,0:T(8,128)(2,1)S(1)}, bf16[2,2,128,128]{3,2,1,0:T(8,128)(2,1)S(1)}, u32[]{:S(2)}, u32[]{:S(2)}) %collective-permute-start.27) | collective-permute-done | bytes 131104 | tf_op jit(solution)/shard_map/ppermute | solution.py:34
  80.0 4.4 %shard_map.70.refs_6_ = f32[4,256,1024]{2,1,0:T(8,128)S(1)} custom-call(s32[7]{0:T(128)S(1)} %copy-done.10, s32[4,12]{1,0:T(4,128)S(1)} %pad_add_fusion.idx, f32[16,8]{1,0:T(8,128)S(1)} %copy.9.table, bf16[4,256,768]{2,1,0:T(8,128)(2,1)S(1)} %copy-done.6, bf16[4,256,256]{2,1,0:T(8,128)(2,1)S(1)} %copy-done.7), custom_call_target="tpu_custom_call" | custom-call | flops 805306368 | bytes 8388608 | tf_op jit(solution)/shard_map/pallas_call | solution.py:65
  84.5 3.9 %shard_map.71 = (bf16[4,256,256]{2,1,0:T(8,128)(2,1)S(1)}, bf16[4,256,768]{2,1,0:T(8,128)(2,1)S(1)}, bf16[2,128,768]{2,1,0:T(8,128)(2,1)S(1)}, bf16[2,128,768]{2,1,0:T(8,128)(2,1)S(1)}) custom-call(s32[7]{0:T(128)S(1)} %copy-done.10, s32[4,12]{1,0:T(4,128)S(1)} %pad_add_fusion.idx, f32[16,8]{1,0:T(8,128)S(1)} %copy.9.table, bf16[256,2048]{1,0:T(8,128)(2,1)S(1)} %copy-done.1, ...), custom_call_target="tpu_custom_call" | custom-call | flops 1610612736 | bytes 12582912 | tf_op jit(solution)/shard_map/pallas_call | solution.py:65
  90.9 3.3 %shard_map.73 = (bf16[4,128,768]{2,1,0:T(8,128)(2,1)S(1)}, bf16[4,128,768]{2,1,0:T(8,128)(2,1)S(1)}) custom-call(s32[7]{0:T(128)S(1)} %copy-done.10, bf16[256,2048]{1,0:T(8,128)(2,1)S(1)} %copy-done.1, bf16[256,2048]{1,0:T(8,128)(2,1)S(1)} %copy-done.3, bf16[256,2048]{1,0:T(8,128)(2,1)S(1)} %copy-done.5, ...), custom_call_target="tpu_custom_call" | custom-call | flops 1610612736 | bytes 9437184 | tf_op jit(solution)/shard_map/pallas_call | solution.py:65
  94.3 2.3 %collective-permute-done.33 = bf16[2,128,768]{2,1,0:T(8,128)(2,1)S(1)} collective-permute-done((bf16[2,128,768]{2,1,0:T(8,128)(2,1)S(1)}, bf16[2,128,768]{2,1,0:T(8,128)(2,1)S(1)}, u32[]{:S(2)}, u32[]{:S(2)}) %collective-permute-start.33) | collective-permute-done | bytes 393248 | tf_op jit(solution)/shard_map/ppermute | solution.py:30
  96.8 2.5 %collective-permute-start.34 = (bf16[4,128,768]{2,1,0:T(8,128)(2,1)S(1)}, bf16[4,128,768]{2,1,0:T(8,128)(2,1)S(1)}, u32[]{:S(2)}, u32[]{:S(2)}) collective-permute-start(bf16[4,128,768]{2,1,0:T(8,128)(2,1)S(1)} %pad_maximum_fusion.1), channel_id=1, source_target_pairs={{0,192},{8,56},{16,208},{24,8},{32,224},{40,24},{48,240},{56,40},{... | collective-permute-start | bytes 2359304 | tf_op jit(solution)/shard_map/ppermute | solution.py:30
  99.8 2.5 %shard_map.72.own = bf16[4,128,768]{2,1,0:T(8,128)(2,1)S(1)} custom-call(s32[7]{0:T(128)S(1)} %copy-done.10, bf16[256,2048]{1,0:T(8,128)(2,1)S(1)} %copy-done.1, bf16[256,2048]{1,0:T(8,128)(2,1)S(1)} %copy-done.3, bf16[256,2048]{1,0:T(8,128)(2,1)S(1)} %copy-done.5, bf16[256,2048]{1,0:T(8,128)(2,1)} %collective-permute-done.15.refs_11_.refs_3_.t3, ...), custom_call_target="tpu_custom_call" | custom-call | flops 402653184 | bytes 9437184 | tf_op jit(solution)/shard_map/pallas_call | solution.py:65
  102.3 6.6 %collective-permute-done.35.from_z = bf16[2,256,256]{2,1,0:T(8,128)(2,1)S(1)} collective-permute-done((bf16[2,256,256]{2,1,0:T(8,128)(2,1)S(1)}, bf16[2,256,256]{2,1,0:T(8,128)(2,1)S(1)}, u32[]{:S(2)}, u32[]{:S(2)}) %collective-permute-start.35) | collective-permute-done | bytes 262176 | tf_op jit(solution)/shard_map/ppermute | solution.py:34
  108.9 3.9 %collective-permute-done.32.r1 = bf16[4,128,768]{2,1,0:T(8,128)(2,1)S(1)} collective-permute-done((bf16[4,128,768]{2,1,0:T(8,128)(2,1)S(1)}, bf16[4,128,768]{2,1,0:T(8,128)(2,1)S(1)}, u32[]{:S(2)}, u32[]{:S(2)}) %collective-permute-start.32) | collective-permute-done | bytes 786464 | tf_op jit(solution)/shard_map/ppermute | solution.py:30
  114.4 2.9 %collective-permute-start.36 = (bf16[128,768]{1,0:T(8,128)(2,1)S(1)}, bf16[128,768]{1,0:T(8,128)(2,1)S(1)}, u32[]{:S(2)}, u32[]{:S(2)}) collective-permute-start(bf16[128,768]{1,0:T(8,128)(2,1)S(1)} %get-tuple-element.49), channel_id=1, source_target_pairs={{0,16},{8,72},{16,32},{24,88},{32,48},{40,104},{48,0},{56,120},{64... | collective-permute-start | bytes 589832 | tf_op jit(solution)/shard_map/ppermute | solution.py:30
  118.1 4.4 %collective-permute-done.36 = bf16[128,768]{1,0:T(8,128)(2,1)S(1)} collective-permute-done((bf16[128,768]{1,0:T(8,128)(2,1)S(1)}, bf16[128,768]{1,0:T(8,128)(2,1)S(1)}, u32[]{:S(2)}, u32[]{:S(2)}) %collective-permute-start.36) | collective-permute-done | bytes 196640 | tf_op jit(solution)/shard_map/ppermute | solution.py:30
  122.6 2.0 %collective-permute-done.37 = bf16[128,768]{1,0:T(8,128)(2,1)S(1)} collective-permute-done((bf16[128,768]{1,0:T(8,128)(2,1)S(1)}, bf16[128,768]{1,0:T(8,128)(2,1)S(1)}, u32[]{:S(2)}, u32[]{:S(2)}) %collective-permute-start.37) | collective-permute-done | bytes 196640 | tf_op jit(solution)/shard_map/ppermute | solution.py:30
  124.6 2.0 %collective-permute-done.38 = bf16[128,768]{1,0:T(8,128)(2,1)S(1)} collective-permute-done((bf16[128,768]{1,0:T(8,128)(2,1)S(1)}, bf16[128,768]{1,0:T(8,128)(2,1)S(1)}, u32[]{:S(2)}, u32[]{:S(2)}) %collective-permute-start.38) | collective-permute-done | bytes 196640 | tf_op jit(solution)/shard_map/ppermute | solution.py:30
  128.1 4.2 %collective-permute-start.40 = (bf16[2,32,768]{2,1,0:T(8,128)(2,1)S(1)}, bf16[2,32,768]{2,1,0:T(8,128)(2,1)S(1)}, u32[]{:S(2)}, u32[]{:S(2)}) collective-permute-start(bf16[2,32,768]{2,1,0:T(8,128)(2,1)S(1)} %pad_maximum_fusion.3), channel_id=1, source_target_pairs={{0,7},{1,2},{2,1},{3,4},{4,3},{5,6},{6,5},{7,0},{8,15},{9,10},{10,... | collective-permute-start | bytes 294920 | tf_op jit(solution)/shard_map/ppermute | solution.py:38
  132.3 3.1 %collective-permute-done.40 = bf16[2,32,768]{2,1,0:T(8,128)(2,1)S(1)} collective-permute-done((bf16[2,32,768]{2,1,0:T(8,128)(2,1)S(1)}, bf16[2,32,768]{2,1,0:T(8,128)(2,1)S(1)}, u32[]{:S(2)}, u32[]{:S(2)}) %collective-permute-start.40) | collective-permute-done | bytes 98336 | tf_op jit(solution)/shard_map/ppermute | solution.py:38
  135.4 2.0 %collective-permute-start.41 = (bf16[2,32,768]{2,1,0:T(8,128)(2,1)S(1)}, bf16[2,32,768]{2,1,0:T(8,128)(2,1)S(1)}, u32[]{:S(2)}, u32[]{:S(2)}) collective-permute-start(bf16[2,32,768]{2,1,0:T(8,128)(2,1)S(1)} %add_convert_fusion.9), channel_id=1, source_target_pairs={{0,3},{1,6},{2,5},{3,0},{4,7},{5,2},{6,1},{7,4},{8,11},{9,14},{10,... | collective-permute-start | bytes 294920 | tf_op jit(solution)/shard_map/ppermute | solution.py:42
  137.3 6.0 %collective-permute-done.41 = bf16[2,32,768]{2,1,0:T(8,128)(2,1)S(1)} collective-permute-done((bf16[2,32,768]{2,1,0:T(8,128)(2,1)S(1)}, bf16[2,32,768]{2,1,0:T(8,128)(2,1)S(1)}, u32[]{:S(2)}, u32[]{:S(2)}) %collective-permute-start.41) | collective-permute-done | bytes 98336 | tf_op jit(solution)/shard_map/ppermute | solution.py:42
  143.4 3.2 %collective-permute-start.42 = (bf16[2,32,768]{2,1,0:T(8,128)(2,1)S(1)}, bf16[2,32,768]{2,1,0:T(8,128)(2,1)S(1)}, u32[]{:S(2)}, u32[]{:S(2)}) collective-permute-start(bf16[2,32,768]{2,1,0:T(8,128)(2,1)S(1)} %add_convert_fusion.8.mine), channel_id=1, source_target_pairs={{0,7},{1,2},{2,1},{3,4},{4,3},{5,6},{6,5},{7,0},{8,15},{9,10},{10,... | collective-permute-start | bytes 294920 | tf_op jit(solution)/shard_map/ppermute | solution.py:38
  146.6 2.7 %collective-permute-done.42.near = bf16[2,32,768]{2,1,0:T(8,128)(2,1)S(1)} collective-permute-done((bf16[2,32,768]{2,1,0:T(8,128)(2,1)S(1)}, bf16[2,32,768]{2,1,0:T(8,128)(2,1)S(1)}, u32[]{:S(2)}, u32[]{:S(2)}) %collective-permute-start.42) | collective-permute-done | bytes 98336 | tf_op jit(solution)/shard_map/ppermute | solution.py:38
  151.2 2.7 %collective-permute-done.44.beyond = bf16[2,32,768]{2,1,0:T(8,128)(2,1)S(1)} collective-permute-done((bf16[2,32,768]{2,1,0:T(8,128)(2,1)S(1)}, bf16[2,32,768]{2,1,0:T(8,128)(2,1)S(1)}, u32[]{:S(2)}, u32[]{:S(2)}) %collective-permute-start.44) | collective-permute-done | bytes 98336 | tf_op jit(solution)/shard_map/ppermute | solution.py:34
  (154 shorter events, 39.4 us)
Async XLA Ops:
  6.2 16.4 %collective-permute-start.2 = (bf16[256,512]{1,0:T(8,128)(2,1)}, bf16[256,512]{1,0:T(8,128)(2,1)S(1)}, u32[]{:S(2)}, u32[]{:S(2)}) collective-permute-start(bf16[256,512]{1,0:T(8,128)(2,1)} %get-tuple-element.27), channel_id=1, source_target_pairs={{0,1},{1,0},{2,3},{3,2},{4,5},{5,4},{6,7},{7,6},{8,9},{9,8},{10,11... | collective-permute-start | bytes 786440 | tf_op jit(solution)/shard_map/ppermute | solution.py:34
  8.5 11.1 %collective-permute-start.8 = (bf16[128,768]{1,0:T(8,128)(2,1)S(1)}, bf16[128,768]{1,0:T(8,128)(2,1)S(1)}, u32[]{:S(2)}, u32[]{:S(2)}) collective-permute-start(bf16[128,768]{1,0:T(8,128)(2,1)S(1)} %get-tuple-element.59), channel_id=1, source_target_pairs={{0,32},{8,136},{16,48},{24,152},{32,0},{40,168},{48,16},{56,184},{... | collective-permute-start | bytes 589832 | tf_op jit(solution)/shard_map/ppermute | solution.py:30
  10.0 7.9 %collective-permute-start.5 = (bf16[128,768]{1,0:T(8,128)(2,1)S(1)}, bf16[128,768]{1,0:T(8,128)(2,1)S(1)}, u32[]{:S(2)}, u32[]{:S(2)}) collective-permute-start(bf16[128,768]{1,0:T(8,128)(2,1)S(1)} %get-tuple-element.59), channel_id=1, source_target_pairs={{0,48},{8,200},{16,0},{24,216},{32,16},{40,232},{48,32},{56,248},{... | collective-permute-start | bytes 589832 | tf_op jit(solution)/shard_map/ppermute | solution.py:30
  11.9 30.1 %collective-permute-start.1 = (bf16[256,2048]{1,0:T(8,128)(2,1)S(1)}, bf16[256,2048]{1,0:T(8,128)(2,1)S(1)}, u32[]{:S(2)}, u32[]{:S(2)}) collective-permute-start(bf16[256,2048]{1,0:T(8,128)(2,1)S(1)} %fusion.refs_8_.refs_0_.t0), channel_id=1, source_target_pairs={{0,1},{1,0},{2,3},{3,2},{4,5},{5,4},{6,7},{7,6},{8,9},{9,8},{10,11... | collective-permute-start | bytes 3145736 | tf_op jit(solution)/shard_map/ppermute | solution.py:34
  12.3 7.3 %collective-permute-start.9 = (bf16[128,768]{1,0:T(8,128)(2,1)S(1)}, bf16[128,768]{1,0:T(8,128)(2,1)S(1)}, u32[]{:S(2)}, u32[]{:S(2)}) collective-permute-start(bf16[128,768]{1,0:T(8,128)(2,1)S(1)} %get-tuple-element.59), channel_id=1, source_target_pairs={{0,16},{8,72},{16,32},{24,88},{32,48},{40,104},{48,0},{56,120},{64... | collective-permute-start | bytes 589832 | tf_op jit(solution)/shard_map/ppermute | solution.py:30
  17.9 9.1 %collective-permute-start.6 = (bf16[256,768]{1,0:T(8,128)(2,1)S(1)}, bf16[256,768]{1,0:T(8,128)(2,1)S(1)}, u32[]{:S(2)}, u32[]{:S(2)}) collective-permute-start(bf16[256,768]{1,0:T(8,128)(2,1)S(1)} %constant_dynamic-update-slice_fusion.2.refs_0_), channel_id=1, source_target_pairs={{0,64},{8,24},{16,80},{24,40},{32,96},{40,56},{48,112},{56,8},{64,... | collective-permute-start | bytes 1179656 | tf_op jit(solution)/shard_map/ppermute | solution.py:30
  19.6 8.3 %collective-permute-start.10 = (bf16[256,768]{1,0:T(8,128)(2,1)S(1)}, bf16[256,768]{1,0:T(8,128)(2,1)S(1)}, u32[]{:S(2)}, u32[]{:S(2)}) collective-permute-start(bf16[256,768]{1,0:T(8,128)(2,1)S(1)} %constant_dynamic-update-slice_fusion.5.refs_1_), channel_id=1, source_target_pairs={{0,192},{8,56},{16,208},{24,8},{32,224},{40,24},{48,240},{56,40},{... | collective-permute-start | bytes 1179656 | tf_op jit(solution)/shard_map/ppermute | solution.py:30
  22.7 9.4 %collective-permute-start.12 = (bf16[256,768]{1,0:T(8,128)(2,1)S(1)}, bf16[256,768]{1,0:T(8,128)(2,1)S(1)}, u32[]{:S(2)}, u32[]{:S(2)}) collective-permute-start(bf16[256,768]{1,0:T(8,128)(2,1)S(1)} %constant_dynamic-update-slice_fusion.2.refs_0_), channel_id=1, source_target_pairs={{0,192},{8,56},{16,208},{24,8},{32,224},{40,24},{48,240},{56,40},{... | collective-permute-start | bytes 1179656 | tf_op jit(solution)/shard_map/ppermute | solution.py:30
  24.4 9.0 %collective-permute-start.13 = (bf16[256,768]{1,0:T(8,128)(2,1)S(1)}, bf16[256,768]{1,0:T(8,128)(2,1)S(1)}, u32[]{:S(2)}, u32[]{:S(2)}) collective-permute-start(bf16[256,768]{1,0:T(8,128)(2,1)S(1)} %constant_dynamic-update-slice_fusion.5.refs_1_), channel_id=1, source_target_pairs={{0,64},{8,24},{16,80},{24,40},{32,96},{40,56},{48,112},{56,8},{64,... | collective-permute-start | bytes 1179656 | tf_op jit(solution)/shard_map/ppermute | solution.py:30
  26.9 10.7 %collective-permute-start.7 = (bf16[256,768]{1,0:T(8,128)(2,1)S(1)}, bf16[256,768]{1,0:T(8,128)(2,1)S(1)}, u32[]{:S(2)}, u32[]{:S(2)}) collective-permute-start(bf16[256,768]{1,0:T(8,128)(2,1)S(1)} %collective-permute-done.6.refs_4_), channel_id=1, source_target_pairs={{0,64},{8,24},{16,80},{24,40},{32,96},{40,56},{48,112},{56,8},{64,... | collective-permute-start | bytes 1179656 | tf_op jit(solution)/shard_map/ppermute | solution.py:30
  27.8 11.7 %collective-permute-start.11 = (bf16[256,768]{1,0:T(8,128)(2,1)S(1)}, bf16[256,768]{1,0:T(8,128)(2,1)S(1)}, u32[]{:S(2)}, u32[]{:S(2)}) collective-permute-start(bf16[256,768]{1,0:T(8,128)(2,1)S(1)} %collective-permute-done.10.refs_3_), channel_id=1, source_target_pairs={{0,192},{8,56},{16,208},{24,8},{32,224},{40,24},{48,240},{56,40},{... | collective-permute-start | bytes 1179656 | tf_op jit(solution)/shard_map/ppermute | solution.py:30
  32.1 13.9 %collective-permute-start.14 = (bf16[256,2048]{1,0:T(8,128)(2,1)S(1)}, bf16[256,2048]{1,0:T(8,128)(2,1)S(1)}, u32[]{:S(2)}, u32[]{:S(2)}) collective-permute-start(bf16[256,2048]{1,0:T(8,128)(2,1)S(1)} %fusion.refs_8_.refs_0_.t0), channel_id=1, source_target_pairs={{0,8},{8,0},{1,9},{9,1},{2,10},{10,2},{3,11},{11,3},{4,12},{12,4},... | collective-permute-start | bytes 3145736 | tf_op jit(solution)/shard_map/ppermute | solution.py:34
  58.4 7.9 %collective-permute-start.24 = (bf16[2,2,128,128]{3,2,1,0:T(8,128)(2,1)S(1)}, bf16[2,2,128,128]{3,2,1,0:T(8,128)(2,1)S(1)}, u32[]{:S(2)}, u32[]{:S(2)}) collective-permute-start(bf16[2,2,128,128]{3,2,1,0:T(8,128)(2,1)S(1)} %get-tuple-element.37), channel_id=1, source_target_pairs={{0,64},{64,0},{128,192},{192,128},{1,65},{65,1},{129,193},{193,129... | collective-permute-start | bytes 393224 | tf_op jit(solution)/shard_map/ppermute | solution.py:34
  58.5 9.8 %collective-permute-start.26 = (bf16[2,2,128,128]{3,2,1,0:T(8,128)(2,1)S(1)}, bf16[2,2,128,128]{3,2,1,0:T(8,128)(2,1)S(1)}, u32[]{:S(2)}, u32[]{:S(2)}) collective-permute-start(bf16[2,2,128,128]{3,2,1,0:T(8,128)(2,1)S(1)} %get-tuple-element.38), channel_id=1, source_target_pairs={{0,192},{64,128},{128,64},{192,0},{1,193},{65,129},{129,65},{193,1... | collective-permute-start | bytes 393224 | tf_op jit(solution)/shard_map/ppermute | solution.py:34
  59.5 8.7 %collective-permute-start.25 = (bf16[2,2,128,128]{3,2,1,0:T(8,128)(2,1)S(1)}, bf16[2,2,128,128]{3,2,1,0:T(8,128)(2,1)S(1)}, u32[]{:S(2)}, u32[]{:S(2)}) collective-permute-start(bf16[2,2,128,128]{3,2,1,0:T(8,128)(2,1)S(1)} %get-tuple-element.38), channel_id=1, source_target_pairs={{0,128},{64,192},{128,0},{192,64},{1,129},{65,193},{129,1},{193,65... | collective-permute-start | bytes 393224 | tf_op jit(solution)/shard_map/ppermute | solution.py:34
  62.6 9.6 %collective-permute-start.20 = (bf16[2,2,128,128]{3,2,1,0:T(8,128)(2,1)S(1)}, bf16[2,2,128,128]{3,2,1,0:T(8,128)(2,1)S(1)}, u32[]{:S(2)}, u32[]{:S(2)}) collective-permute-start(bf16[2,2,128,128]{3,2,1,0:T(8,128)(2,1)S(1)} %get-tuple-element.36), channel_id=1, source_target_pairs={{0,48},{16,32},{32,16},{48,0},{1,49},{17,33},{33,17},{49,1},{2,50}... | collective-permute-start | bytes 393224 | tf_op jit(solution)/shard_map/ppermute | solution.py:34
  66.2 7.6 %collective-permute-start.19 = (bf16[2,2,128,128]{3,2,1,0:T(8,128)(2,1)S(1)}, bf16[2,2,128,128]{3,2,1,0:T(8,128)(2,1)S(1)}, u32[]{:S(2)}, u32[]{:S(2)}) collective-permute-start(bf16[2,2,128,128]{3,2,1,0:T(8,128)(2,1)S(1)} %get-tuple-element.36), channel_id=1, source_target_pairs={{0,32},{16,48},{32,0},{48,16},{1,33},{17,49},{33,1},{49,17},{2,34}... | collective-permute-start | bytes 393224 | tf_op jit(solution)/shard_map/ppermute | solution.py:34
  66.2 7.6 %collective-permute-start.18 = (bf16[2,2,128,128]{3,2,1,0:T(8,128)(2,1)S(1)}, bf16[2,2,128,128]{3,2,1,0:T(8,128)(2,1)S(1)}, u32[]{:S(2)}, u32[]{:S(2)}) collective-permute-start(bf16[2,2,128,128]{3,2,1,0:T(8,128)(2,1)S(1)} %get-tuple-element.36), channel_id=1, source_target_pairs={{0,16},{16,0},{32,48},{48,32},{1,17},{17,1},{33,49},{49,33},{2,18}... | collective-permute-start | bytes 393224 | tf_op jit(solution)/shard_map/ppermute | solution.py:34
  68.4 16.1 %collective-permute-start.29 = (bf16[2,2,128,128]{3,2,1,0:T(8,128)(2,1)S(1)}, bf16[2,2,128,128]{3,2,1,0:T(8,128)(2,1)S(1)}, u32[]{:S(2)}, u32[]{:S(2)}) collective-permute-start(bf16[2,2,128,128]{3,2,1,0:T(8,128)(2,1)S(1)} %get-tuple-element.52), channel_id=1, source_target_pairs={{0,48},{16,32},{32,16},{48,0},{1,49},{17,33},{33,17},{49,1},{2,50}... | collective-permute-start | bytes 393224 | tf_op jit(solution)/shard_map/ppermute | solution.py:34
  72.1 12.3 %collective-permute-start.28 = (bf16[2,2,128,128]{3,2,1,0:T(8,128)(2,1)S(1)}, bf16[2,2,128,128]{3,2,1,0:T(8,128)(2,1)S(1)}, u32[]{:S(2)}, u32[]{:S(2)}) collective-permute-start(bf16[2,2,128,128]{3,2,1,0:T(8,128)(2,1)S(1)} %get-tuple-element.52), channel_id=1, source_target_pairs={{0,32},{16,48},{32,0},{48,16},{1,33},{17,49},{33,1},{49,17},{2,34}... | collective-permute-start | bytes 393224 | tf_op jit(solution)/shard_map/ppermute | solution.py:34
  73.9 10.6 %collective-permute-start.23 = (bf16[2,2,128,128]{3,2,1,0:T(8,128)(2,1)S(1)}, bf16[2,2,128,128]{3,2,1,0:T(8,128)(2,1)S(1)}, u32[]{:S(2)}, u32[]{:S(2)}) collective-permute-start(bf16[2,2,128,128]{3,2,1,0:T(8,128)(2,1)S(1)} %add_convert_fusion.7), channel_id=1, source_target_pairs={{0,192},{64,128},{128,64},{192,0},{1,193},{65,129},{129,65},{193,1... | collective-permute-start | bytes 393224 | tf_op jit(solution)/shard_map/ppermute | solution.py:34
  74.9 9.5 %collective-permute-start.22 = (bf16[2,2,128,128]{3,2,1,0:T(8,128)(2,1)S(1)}, bf16[2,2,128,128]{3,2,1,0:T(8,128)(2,1)S(1)}, u32[]{:S(2)}, u32[]{:S(2)}) collective-permute-start(bf16[2,2,128,128]{3,2,1,0:T(8,128)(2,1)S(1)} %add_convert_fusion.7), channel_id=1, source_target_pairs={{0,128},{64,192},{128,0},{192,64},{1,129},{65,193},{129,1},{193,65... | collective-permute-start | bytes 393224 | tf_op jit(solution)/shard_map/ppermute | solution.py:34
  88.6 8.1 %collective-permute-start.33 = (bf16[2,128,768]{2,1,0:T(8,128)(2,1)S(1)}, bf16[2,128,768]{2,1,0:T(8,128)(2,1)S(1)}, u32[]{:S(2)}, u32[]{:S(2)}) collective-permute-start(bf16[2,128,768]{2,1,0:T(8,128)(2,1)S(1)} %get-tuple-element.46), channel_id=1, source_target_pairs={{0,192},{8,56},{16,208},{24,8},{32,224},{40,24},{48,240},{56,40},{... | collective-permute-start | bytes 1179656 | tf_op jit(solution)/shard_map/ppermute | solution.py:30
  90.1 9.2 %collective-permute-start.31 = (bf16[2,128,768]{2,1,0:T(8,128)(2,1)S(1)}, bf16[2,128,768]{2,1,0:T(8,128)(2,1)S(1)}, u32[]{:S(2)}, u32[]{:S(2)}) collective-permute-start(bf16[2,128,768]{2,1,0:T(8,128)(2,1)S(1)} %get-tuple-element.44), channel_id=1, source_target_pairs={{0,64},{8,24},{16,80},{24,40},{32,96},{40,56},{48,112},{56,8},{64,... | collective-permute-start | bytes 1179656 | tf_op jit(solution)/shard_map/ppermute | solution.py:30
  96.8 12.1 %collective-permute-start.34 = (bf16[4,128,768]{2,1,0:T(8,128)(2,1)S(1)}, bf16[4,128,768]{2,1,0:T(8,128)(2,1)S(1)}, u32[]{:S(2)}, u32[]{:S(2)}) collective-permute-start(bf16[4,128,768]{2,1,0:T(8,128)(2,1)S(1)} %pad_maximum_fusion.1), channel_id=1, source_target_pairs={{0,192},{8,56},{16,208},{24,8},{32,224},{40,24},{48,240},{56,40},{... | collective-permute-start | bytes 2359304 | tf_op jit(solution)/shard_map/ppermute | solution.py:30
  99.5 13.3 %collective-permute-start.32 = (bf16[4,128,768]{2,1,0:T(8,128)(2,1)S(1)}, bf16[4,128,768]{2,1,0:T(8,128)(2,1)S(1)}, u32[]{:S(2)}, u32[]{:S(2)}) collective-permute-start(bf16[4,128,768]{2,1,0:T(8,128)(2,1)S(1)} %pad_maximum_fusion), channel_id=1, source_target_pairs={{0,64},{8,24},{16,80},{24,40},{32,96},{40,56},{48,112},{56,8},{64,... | collective-permute-start | bytes 2359304 | tf_op jit(solution)/shard_map/ppermute | solution.py:30
  99.7 9.1 %collective-permute-start.35 = (bf16[2,256,256]{2,1,0:T(8,128)(2,1)S(1)}, bf16[2,256,256]{2,1,0:T(8,128)(2,1)S(1)}, u32[]{:S(2)}, u32[]{:S(2)}) collective-permute-start(bf16[2,256,256]{2,1,0:T(8,128)(2,1)S(1)} %pad_maximum_fusion.2), channel_id=1, source_target_pairs={{0,1},{1,0},{2,3},{3,2},{4,5},{5,4},{6,7},{7,6},{8,9},{9,8},{10,11... | collective-permute-start | bytes 786440 | tf_op jit(solution)/shard_map/ppermute | solution.py:34
  114.4 8.2 %collective-permute-start.36 = (bf16[128,768]{1,0:T(8,128)(2,1)S(1)}, bf16[128,768]{1,0:T(8,128)(2,1)S(1)}, u32[]{:S(2)}, u32[]{:S(2)}) collective-permute-start(bf16[128,768]{1,0:T(8,128)(2,1)S(1)} %get-tuple-element.49), channel_id=1, source_target_pairs={{0,16},{8,72},{16,32},{24,88},{32,48},{40,104},{48,0},{56,120},{64... | collective-permute-start | bytes 589832 | tf_op jit(solution)/shard_map/ppermute | solution.py:30
  117.3 7.3 %collective-permute-start.37 = (bf16[128,768]{1,0:T(8,128)(2,1)S(1)}, bf16[128,768]{1,0:T(8,128)(2,1)S(1)}, u32[]{:S(2)}, u32[]{:S(2)}) collective-permute-start(bf16[128,768]{1,0:T(8,128)(2,1)S(1)} %get-tuple-element.50), channel_id=1, source_target_pairs={{0,32},{8,136},{16,48},{24,152},{32,0},{40,168},{48,16},{56,184},{... | collective-permute-start | bytes 589832 | tf_op jit(solution)/shard_map/ppermute | solution.py:30
  117.6 9.0 %collective-permute-start.38 = (bf16[128,768]{1,0:T(8,128)(2,1)S(1)}, bf16[128,768]{1,0:T(8,128)(2,1)S(1)}, u32[]{:S(2)}, u32[]{:S(2)}) collective-permute-start(bf16[128,768]{1,0:T(8,128)(2,1)S(1)} %get-tuple-element.51), channel_id=1, source_target_pairs={{0,48},{8,200},{16,0},{24,216},{32,16},{40,232},{48,32},{56,248},{... | collective-permute-start | bytes 589832 | tf_op jit(solution)/shard_map/ppermute | solution.py:30
  128.1 7.3 %collective-permute-start.40 = (bf16[2,32,768]{2,1,0:T(8,128)(2,1)S(1)}, bf16[2,32,768]{2,1,0:T(8,128)(2,1)S(1)}, u32[]{:S(2)}, u32[]{:S(2)}) collective-permute-start(bf16[2,32,768]{2,1,0:T(8,128)(2,1)S(1)} %pad_maximum_fusion.3), channel_id=1, source_target_pairs={{0,7},{1,2},{2,1},{3,4},{4,3},{5,6},{6,5},{7,0},{8,15},{9,10},{10,... | collective-permute-start | bytes 294920 | tf_op jit(solution)/shard_map/ppermute | solution.py:38
  135.4 7.9 %collective-permute-start.41 = (bf16[2,32,768]{2,1,0:T(8,128)(2,1)S(1)}, bf16[2,32,768]{2,1,0:T(8,128)(2,1)S(1)}, u32[]{:S(2)}, u32[]{:S(2)}) collective-permute-start(bf16[2,32,768]{2,1,0:T(8,128)(2,1)S(1)} %add_convert_fusion.9), channel_id=1, source_target_pairs={{0,3},{1,6},{2,5},{3,0},{4,7},{5,2},{6,1},{7,4},{8,11},{9,14},{10,... | collective-permute-start | bytes 294920 | tf_op jit(solution)/shard_map/ppermute | solution.py:42
  (39 other events, 426.0 us)

commit v4 on v3

--- a/solution.py
+++ b/solution.py
@@ -107,13 +107,11 @@
     to_z[:, 256:] = cot[:, columns(1, 1)]
 
 
-def project_kernel(pos, idx, table, c0, c1, c2, c3, *refs):
+def project_kernel(pos, idx, table, t0, t1, t2, t3, c0, c1, c2, c3, *refs):
+    toks = (t0, t1, t2, t3)
     parts = (refs[0:2], refs[2:4], refs[6:8], refs[4:6])
-    qkv, cots, s1, x0, g1, m2, m3, m4, m5, w, toks, sems = refs[12:]
+    qkv, cots, s1, x0, g1, m2, m3, m4, m5, w = refs[8:]
     y, x, core = pos[0], pos[1], pos[2]
-    copies = [pltpu.make_async_copy(refs[8 + b], toks.at[b], sems.at[b]) for b in range(4)]
-    for copy in copies:
-        copy.start()
     for slot in range(4):
         for dist in range(4):
             yy = (y + dist + core * (slot - dist)) & 3
@@ -125,13 +123,11 @@
     for blk, src in enumerate((c0, c1, c2, c3)):
         cots[blk] = src[...]
 
-    for blk in range(4):
-        copies[blk].wait()
-
-        @pl.loop(0, 3)
-        def _(part, blk=blk):
-            cols = pl.ds(pl.multiple_of(part * 256, 256), 256)
-            qkv[blk, :, cols] = dot(toks[blk], w[:, cols], 1, 0).astype(BF)
+    @pl.loop(0, 3)
+    def _(part):
+        cols = pl.ds(pl.multiple_of(part * 256, 256), 256)
+        for blk in range(4):
+            qkv[blk, :, cols] = dot(toks[blk][...], w[:, cols], 1, 0).astype(BF)
 
     @pl.loop(0, 4)
     def _(step):
@@ -345,7 +341,7 @@
     tile = (HEAD, HEAD)
     qkv, cots, s1, x0, g1, m2, m3, m4, m5 = call(
         project_kernel,
-        scalars + [c_own, c_near, c_core, c_across] + gathered + toks,
+        scalars + toks + [c_own, c_near, c_core, c_across] + gathered,
         3,
         [
             ((4, BLOCK, COLS), BF),
@@ -358,13 +354,8 @@
             ((2, 2) + tile, BF),
             ((2, 2) + tile, BF),
         ],
-        scratch=[
-            pltpu.VMEM((D, COLS), BF),
-            pltpu.VMEM((4, BLOCK, D), BF),
-            pltpu.SemaphoreType.DMA((4,)),
-        ],
+        scratch=[pltpu.VMEM((D, COLS), BF)],
         grant=52,
-        n_any=4,
         flops=2 * 1024 * D * COLS,
         nbytes=10 * MIB,
     )

time: 156 us -> 154 us (0.987)
  no operation moved by 1% of the time
where the time goes in v4:
time: 154 us
  starting transfers between devices  55.1 us (36%)
  waiting for transfers between devices  53.8 us (35%)
  Pallas kernels  29.2 us (19%)
  local copies, waits for them, and re-layouts  8.05 us (5%)
  between operations  5.08 us (3%)
  other arithmetic  2.39 us (2%)
    pallas_call x8, Pallas kernels, call(): pl.pallas_call(kernel, out_shape=[jax.ShapeDtypeStruct(*out) for out in o...  29.2 us
    ppermute x16, starting transfers between devices, ring(): return lax.ppermute(value, ('y', 'x', 'core'), pairs)  25.8 us
    ppermute x16, waiting for transfers between devices, ring(): return lax.ppermute(value, ('y', 'x', 'core'), pairs)  23.4 us
    ppermute x26, starting transfers between devices, swap(): return lax.ppermute(value, axis, [(i, i ^ mask) for i in range(size)])  20.1 us
    ppermute x26, waiting for transfers between devices, swap(): return lax.ppermute(value, axis, [(i, i ^ mask) for i in range(size)])  18.4 us
    ppermute x2, starting transfers between devices, same_set_neighbour(): lax.ppermute(value, 'dp', [(z, (z + 1 if z % 2 else z - 1) % 8) for z in...  7.21 us
    ppermute x1, waiting for transfers between devices, same_set_far(): lax.ppermute(value, 'dp', [(z, ((7 if SETS >> z & 1 else 3) - z) % 8) for...  6 us
    ppermute x2, waiting for transfers between devices, same_set_neighbour(): lax.ppermute(value, 'dp', [(z, (z + 1 if z % 2 else z - 1) % 8) for z in...  5.97 us
  transfers between devices with their start and end apart: 45, of which 21 were waited for; matrix products, arithmetic and copies ran while one was open for 5% of the time, Pallas kernels for 8%

profile of v4, /device:TPU:6, one launch (start us, length us, event | category | flops | bytes accessed | tf_op | source)
XLA Modules:
  0.0 153.6 jit_solution(10397565417272906516)
XLA Ops:
  1.5 1.9 %collective-permute-start = (s32[1,12]{1,0:T(1,128)S(1)}, s32[1,12]{1,0:T(1,128)S(1)}, u32[]{:S(2)}, u32[]{:S(2)}) collective-permute-start(s32[1,12]{1,0:T(1,128)S(1)} %reshape.24), channel_id=1, source_target_pairs={{0,1},{1,0},{2,3},{3,2},{4,5},{5,4},{6,7},{7,6},{8,9},{9,8},{10,11... | collective-permute-start | bytes 152 | tf_op jit(solution)/shard_map/ppermute | solution.py:34
  4.0 2.1 %shard_map.68 = (bf16[64,768]{1,0:T(8,128)(2,1)}, bf16[64,768]{1,0:T(8,128)(2,1)}, bf16[256,256]{1,0:T(8,128)(2,1)}, bf16[256,256]{1,0:T(8,128)(2,1)}, bf16[256,512]{1,0:T(8,128)(2,1)}) custom-call(s32[7]{0:T(128)} %stack.43.pos, bf16[3,64,1024]{2,1,0:T(8,128)(2,1)} %bitcast.23, bf16[256,1024]{1,0:T(8,128)(2,1)} %bitcast.22), custom_call_target="tpu_custom_call" | custom-call | bytes 2097152 | tf_op jit(solution)/shard_map/pallas_call | solution.py:65
  12.3 3.2 %collective-permute-start.9 = (bf16[128,768]{1,0:T(8,128)(2,1)S(1)}, bf16[128,768]{1,0:T(8,128)(2,1)S(1)}, u32[]{:S(2)}, u32[]{:S(2)}) collective-permute-start(bf16[128,768]{1,0:T(8,128)(2,1)S(1)} %get-tuple-element.59), channel_id=1, source_target_pairs={{0,16},{8,72},{16,32},{24,88},{32,48},{40,104},{48,0},{56,120},{64... | collective-permute-start | bytes 589832 | tf_op jit(solution)/shard_map/ppermute | solution.py:30
  15.5 2.3 %collective-permute-done.5 = bf16[128,768]{1,0:T(8,128)(2,1)S(1)} collective-permute-done((bf16[128,768]{1,0:T(8,128)(2,1)S(1)}, bf16[128,768]{1,0:T(8,128)(2,1)S(1)}, u32[]{:S(2)}, u32[]{:S(2)}) %collective-permute-start.5) | collective-permute-done | bytes 196640 | tf_op jit(solution)/shard_map/ppermute | solution.py:30
  19.6 3.0 %collective-permute-start.10 = (bf16[256,768]{1,0:T(8,128)(2,1)S(1)}, bf16[256,768]{1,0:T(8,128)(2,1)S(1)}, u32[]{:S(2)}, u32[]{:S(2)}) collective-permute-start(bf16[256,768]{1,0:T(8,128)(2,1)S(1)} %constant_dynamic-update-slice_fusion.5.refs_1_), channel_id=1, source_target_pairs={{0,192},{8,56},{16,208},{24,8},{32,224},{40,24},{48,240},{56,40},{... | collective-permute-start | bytes 1179656 | tf_op jit(solution)/shard_map/ppermute | solution.py:30
  24.8 2.1 %collective-permute-done.6.refs_4_ = bf16[256,768]{1,0:T(8,128)(2,1)S(1)} collective-permute-done((bf16[256,768]{1,0:T(8,128)(2,1)S(1)}, bf16[256,768]{1,0:T(8,128)(2,1)S(1)}, u32[]{:S(2)}, u32[]{:S(2)}) %collective-permute-start.6) | collective-permute-done | bytes 393248 | tf_op jit(solution)/shard_map/ppermute | solution.py:30
  27.8 3.7 %collective-permute-start.11 = (bf16[256,768]{1,0:T(8,128)(2,1)S(1)}, bf16[256,768]{1,0:T(8,128)(2,1)S(1)}, u32[]{:S(2)}, u32[]{:S(2)}) collective-permute-start(bf16[256,768]{1,0:T(8,128)(2,1)S(1)} %collective-permute-done.10.refs_3_), channel_id=1, source_target_pairs={{0,192},{8,56},{16,208},{24,8},{32,224},{40,24},{48,240},{56,40},{... | collective-permute-start | bytes 1179656 | tf_op jit(solution)/shard_map/ppermute | solution.py:30
  34.0 3.7 %collective-permute-done.7.refs_6_ = bf16[256,768]{1,0:T(8,128)(2,1)S(1)} collective-permute-done((bf16[256,768]{1,0:T(8,128)(2,1)S(1)}, bf16[256,768]{1,0:T(8,128)(2,1)S(1)}, u32[]{:S(2)}, u32[]{:S(2)}) %collective-permute-start.7) | collective-permute-done | bytes 393248 | tf_op jit(solution)/shard_map/ppermute | solution.py:30
  47.0 9.8 %shard_map.69 = (bf16[4,256,768]{2,1,0:T(8,128)(2,1)}, bf16[4,256,256]{2,1,0:T(8,128)(2,1)}, bf16[4,2,128,128]{3,2,1,0:T(8,128)(2,1)S(1)}, bf16[2,2,128,128]{3,2...) custom-call(s32[7]{0:T(128)S(1)} %copy-done.10, ...), custom_call_target="tpu_custom_call" | custom-call | flops 3221225472 | bytes 10485760 | tf_op jit(solution)/shard_map/pallas_call | solution.py:65
  57.9 3.0 %collective-permute-start.25 = (bf16[2,2,128,128]{3,2,1,0:T(8,128)(2,1)S(1)}, bf16[2,2,128,128]{3,2,1,0:T(8,128)(2,1)S(1)}, u32[]{:S(2)}, u32[]{:S(2)}) collective-permute-start(bf16[2,2,128,128]{3,2,1,0:T(8,128)(2,1)S(1)} %get-tuple-element.38), channel_id=1, source_target_pairs={{0,128},{64,192},{128,0},{192,64},{1,129},{65,193},{129,1},{193,65... | collective-permute-start | bytes 393224 | tf_op jit(solution)/shard_map/ppermute | solution.py:34
  60.9 3.7 %collective-permute-start.20 = (bf16[2,2,128,128]{3,2,1,0:T(8,128)(2,1)S(1)}, bf16[2,2,128,128]{3,2,1,0:T(8,128)(2,1)S(1)}, u32[]{:S(2)}, u32[]{:S(2)}) collective-permute-start(bf16[2,2,128,128]{3,2,1,0:T(8,128)(2,1)S(1)} %get-tuple-element.36), channel_id=1, source_target_pairs={{0,48},{16,32},{32,16},{48,0},{1,49},{17,33},{33,17},{49,1},{2,50}... | collective-permute-start | bytes 393224 | tf_op jit(solution)/shard_map/ppermute | solution.py:34
  66.8 3.8 %collective-permute-start.29 = (bf16[2,2,128,128]{3,2,1,0:T(8,128)(2,1)S(1)}, bf16[2,2,128,128]{3,2,1,0:T(8,128)(2,1)S(1)}, u32[]{:S(2)}, u32[]{:S(2)}) collective-permute-start(bf16[2,2,128,128]{3,2,1,0:T(8,128)(2,1)S(1)} %get-tuple-element.52), channel_id=1, source_target_pairs={{0,48},{16,32},{32,16},{48,0},{1,49},{17,33},{33,17},{49,1},{2,50}... | collective-permute-start | bytes 393224 | tf_op jit(solution)/shard_map/ppermute | solution.py:34
  74.8 2.4 %collective-permute-done.27.refs_16_ = bf16[2,2,128,128]{3,2,1,0:T(8,128)(2,1)S(1)} collective-permute-done((bf16[2,2,128,128]{3,2,1,0:T(8,128)(2,1)S(1)}, bf16[2,2,128,128]{3,2,1,0:T(8,128)(2,1)S(1)}, u32[]{:S(2)}, u32[]{:S(2)}) %collective-permute-start.27) | collective-permute-done | bytes 131104 | tf_op jit(solution)/shard_map/ppermute | solution.py:34
  78.4 4.4 %shard_map.70.refs_6_ = f32[4,256,1024]{2,1,0:T(8,128)S(1)} custom-call(s32[7]{0:T(128)S(1)} %copy-done.10, s32[4,12]{1,0:T(4,128)S(1)} %pad_add_fusion.idx, f32[16,8]{1,0:T(8,128)S(1)} %copy.9.table, bf16[4,256,768]{2,1,0:T(8,128)(2,1)S(1)} %copy-done.6, bf16[4,256,256]{2,1,0:T(8,128)(2,1)S(1)} %copy-done.7), custom_call_target="tpu_custom_call" | custom-call | flops 805306368 | bytes 8388608 | tf_op jit(solution)/shard_map/pallas_call | solution.py:65
  82.9 3.9 %shard_map.71 = (bf16[4,256,256]{2,1,0:T(8,128)(2,1)S(1)}, bf16[4,256,768]{2,1,0:T(8,128)(2,1)S(1)}, bf16[2,128,768]{2,1,0:T(8,128)(2,1)S(1)}, bf16[2,128,768]{2,1,0:T(8,128)(2,1)S(1)}) custom-call(s32[7]{0:T(128)S(1)} %copy-done.10, s32[4,12]{1,0:T(4,128)S(1)} %pad_add_fusion.idx, f32[16,8]{1,0:T(8,128)S(1)} %copy.9.table, bf16[256,2048]{1,0:T(8,128)(2,1)S(1)} %copy-done.1, ...), custom_call_target="tpu_custom_call" | custom-call | flops 1610612736 | bytes 12582912 | tf_op jit(solution)/shard_map/pallas_call | solution.py:65
  89.2 3.3 %shard_map.73 = (bf16[4,128,768]{2,1,0:T(8,128)(2,1)S(1)}, bf16[4,128,768]{2,1,0:T(8,128)(2,1)S(1)}) custom-call(s32[7]{0:T(128)S(1)} %copy-done.10, bf16[256,2048]{1,0:T(8,128)(2,1)S(1)} %copy-done.1, bf16[256,2048]{1,0:T(8,128)(2,1)S(1)} %copy-done.3, bf16[256,2048]{1,0:T(8,128)(2,1)S(1)} %copy-done.5, ...), custom_call_target="tpu_custom_call" | custom-call | flops 1610612736 | bytes 9437184 | tf_op jit(solution)/shard_map/pallas_call | solution.py:65
  92.7 2.1 %collective-permute-done.33 = bf16[2,128,768]{2,1,0:T(8,128)(2,1)S(1)} collective-permute-done((bf16[2,128,768]{2,1,0:T(8,128)(2,1)S(1)}, bf16[2,128,768]{2,1,0:T(8,128)(2,1)S(1)}, u32[]{:S(2)}, u32[]{:S(2)}) %collective-permute-start.33) | collective-permute-done | bytes 393248 | tf_op jit(solution)/shard_map/ppermute | solution.py:30
  95.0 2.5 %collective-permute-start.34 = (bf16[4,128,768]{2,1,0:T(8,128)(2,1)S(1)}, bf16[4,128,768]{2,1,0:T(8,128)(2,1)S(1)}, u32[]{:S(2)}, u32[]{:S(2)}) collective-permute-start(bf16[4,128,768]{2,1,0:T(8,128)(2,1)S(1)} %pad_maximum_fusion.1), channel_id=1, source_target_pairs={{0,192},{8,56},{16,208},{24,8},{32,224},{40,24},{48,240},{56,40},{... | collective-permute-start | bytes 2359304 | tf_op jit(solution)/shard_map/ppermute | solution.py:30
  98.0 2.5 %shard_map.72.own = bf16[4,128,768]{2,1,0:T(8,128)(2,1)S(1)} custom-call(s32[7]{0:T(128)S(1)} %copy-done.10, bf16[256,2048]{1,0:T(8,128)(2,1)S(1)} %copy-done.1, bf16[256,2048]{1,0:T(8,128)(2,1)S(1)} %copy-done.3, bf16[256,2048]{1,0:T(8,128)(2,1)S(1)} %copy-done.5, bf16[256,2048]{1,0:T(8,128)(2,1)} %collective-permute-done.15.t3.refs_3_, ...), custom_call_target="tpu_custom_call" | custom-call | flops 402653184 | bytes 9437184 | tf_op jit(solution)/shard_map/pallas_call | solution.py:65
  100.5 6.6 %collective-permute-done.35.from_z = bf16[2,256,256]{2,1,0:T(8,128)(2,1)S(1)} collective-permute-done((bf16[2,256,256]{2,1,0:T(8,128)(2,1)S(1)}, bf16[2,256,256]{2,1,0:T(8,128)(2,1)S(1)}, u32[]{:S(2)}, u32[]{:S(2)}) %collective-permute-start.35) | collective-permute-done | bytes 262176 | tf_op jit(solution)/shard_map/ppermute | solution.py:34
  107.1 3.9 %collective-permute-done.32.r1 = bf16[4,128,768]{2,1,0:T(8,128)(2,1)S(1)} collective-permute-done((bf16[4,128,768]{2,1,0:T(8,128)(2,1)S(1)}, bf16[4,128,768]{2,1,0:T(8,128)(2,1)S(1)}, u32[]{:S(2)}, u32[]{:S(2)}) %collective-permute-start.32) | collective-permute-done | bytes 786464 | tf_op jit(solution)/shard_map/ppermute | solution.py:30
  112.6 2.9 %collective-permute-start.36 = (bf16[128,768]{1,0:T(8,128)(2,1)S(1)}, bf16[128,768]{1,0:T(8,128)(2,1)S(1)}, u32[]{:S(2)}, u32[]{:S(2)}) collective-permute-start(bf16[128,768]{1,0:T(8,128)(2,1)S(1)} %get-tuple-element.49), channel_id=1, source_target_pairs={{0,16},{8,72},{16,32},{24,88},{32,48},{40,104},{48,0},{56,120},{64... | collective-permute-start | bytes 589832 | tf_op jit(solution)/shard_map/ppermute | solution.py:30
  116.3 4.4 %collective-permute-done.36 = bf16[128,768]{1,0:T(8,128)(2,1)S(1)} collective-permute-done((bf16[128,768]{1,0:T(8,128)(2,1)S(1)}, bf16[128,768]{1,0:T(8,128)(2,1)S(1)}, u32[]{:S(2)}, u32[]{:S(2)}) %collective-permute-start.36) | collective-permute-done | bytes 196640 | tf_op jit(solution)/shard_map/ppermute | solution.py:30
  120.7 2.0 %collective-permute-done.37 = bf16[128,768]{1,0:T(8,128)(2,1)S(1)} collective-permute-done((bf16[128,768]{1,0:T(8,128)(2,1)S(1)}, bf16[128,768]{1,0:T(8,128)(2,1)S(1)}, u32[]{:S(2)}, u32[]{:S(2)}) %collective-permute-start.37) | collective-permute-done | bytes 196640 | tf_op jit(solution)/shard_map/ppermute | solution.py:30
  122.7 2.0 %collective-permute-done.38 = bf16[128,768]{1,0:T(8,128)(2,1)S(1)} collective-permute-done((bf16[128,768]{1,0:T(8,128)(2,1)S(1)}, bf16[128,768]{1,0:T(8,128)(2,1)S(1)}, u32[]{:S(2)}, u32[]{:S(2)}) %collective-permute-start.38) | collective-permute-done | bytes 196640 | tf_op jit(solution)/shard_map/ppermute | solution.py:30
  126.2 4.2 %collective-permute-start.40 = (bf16[2,32,768]{2,1,0:T(8,128)(2,1)S(1)}, bf16[2,32,768]{2,1,0:T(8,128)(2,1)S(1)}, u32[]{:S(2)}, u32[]{:S(2)}) collective-permute-start(bf16[2,32,768]{2,1,0:T(8,128)(2,1)S(1)} %pad_maximum_fusion.3), channel_id=1, source_target_pairs={{0,7},{1,2},{2,1},{3,4},{4,3},{5,6},{6,5},{7,0},{8,15},{9,10},{10,... | collective-permute-start | bytes 294920 | tf_op jit(solution)/shard_map/ppermute | solution.py:38
  130.4 3.1 %collective-permute-done.40 = bf16[2,32,768]{2,1,0:T(8,128)(2,1)S(1)} collective-permute-done((bf16[2,32,768]{2,1,0:T(8,128)(2,1)S(1)}, bf16[2,32,768]{2,1,0:T(8,128)(2,1)S(1)}, u32[]{:S(2)}, u32[]{:S(2)}) %collective-permute-start.40) | collective-permute-done | bytes 98336 | tf_op jit(solution)/shard_map/ppermute | solution.py:38
  133.5 2.0 %collective-permute-start.41 = (bf16[2,32,768]{2,1,0:T(8,128)(2,1)S(1)}, bf16[2,32,768]{2,1,0:T(8,128)(2,1)S(1)}, u32[]{:S(2)}, u32[]{:S(2)}) collective-permute-start(bf16[2,32,768]{2,1,0:T(8,128)(2,1)S(1)} %add_convert_fusion.9), channel_id=1, source_target_pairs={{0,3},{1,6},{2,5},{3,0},{4,7},{5,2},{6,1},{7,4},{8,11},{9,14},{10,... | collective-permute-start | bytes 294920 | tf_op jit(solution)/shard_map/ppermute | solution.py:42
  135.5 6.0 %collective-permute-done.41 = bf16[2,32,768]{2,1,0:T(8,128)(2,1)S(1)} collective-permute-done((bf16[2,32,768]{2,1,0:T(8,128)(2,1)S(1)}, bf16[2,32,768]{2,1,0:T(8,128)(2,1)S(1)}, u32[]{:S(2)}, u32[]{:S(2)}) %collective-permute-start.41) | collective-permute-done | bytes 98336 | tf_op jit(solution)/shard_map/ppermute | solution.py:42
  141.6 3.0 %collective-permute-start.42 = (bf16[2,32,768]{2,1,0:T(8,128)(2,1)S(1)}, bf16[2,32,768]{2,1,0:T(8,128)(2,1)S(1)}, u32[]{:S(2)}, u32[]{:S(2)}) collective-permute-start(bf16[2,32,768]{2,1,0:T(8,128)(2,1)S(1)} %add_convert_fusion.8.mine), channel_id=1, source_target_pairs={{0,7},{1,2},{2,1},{3,4},{4,3},{5,6},{6,5},{7,0},{8,15},{9,10},{10,... | collective-permute-start | bytes 294920 | tf_op jit(solution)/shard_map/ppermute | solution.py:38
  144.6 2.9 %collective-permute-done.42.near = bf16[2,32,768]{2,1,0:T(8,128)(2,1)S(1)} collective-permute-done((bf16[2,32,768]{2,1,0:T(8,128)(2,1)S(1)}, bf16[2,32,768]{2,1,0:T(8,128)(2,1)S(1)}, u32[]{:S(2)}, u32[]{:S(2)}) %collective-permute-start.42) | collective-permute-done | bytes 98336 | tf_op jit(solution)/shard_map/ppermute | solution.py:38
  149.2 2.9 %collective-permute-done.44.beyond = bf16[2,32,768]{2,1,0:T(8,128)(2,1)S(1)} collective-permute-done((bf16[2,32,768]{2,1,0:T(8,128)(2,1)S(1)}, bf16[2,32,768]{2,1,0:T(8,128)(2,1)S(1)}, u32[]{:S(2)}, u32[]{:S(2)}) %collective-permute-start.44) | collective-permute-done | bytes 98336 | tf_op jit(solution)/shard_map/ppermute | solution.py:34
  (154 shorter events, 39.0 us)
Async XLA Ops:
  6.2 16.4 %collective-permute-start.2 = (bf16[256,512]{1,0:T(8,128)(2,1)}, bf16[256,512]{1,0:T(8,128)(2,1)S(1)}, u32[]{:S(2)}, u32[]{:S(2)}) collective-permute-start(bf16[256,512]{1,0:T(8,128)(2,1)} %get-tuple-element.27), channel_id=1, source_target_pairs={{0,1},{1,0},{2,3},{3,2},{4,5},{5,4},{6,7},{7,6},{8,9},{9,8},{10,11... | collective-permute-start | bytes 786440 | tf_op jit(solution)/shard_map/ppermute | solution.py:34
  8.5 11.1 %collective-permute-start.8 = (bf16[128,768]{1,0:T(8,128)(2,1)S(1)}, bf16[128,768]{1,0:T(8,128)(2,1)S(1)}, u32[]{:S(2)}, u32[]{:S(2)}) collective-permute-start(bf16[128,768]{1,0:T(8,128)(2,1)S(1)} %get-tuple-element.59), channel_id=1, source_target_pairs={{0,32},{8,136},{16,48},{24,152},{32,0},{40,168},{48,16},{56,184},{... | collective-permute-start | bytes 589832 | tf_op jit(solution)/shard_map/ppermute | solution.py:30
  10.0 7.9 %collective-permute-start.5 = (bf16[128,768]{1,0:T(8,128)(2,1)S(1)}, bf16[128,768]{1,0:T(8,128)(2,1)S(1)}, u32[]{:S(2)}, u32[]{:S(2)}) collective-permute-start(bf16[128,768]{1,0:T(8,128)(2,1)S(1)} %get-tuple-element.59), channel_id=1, source_target_pairs={{0,48},{8,200},{16,0},{24,216},{32,16},{40,232},{48,32},{56,248},{... | collective-permute-start | bytes 589832 | tf_op jit(solution)/shard_map/ppermute | solution.py:30
  11.9 30.1 %collective-permute-start.1 = (bf16[256,2048]{1,0:T(8,128)(2,1)S(1)}, bf16[256,2048]{1,0:T(8,128)(2,1)S(1)}, u32[]{:S(2)}, u32[]{:S(2)}) collective-permute-start(bf16[256,2048]{1,0:T(8,128)(2,1)S(1)} %fusion.t0.refs_0_), channel_id=1, source_target_pairs={{0,1},{1,0},{2,3},{3,2},{4,5},{5,4},{6,7},{7,6},{8,9},{9,8},{10,11... | collective-permute-start | bytes 3145736 | tf_op jit(solution)/shard_map/ppermute | solution.py:34
  12.3 7.3 %collective-permute-start.9 = (bf16[128,768]{1,0:T(8,128)(2,1)S(1)}, bf16[128,768]{1,0:T(8,128)(2,1)S(1)}, u32[]{:S(2)}, u32[]{:S(2)}) collective-permute-start(bf16[128,768]{1,0:T(8,128)(2,1)S(1)} %get-tuple-element.59), channel_id=1, source_target_pairs={{0,16},{8,72},{16,32},{24,88},{32,48},{40,104},{48,0},{56,120},{64... | collective-permute-start | bytes 589832 | tf_op jit(solution)/shard_map/ppermute | solution.py:30
  17.9 9.1 %collective-permute-start.6 = (bf16[256,768]{1,0:T(8,128)(2,1)S(1)}, bf16[256,768]{1,0:T(8,128)(2,1)S(1)}, u32[]{:S(2)}, u32[]{:S(2)}) collective-permute-start(bf16[256,768]{1,0:T(8,128)(2,1)S(1)} %constant_dynamic-update-slice_fusion.2.refs_0_), channel_id=1, source_target_pairs={{0,64},{8,24},{16,80},{24,40},{32,96},{40,56},{48,112},{56,8},{64,... | collective-permute-start | bytes 1179656 | tf_op jit(solution)/shard_map/ppermute | solution.py:30
  19.6 8.3 %collective-permute-start.10 = (bf16[256,768]{1,0:T(8,128)(2,1)S(1)}, bf16[256,768]{1,0:T(8,128)(2,1)S(1)}, u32[]{:S(2)}, u32[]{:S(2)}) collective-permute-start(bf16[256,768]{1,0:T(8,128)(2,1)S(1)} %constant_dynamic-update-slice_fusion.5.refs_1_), channel_id=1, source_target_pairs={{0,192},{8,56},{16,208},{24,8},{32,224},{40,24},{48,240},{56,40},{... | collective-permute-start | bytes 1179656 | tf_op jit(solution)/shard_map/ppermute | solution.py:30
  22.7 9.4 %collective-permute-start.12 = (bf16[256,768]{1,0:T(8,128)(2,1)S(1)}, bf16[256,768]{1,0:T(8,128)(2,1)S(1)}, u32[]{:S(2)}, u32[]{:S(2)}) collective-permute-start(bf16[256,768]{1,0:T(8,128)(2,1)S(1)} %constant_dynamic-update-slice_fusion.2.refs_0_), channel_id=1, source_target_pairs={{0,192},{8,56},{16,208},{24,8},{32,224},{40,24},{48,240},{56,40},{... | collective-permute-start | bytes 1179656 | tf_op jit(solution)/shard_map/ppermute | solution.py:30
  24.4 9.0 %collective-permute-start.13 = (bf16[256,768]{1,0:T(8,128)(2,1)S(1)}, bf16[256,768]{1,0:T(8,128)(2,1)S(1)}, u32[]{:S(2)}, u32[]{:S(2)}) collective-permute-start(bf16[256,768]{1,0:T(8,128)(2,1)S(1)} %constant_dynamic-update-slice_fusion.5.refs_1_), channel_id=1, source_target_pairs={{0,64},{8,24},{16,80},{24,40},{32,96},{40,56},{48,112},{56,8},{64,... | collective-permute-start | bytes 1179656 | tf_op jit(solution)/shard_map/ppermute | solution.py:30
  26.9 10.7 %collective-permute-start.7 = (bf16[256,768]{1,0:T(8,128)(2,1)S(1)}, bf16[256,768]{1,0:T(8,128)(2,1)S(1)}, u32[]{:S(2)}, u32[]{:S(2)}) collective-permute-start(bf16[256,768]{1,0:T(8,128)(2,1)S(1)} %collective-permute-done.6.refs_4_), channel_id=1, source_target_pairs={{0,64},{8,24},{16,80},{24,40},{32,96},{40,56},{48,112},{56,8},{64,... | collective-permute-start | bytes 1179656 | tf_op jit(solution)/shard_map/ppermute | solution.py:30
  27.8 11.7 %collective-permute-start.11 = (bf16[256,768]{1,0:T(8,128)(2,1)S(1)}, bf16[256,768]{1,0:T(8,128)(2,1)S(1)}, u32[]{:S(2)}, u32[]{:S(2)}) collective-permute-start(bf16[256,768]{1,0:T(8,128)(2,1)S(1)} %collective-permute-done.10.refs_3_), channel_id=1, source_target_pairs={{0,192},{8,56},{16,208},{24,8},{32,224},{40,24},{48,240},{56,40},{... | collective-permute-start | bytes 1179656 | tf_op jit(solution)/shard_map/ppermute | solution.py:30
  32.1 13.9 %collective-permute-start.14 = (bf16[256,2048]{1,0:T(8,128)(2,1)S(1)}, bf16[256,2048]{1,0:T(8,128)(2,1)S(1)}, u32[]{:S(2)}, u32[]{:S(2)}) collective-permute-start(bf16[256,2048]{1,0:T(8,128)(2,1)S(1)} %fusion.t0.refs_0_), channel_id=1, source_target_pairs={{0,8},{8,0},{1,9},{9,1},{2,10},{10,2},{3,11},{11,3},{4,12},{12,4},... | collective-permute-start | bytes 3145736 | tf_op jit(solution)/shard_map/ppermute | solution.py:34
  56.8 7.8 %collective-permute-start.24 = (bf16[2,2,128,128]{3,2,1,0:T(8,128)(2,1)S(1)}, bf16[2,2,128,128]{3,2,1,0:T(8,128)(2,1)S(1)}, u32[]{:S(2)}, u32[]{:S(2)}) collective-permute-start(bf16[2,2,128,128]{3,2,1,0:T(8,128)(2,1)S(1)} %get-tuple-element.37), channel_id=1, source_target_pairs={{0,64},{64,0},{128,192},{192,128},{1,65},{65,1},{129,193},{193,129... | collective-permute-start | bytes 393224 | tf_op jit(solution)/shard_map/ppermute | solution.py:34
  56.8 9.8 %collective-permute-start.26 = (bf16[2,2,128,128]{3,2,1,0:T(8,128)(2,1)S(1)}, bf16[2,2,128,128]{3,2,1,0:T(8,128)(2,1)S(1)}, u32[]{:S(2)}, u32[]{:S(2)}) collective-permute-start(bf16[2,2,128,128]{3,2,1,0:T(8,128)(2,1)S(1)} %get-tuple-element.38), channel_id=1, source_target_pairs={{0,192},{64,128},{128,64},{192,0},{1,193},{65,129},{129,65},{193,1... | collective-permute-start | bytes 393224 | tf_op jit(solution)/shard_map/ppermute | solution.py:34
  57.9 8.8 %collective-permute-start.25 = (bf16[2,2,128,128]{3,2,1,0:T(8,128)(2,1)S(1)}, bf16[2,2,128,128]{3,2,1,0:T(8,128)(2,1)S(1)}, u32[]{:S(2)}, u32[]{:S(2)}) collective-permute-start(bf16[2,2,128,128]{3,2,1,0:T(8,128)(2,1)S(1)} %get-tuple-element.38), channel_id=1, source_target_pairs={{0,128},{64,192},{128,0},{192,64},{1,129},{65,193},{129,1},{193,65... | collective-permute-start | bytes 393224 | tf_op jit(solution)/shard_map/ppermute | solution.py:34
  60.9 9.6 %collective-permute-start.20 = (bf16[2,2,128,128]{3,2,1,0:T(8,128)(2,1)S(1)}, bf16[2,2,128,128]{3,2,1,0:T(8,128)(2,1)S(1)}, u32[]{:S(2)}, u32[]{:S(2)}) collective-permute-start(bf16[2,2,128,128]{3,2,1,0:T(8,128)(2,1)S(1)} %get-tuple-element.36), channel_id=1, source_target_pairs={{0,48},{16,32},{32,16},{48,0},{1,49},{17,33},{33,17},{49,1},{2,50}... | collective-permute-start | bytes 393224 | tf_op jit(solution)/shard_map/ppermute | solution.py:34
  64.6 7.6 %collective-permute-start.19 = (bf16[2,2,128,128]{3,2,1,0:T(8,128)(2,1)S(1)}, bf16[2,2,128,128]{3,2,1,0:T(8,128)(2,1)S(1)}, u32[]{:S(2)}, u32[]{:S(2)}) collective-permute-start(bf16[2,2,128,128]{3,2,1,0:T(8,128)(2,1)S(1)} %get-tuple-element.36), channel_id=1, source_target_pairs={{0,32},{16,48},{32,0},{48,16},{1,33},{17,49},{33,1},{49,17},{2,34}... | collective-permute-start | bytes 393224 | tf_op jit(solution)/shard_map/ppermute | solution.py:34
  64.6 7.6 %collective-permute-start.18 = (bf16[2,2,128,128]{3,2,1,0:T(8,128)(2,1)S(1)}, bf16[2,2,128,128]{3,2,1,0:T(8,128)(2,1)S(1)}, u32[]{:S(2)}, u32[]{:S(2)}) collective-permute-start(bf16[2,2,128,128]{3,2,1,0:T(8,128)(2,1)S(1)} %get-tuple-element.36), channel_id=1, source_target_pairs={{0,16},{16,0},{32,48},{48,32},{1,17},{17,1},{33,49},{49,33},{2,18}... | collective-permute-start | bytes 393224 | tf_op jit(solution)/shard_map/ppermute | solution.py:34
  66.8 16.1 %collective-permute-start.29 = (bf16[2,2,128,128]{3,2,1,0:T(8,128)(2,1)S(1)}, bf16[2,2,128,128]{3,2,1,0:T(8,128)(2,1)S(1)}, u32[]{:S(2)}, u32[]{:S(2)}) collective-permute-start(bf16[2,2,128,128]{3,2,1,0:T(8,128)(2,1)S(1)} %get-tuple-element.52), channel_id=1, source_target_pairs={{0,48},{16,32},{32,16},{48,0},{1,49},{17,33},{33,17},{49,1},{2,50}... | collective-permute-start | bytes 393224 | tf_op jit(solution)/shard_map/ppermute | solution.py:34
  70.5 12.3 %collective-permute-start.28 = (bf16[2,2,128,128]{3,2,1,0:T(8,128)(2,1)S(1)}, bf16[2,2,128,128]{3,2,1,0:T(8,128)(2,1)S(1)}, u32[]{:S(2)}, u32[]{:S(2)}) collective-permute-start(bf16[2,2,128,128]{3,2,1,0:T(8,128)(2,1)S(1)} %get-tuple-element.52), channel_id=1, source_target_pairs={{0,32},{16,48},{32,0},{48,16},{1,33},{17,49},{33,1},{49,17},{2,34}... | collective-permute-start | bytes 393224 | tf_op jit(solution)/shard_map/ppermute | solution.py:34
  72.3 10.6 %collective-permute-start.23 = (bf16[2,2,128,128]{3,2,1,0:T(8,128)(2,1)S(1)}, bf16[2,2,128,128]{3,2,1,0:T(8,128)(2,1)S(1)}, u32[]{:S(2)}, u32[]{:S(2)}) collective-permute-start(bf16[2,2,128,128]{3,2,1,0:T(8,128)(2,1)S(1)} %add_convert_fusion.7), channel_id=1, source_target_pairs={{0,192},{64,128},{128,64},{192,0},{1,193},{65,129},{129,65},{193,1... | collective-permute-start | bytes 393224 | tf_op jit(solution)/shard_map/ppermute | solution.py:34
  73.4 9.5 %collective-permute-start.22 = (bf16[2,2,128,128]{3,2,1,0:T(8,128)(2,1)S(1)}, bf16[2,2,128,128]{3,2,1,0:T(8,128)(2,1)S(1)}, u32[]{:S(2)}, u32[]{:S(2)}) collective-permute-start(bf16[2,2,128,128]{3,2,1,0:T(8,128)(2,1)S(1)} %add_convert_fusion.7), channel_id=1, source_target_pairs={{0,128},{64,192},{128,0},{192,64},{1,129},{65,193},{129,1},{193,65... | collective-permute-start | bytes 393224 | tf_op jit(solution)/shard_map/ppermute | solution.py:34
  87.0 7.9 %collective-permute-start.33 = (bf16[2,128,768]{2,1,0:T(8,128)(2,1)S(1)}, bf16[2,128,768]{2,1,0:T(8,128)(2,1)S(1)}, u32[]{:S(2)}, u32[]{:S(2)}) collective-permute-start(bf16[2,128,768]{2,1,0:T(8,128)(2,1)S(1)} %get-tuple-element.46), channel_id=1, source_target_pairs={{0,192},{8,56},{16,208},{24,8},{32,224},{40,24},{48,240},{56,40},{... | collective-permute-start | bytes 1179656 | tf_op jit(solution)/shard_map/ppermute | solution.py:30
  88.3 9.2 %collective-permute-start.31 = (bf16[2,128,768]{2,1,0:T(8,128)(2,1)S(1)}, bf16[2,128,768]{2,1,0:T(8,128)(2,1)S(1)}, u32[]{:S(2)}, u32[]{:S(2)}) collective-permute-start(bf16[2,128,768]{2,1,0:T(8,128)(2,1)S(1)} %get-tuple-element.44), channel_id=1, source_target_pairs={{0,64},{8,24},{16,80},{24,40},{32,96},{40,56},{48,112},{56,8},{64,... | collective-permute-start | bytes 1179656 | tf_op jit(solution)/shard_map/ppermute | solution.py:30
  95.0 12.1 %collective-permute-start.34 = (bf16[4,128,768]{2,1,0:T(8,128)(2,1)S(1)}, bf16[4,128,768]{2,1,0:T(8,128)(2,1)S(1)}, u32[]{:S(2)}, u32[]{:S(2)}) collective-permute-start(bf16[4,128,768]{2,1,0:T(8,128)(2,1)S(1)} %pad_maximum_fusion.1), channel_id=1, source_target_pairs={{0,192},{8,56},{16,208},{24,8},{32,224},{40,24},{48,240},{56,40},{... | collective-permute-start | bytes 2359304 | tf_op jit(solution)/shard_map/ppermute | solution.py:30
  97.7 13.3 %collective-permute-start.32 = (bf16[4,128,768]{2,1,0:T(8,128)(2,1)S(1)}, bf16[4,128,768]{2,1,0:T(8,128)(2,1)S(1)}, u32[]{:S(2)}, u32[]{:S(2)}) collective-permute-start(bf16[4,128,768]{2,1,0:T(8,128)(2,1)S(1)} %pad_maximum_fusion), channel_id=1, source_target_pairs={{0,64},{8,24},{16,80},{24,40},{32,96},{40,56},{48,112},{56,8},{64,... | collective-permute-start | bytes 2359304 | tf_op jit(solution)/shard_map/ppermute | solution.py:30
  97.9 9.2 %collective-permute-start.35 = (bf16[2,256,256]{2,1,0:T(8,128)(2,1)S(1)}, bf16[2,256,256]{2,1,0:T(8,128)(2,1)S(1)}, u32[]{:S(2)}, u32[]{:S(2)}) collective-permute-start(bf16[2,256,256]{2,1,0:T(8,128)(2,1)S(1)} %pad_maximum_fusion.2), channel_id=1, source_target_pairs={{0,1},{1,0},{2,3},{3,2},{4,5},{5,4},{6,7},{7,6},{8,9},{9,8},{10,11... | collective-permute-start | bytes 786440 | tf_op jit(solution)/shard_map/ppermute | solution.py:34
  112.6 8.2 %collective-permute-start.36 = (bf16[128,768]{1,0:T(8,128)(2,1)S(1)}, bf16[128,768]{1,0:T(8,128)(2,1)S(1)}, u32[]{:S(2)}, u32[]{:S(2)}) collective-permute-start(bf16[128,768]{1,0:T(8,128)(2,1)S(1)} %get-tuple-element.49), channel_id=1, source_target_pairs={{0,16},{8,72},{16,32},{24,88},{32,48},{40,104},{48,0},{56,120},{64... | collective-permute-start | bytes 589832 | tf_op jit(solution)/shard_map/ppermute | solution.py:30
  115.5 7.3 %collective-permute-start.37 = (bf16[128,768]{1,0:T(8,128)(2,1)S(1)}, bf16[128,768]{1,0:T(8,128)(2,1)S(1)}, u32[]{:S(2)}, u32[]{:S(2)}) collective-permute-start(bf16[128,768]{1,0:T(8,128)(2,1)S(1)} %get-tuple-element.50), channel_id=1, source_target_pairs={{0,32},{8,136},{16,48},{24,152},{32,0},{40,168},{48,16},{56,184},{... | collective-permute-start | bytes 589832 | tf_op jit(solution)/shard_map/ppermute | solution.py:30
  115.7 9.0 %collective-permute-start.38 = (bf16[128,768]{1,0:T(8,128)(2,1)S(1)}, bf16[128,768]{1,0:T(8,128)(2,1)S(1)}, u32[]{:S(2)}, u32[]{:S(2)}) collective-permute-start(bf16[128,768]{1,0:T(8,128)(2,1)S(1)} %get-tuple-element.51), channel_id=1, source_target_pairs={{0,48},{8,200},{16,0},{24,216},{32,16},{40,232},{48,32},{56,248},{... | collective-permute-start | bytes 589832 | tf_op jit(solution)/shard_map/ppermute | solution.py:30
  126.2 7.3 %collective-permute-start.40 = (bf16[2,32,768]{2,1,0:T(8,128)(2,1)S(1)}, bf16[2,32,768]{2,1,0:T(8,128)(2,1)S(1)}, u32[]{:S(2)}, u32[]{:S(2)}) collective-permute-start(bf16[2,32,768]{2,1,0:T(8,128)(2,1)S(1)} %pad_maximum_fusion.3), channel_id=1, source_target_pairs={{0,7},{1,2},{2,1},{3,4},{4,3},{5,6},{6,5},{7,0},{8,15},{9,10},{10,... | collective-permute-start | bytes 294920 | tf_op jit(solution)/shard_map/ppermute | solution.py:38
  133.5 8.0 %collective-permute-start.41 = (bf16[2,32,768]{2,1,0:T(8,128)(2,1)S(1)}, bf16[2,32,768]{2,1,0:T(8,128)(2,1)S(1)}, u32[]{:S(2)}, u32[]{:S(2)}) collective-permute-start(bf16[2,32,768]{2,1,0:T(8,128)(2,1)S(1)} %add_convert_fusion.9), channel_id=1, source_target_pairs={{0,3},{1,6},{2,5},{3,0},{4,7},{5,2},{6,1},{7,4},{8,11},{9,14},{10,... | collective-permute-start | bytes 294920 | tf_op jit(solution)/shard_map/ppermute | solution.py:42
  (39 other events, 425.9 us)
